TPU v7x, 32 devices: a whole 2x2x4 slice. The times are simulated.
32 devices in a mesh: wide: 8 (over z, x), narrow: 4 (over y, core).
Axes of the slice: x: 2, y: 2, z: 4, core: 2. Of those that a mesh axis runs over, the one named last changes fastest.
Arguments:
- record: float32 [128, 128, 64, 128], P('wide', 'narrow'), may hold values from -6 to 6
Outputs:
- spectrum: float32 [2, 128, 4, 32, 64, 128], P(None, 'wide', 'narrow')
All inputs are finite; a program needn't handle non-finite values.
Results may differ from a plain program's by a relative error of at most 0.00007.
Values sent between devices are 32-bit elements; how exact they have to be, the bound alone decides.
A program may use at most 192 MiB of HBM per device.

v0:
```python
import math

import jax
import jax.numpy as jnp
from jax import lax
from jax.sharding import PartitionSpec as P

PRECISE = lax.Precision.HIGHEST
TWO_PI = 2.0 * math.pi


def partner_2(block, axis, apart):
    count = lax.axis_size(axis)
    route = []
    for low in range(count):
        high = low | 1 << apart
        if high != low and high < count:
            route += [(low, high), (high, low)]
    return lax.ppermute(block, axis, route)


def block_table(inputs, outputs, length, factor):
    phases = inputs[:, None] * outputs[None, :] % length
    angles = phases.astype(jnp.float32) * (TWO_PI / length)
    cosine = jnp.cos(angles) * factor
    sines = jnp.sin(angles) * factor
    return jnp.stack([jnp.stack([cosine, sines]), jnp.stack([-sines, cosine])])


def rotate(values, angles):
    cosine = jnp.cos(angles)
    sines = jnp.sin(angles)
    return jnp.stack(
        [values[0] * cosine + values[1] * sines, values[1] * cosine - values[0] * sines]
    )


def reversed_digits(number, bit_count):
    result = 0 * number
    for position in range(bit_count):
        result = result + number // (1 << position) % 2 * (1 << bit_count - 1 - position)
    return result


def turn_mixed(values, frequency, cell_index, extent, length):
    offset = cell_index[:, None] * extent + jnp.arange(extent, dtype=jnp.int32)[None, :]
    phases = offset[None, :, :] * frequency[:, None, None] % length
    return rotate(values, phases.astype(jnp.float32) * (TWO_PI / length))


def first_factor(gathered, index_a, size_a, total_count):
    table_a = block_table(index_a, index_a, size_a, 1.0 / math.sqrt(total_count))[:, 0]
    return jnp.einsum("pak,arn->pkrn", table_a, gathered, precision=PRECISE)


def shards(record):
    local_a, local_b, size_c, size_d = record.shape
    wide_size = lax.axis_size("wide")
    narrow_size = lax.axis_size("narrow")
    levels = narrow_size.bit_length() - 1
    size_a = local_a * wide_size
    size_b = local_b * narrow_size
    total_count = size_a * size_b * size_c * size_d
    row_count = local_b * size_c
    row_share = row_count // wide_size
    wide_at = lax.axis_index("wide")
    narrow_at = lax.axis_index("narrow")
    index_a = jnp.arange(size_a, dtype=jnp.int32)
    third_index = jnp.arange(size_c, dtype=jnp.int32)
    inner_length = size_b * size_c * size_d
    row_index = narrow_at * row_count + wide_at * row_share + jnp.arange(row_share, dtype=jnp.int32)
    offset = row_index[:, None] * size_d + jnp.arange(size_d, dtype=jnp.int32)[None, :]
    phases = offset[None, :, :] * index_a[:, None, None] % total_count
    gathered = lax.all_to_all(
        record.reshape(local_a, row_count, size_d), "wide", split_axis=1, concat_axis=0, tiled=True
    )
    section_a = rotate(
        first_factor(gathered, index_a, size_a, total_count),
        phases.astype(jnp.float32) * (TWO_PI / total_count),
    )
    blocks = lax.all_to_all(section_a, "wide", split_axis=1, concat_axis=2, tiled=True).reshape(
        2, local_a, local_b, size_c, size_d
    )
    current = blocks
    for digit_place in reversed(range(levels)):
        partner = partner_2(current, "narrow", digit_place)
        upper_bit = narrow_at // (1 << digit_place) % 2
        current = partner + (1 - 2 * upper_bit).astype(jnp.float32) * current
        if digit_place > 0:
            lower_part = narrow_at % (1 << digit_place)
            current = rotate(
                current,
                (lower_part * upper_bit).astype(jnp.float32) * (TWO_PI / (2 << digit_place)),
            )
    residue = reversed_digits(narrow_at, levels)
    outputs_b = narrow_size * jnp.arange(local_b, dtype=jnp.int32) + residue
    table_b = block_table(jnp.arange(local_b, dtype=jnp.int32), outputs_b, size_b, 1.0)
    section_b = jnp.einsum("pqlm,qalcd->pamcd", table_b, current, precision=PRECISE)
    section_b = turn_mixed(section_b, outputs_b, third_index, size_d, inner_length)
    table_c = block_table(third_index, third_index, size_c, 1.0)
    section_c = jnp.einsum("pqck,qamcd->pamkd", table_c, section_b, precision=PRECISE)
    depth_index = jnp.arange(size_d, dtype=jnp.int32)
    phase_c = third_index[:, None] * depth_index[None, :] % (size_c * size_d)
    section_c = rotate(section_c, phase_c.astype(jnp.float32) * (TWO_PI / (size_c * size_d)))
    table_d = block_table(depth_index, depth_index, size_d, 1.0)
    section_d = jnp.einsum("pqdk,qamcd->pamck", table_d, section_c, precision=PRECISE)
    return section_d.reshape(2, local_a, 1, local_b, size_c, size_d)


def solution(mesh):
    return jax.shard_map(
        shards,
        mesh=mesh,
        in_specs=(P("wide", "narrow", None, None),),
        out_specs=P(None, "wide", "narrow", None, None, None),
        check_vma=False,
    )
```

profile of v0, /device:TPU:0, one launch (start us, length us, event | category | flops | bytes accessed | tf_op | source)
XLA Modules:
  0.0 2370.3 jit_solution(13239822143825194450)
XLA Ops:
  0.0 18.5 copy.23
  18.5 7.5 all-to-all-start
  26.1 0.3 fusion.58
  26.3 0.3 broadcast_multiply_fusion
  26.6 0.1 iota_add_fusion
  26.7 362.4 %all-to-all-done = f32[16,2048,128]{2,0,1:T(8,128)} async-done(((f32[16,2048,128]{2,0,1:T(8,128)}), f32[16,2048,128]{2,0,1:T(8,128)}, u32[]{:S(2)}, u32[]{:S(2)}) %all-to-all-start) | async-done | bytes 16777248 | tf_op jit(solution)/shard_map/all_to_all | solution.py:74
  389.1 7.1 copy.25
  396.3 32.0 %fusion.30 = f32[2,128,256,128]{3,1,2,0:T(8,128)} fusion(f32[128,256,128,1]{2,0,1,3:T(8,128)S(1)} %bitcast.94, f32[1,2,128,128]{2,3,0,1:T(8,128)S(1)} %get-tuple-element.16, f32[1,2,128,128]{2,3,0,1:T(8,128)S(1)} %get-tuple-element.15), kind=kOutput, calls=%fused_computation.50 | convolution fusion | flops 12884934656 | bytes 50593792 | tf_op jit(solution)/shard_map/pak,arn->pkrn/dot_general | solution.py:53
  428.3 72.9 %multiply_add_fusion.4 = (f32[1,128,256,128]{3,1,2,0:T(8,128)}, f32[1,128,256,128]{3,1,2,0:T(8,128)}) fusion(f32[2,128,256,128]{3,1,2,0:T(8,128)} %fusion.30, s32[256,128]{1,0:T(8,128)S(1)} %iota_add_fusion), kind=kLoop, calls=%fused_computation.26 | loop fusion | flops 83886080 | bytes 67239936 | tf_op jit(solution)/shard_map/add | solution.py:34
  501.2 12.0 pad_maximum_fusion
  513.2 37.1 %copy.26 = f32[2,128,256,128]{3,2,0,1:T(8,128)} copy(f32[2,128,256,128]{3,1,2,0:T(8,128)S(1)} %pad_maximum_fusion) | data formatting | bytes 67108864 | tf_op jit(solution)/shard_map/stack | solution.py:33
  550.4 728.0 %all_to_all.33 = f32[2,128,256,128]{3,2,0,1:T(8,128)S(1)} all-to-all(f32[2,128,256,128]{3,2,0,1:T(8,128)} %copy.26), channel_id=1, replica_groups=mesh['wide'=8,'narrow'=4] {'wide'}, dimensions={1} | all-to-all | bytes 67108864 | tf_op jit(solution)/shard_map/all_to_all | solution.py:81
  1278.4 11.2 copy.28
  1289.6 1.3 collective-permute-start
  1291.1 718.6 %collective-permute-done = f32[2,16,32,64,128]{4,3,2,1,0:T(8,128)} collective-permute-done((f32[2,16,32,64,128]{4,3,2,1,0:T(8,128)}, f32[2,16,32,64,128]{4,3,2,1,0:T(8,128)}, u32[]{:S(2)}, u32[]{:S(2)}) %collective-permute-start) | collective-permute-done | bytes 33554464 | tf_op jit(solution)/shard_map/ppermute | solution.py:19
  2009.7 33.3 %multiply_add_fusion = f32[2,16,32,64,128]{4,3,2,1,0:T(8,128)} fusion(f32[2,16,32,64,128]{4,3,2,1,0:T(8,128)} %collective-permute-done, f32[2,16,32,64,128]{4,3,2,1,0:T(8,128)} %bitcast.93, f32[]{:T(128)S(6)} %convert_element_type.138), kind=kLoop, calls=%fused_computation.12 | loop fusion | flops 16777216 | bytes 100663296 | tf_op jit(solution)/shard_map/add | solution.py:88
  2042.9 17.4 multiply_add_fusion.3
  2060.3 0.0 copy-start
  2060.3 21.1 pad_maximum_fusion.1
  2081.4 0.6 copy-done
  2082.1 0.0 collective-permute-start.1
  2082.1 0.1 fusion.69
  2082.2 0.1 fusion.64
  2082.4 0.1 fusion.62
  2082.5 0.3 fusion.55
  2082.8 0.2 fusion.70
  2083.0 0.3 fusion.53
  2083.3 0.1 iota_add_fusion.1
  2083.4 4.1 fusion.26
  2087.5 44.1 %collective-permute-done.1 = f32[2,16,32,64,128]{4,3,2,1,0:T(8,128)} collective-permute-done((f32[2,16,32,64,128]{4,3,2,1,0:T(8,128)}, f32[2,16,32,64,128]{4,3,2,1,0:T(8,128)}, u32[]{:S(2)}, u32[]{:S(2)}) %collective-permute-start.1) | collective-permute-done | bytes 33554464 | tf_op jit(solution)/shard_map/ppermute | solution.py:19
  2131.6 33.3 %add_bitcast_fusion = f32[2,16,32,64,128,1]{4,3,2,1,0,5:T(8,128)} fusion(f32[2,16,32,64,128]{4,3,2,1,0:T(8,128)} %collective-permute-done.1, f32[]{:T(128)S(6)} %convert_element_type.140, f32[1,16,32,64,128]{4,3,2,1,0:T(8,128)} %get-tuple-element.12, f32[1,16,32,64,128]{4,3,2,1,0:T(8,128)} %copy-done), kind=kLoop, calls=%fused_computation.11 | loop fusion | flops 25165824 | bytes 100663296 | tf_op jit(solution)/shard_map/add | solution.py:88
  2164.8 58.1 %fusion.16 = f32[2,16,32,64,128]{4,2,0,3,1:T(8,128)} fusion(f32[2,16,32,64,128,1]{4,3,2,1,0,5:T(8,128)} %add_bitcast_fusion, f32[1,2,32,32]{2,3,1,0:T(8,128)S(1)} %get-tuple-element.22, f32[1,2,32,32]{2,3,1,0:T(8,128)S(1)} %get-tuple-element.21), kind=kOutput, calls=%fused_computation.31 | convolution fusion | flops 6442455040 | bytes 67125248 | tf_op jit(solution)/shard_map/pqlm,qalcd->pamcd/dot_general | solution.py:98
  2222.9 22.2 multiply_add_fusion.2
  2245.1 12.8 maximum_bitcast_fusion
  2257.9 46.8 %fusion.13 = f32[2,16,32,64,128]{4,3,0,2,1:T(8,128)} fusion(f32[2,16,32,64,128,1]{4,2,0,3,1,5:T(8,128)S(1)} %maximum_bitcast_fusion, f32[1,2,64,64]{2,3,1,0:T(8,128)S(1)} %get-tuple-element.20, f32[1,2,64,64]{2,3,1,0:T(8,128)S(1)} %get-tuple-element.19), kind=kOutput, calls=%fused_computation.30 | convolution fusion | flops 12884918272 | bytes 67174400 | tf_op jit(solution)/shard_map/pqck,qamcd->pamkd/dot_general | solution.py:101
  2304.8 21.5 multiply_add_fusion.1
  2326.2 32.1 %fusion.19 = f32[2,16,1,32,64,128]{5,4,0,3,1,2:T(8,128)S(1)} fusion(f32[1,16,32,64,128]{4,3,0,2,1:T(8,128)} %get-tuple-element.10, f32[1,16,32,64,128]{4,3,0,2,1:T(8,128)} %get-tuple-element.9, f32[1,2,128,128]{2,3,1,0:T(8,128)S(1)} %get-tuple-element.14, f32[1,2,128,128]{2,3,1,0:T(8,128)S(1)} %get-tuple-element.13), kind=kOutput, calls=%fused_computation.32 | convolution fusion | flops 25778257920 | bytes 67371008 | tf_op jit(solution)/shard_map/pqdk,qamcd->pamck/dot_general | solution.py:106
  2358.4 11.7 copy.32
  (7 shorter events, 0.1 us)
Async XLA Ops:
  18.5 370.6 %all-to-all-start = ((f32[16,2048,128]{2,0,1:T(8,128)}), f32[16,2048,128]{2,0,1:T(8,128)}, u32[]{:S(2)}, u32[]{:S(2)}) async-start(f32[16,2048,128]{2,0,1:T(8,128)} %bitcast.95), calls=%async_computation | async-start | bytes 33554432 | tf_op jit(solution)/shard_map/all_to_all | solution.py:74
  1289.6 720.0 %collective-permute-start = (f32[2,16,32,64,128]{4,3,2,1,0:T(8,128)}, f32[2,16,32,64,128]{4,3,2,1,0:T(8,128)}, u32[]{:S(2)}, u32[]{:S(2)}) collective-permute-start(f32[2,16,32,64,128]{4,3,2,1,0:T(8,128)} %bitcast.92), channel_id=1, source_target_pairs={{0,2},{2,0},{1,3},{3,1},{4,6},{6,4},{5,7},{7,5},{8,10},{10,8},{9,1... | collective-permute-start | bytes 100663304 | tf_op jit(solution)/shard_map/ppermute | solution.py:19
  2060.3 21.8 copy-start
  2082.1 49.5 %collective-permute-start.1 = (f32[2,16,32,64,128]{4,3,2,1,0:T(8,128)}, f32[2,16,32,64,128]{4,3,2,1,0:T(8,128)}, u32[]{:S(2)}, u32[]{:S(2)}) collective-permute-start(f32[2,16,32,64,128]{4,3,2,1,0:T(8,128)} %pad_maximum_fusion.1), channel_id=1, source_target_pairs={{0,1},{1,0},{2,3},{3,2},{4,5},{5,4},{6,7},{7,6},{8,9},{9,8},{10,11... | collective-permute-start | bytes 100663304 | tf_op jit(solution)/shard_map/ppermute | solution.py:19
where the time goes:
time: 2370 us
  waiting for transfers between devices  1130 us (48%)
  blocking collectives  728 us (31%)
  other arithmetic  252 us (11%)
  matrix products  169 us (7%)
  local copies, waits for them, and re-layouts  86.4 us (4%)
    ppermute x2, waiting for transfers between devices, partner_2(): return lax.ppermute(block, axis, route)  763 us
    all_to_all x1, blocking collectives, shards(): lax.all_to_all(section_a, 'wide', split_axis=1, concat_axis=2, tiled=True)  728 us
    all_to_all x1, waiting for transfers between devices, shards(): lax.all_to_all(record.reshape(local_a, row_count, size_d), 'wide', split_...  362 us
    add x4, other arithmetic, rotate(): values[0] * cosine + values[1] * sines  134 us
    add x2, other arithmetic, shards(): current = partner + (1 - 2 * upper_bit).astype(jnp.float32) * current  66.5 us
    dot_general x1, matrix products, shards(): jnp.einsum('pqlm,qalcd->pamcd', table_b, current, precision=PRECISE)  58.1 us
  transfers between devices with their start and end apart: 3, of which 3 were waited for; matrix products, arithmetic and copies ran while one was open for 0% of the time, Pallas kernels for 0%

commit v1 on v0

v1 whole, which is shorter than its diff:
```python
import functools
import math

import jax
import jax.numpy as jnp
from jax import lax
from jax.experimental import pallas as pl
from jax.experimental.pallas import tpu as pltpu
from jax.sharding import PartitionSpec as P

SPLIT = lax.Precision.HIGH
TWO_PI = 2.0 * math.pi
CHUNKS = 8


def swap(block, axis, place):
    count = lax.axis_size(axis)
    return lax.ppermute(block, axis, [(at, at ^ (1 << place)) for at in range(count)])


def turn(phases, length):
    angles = (phases % length).astype(jnp.float32) * (TWO_PI / length)
    return jnp.cos(angles), jnp.sin(angles)


def reversed_digits(number, bit_count):
    result = 0 * number
    for position in range(bit_count):
        result = result + number // (1 << position) % 2 * (1 << bit_count - 1 - position)
    return result


def halves(values, upper):
    size = values.shape[-2] // 2
    axis = values.ndim - 2
    keep = lax.dynamic_slice_in_dim(values, upper * size, size, axis)
    send = lax.dynamic_slice_in_dim(values, (1 - upper) * size, size, axis)
    return keep, send


def two_parts(table):
    high = lax.reduce_precision(table, 8, 7)
    low = lax.reduce_precision(table - high, 8, 7)
    return high.astype(jnp.bfloat16), low.astype(jnp.bfloat16)


def last_factors(pieces, group, *refs):
    blocks = refs[:pieces]
    turn_p, turn_m, table_c, turn_c, table_d, out = refs[pieces:]
    count_m = out.shape[2]
    size_d = out.shape[4]
    size_c = out.shape[3]
    cos_p, sin_p = turn_p[0, 0], turn_p[1, 0]
    cos_c, sin_c = turn_c[0], turn_c[1]

    def parts(values):
        high = values.astype(jnp.bfloat16)
        low = (values - high.astype(jnp.float32)).astype(jnp.bfloat16)
        return high, low

    def body(step, carry):
        columns = []
        for index in range(group):
            m = step * group + index
            real = jnp.concatenate([block[0, 0, m] for block in blocks], axis=0)
            imag = jnp.concatenate([block[0, 1, m] for block in blocks], axis=0)
            cos_m, sin_m = turn_m[0, m], turn_m[1, m]
            cosine = cos_p * cos_m - sin_p * sin_m
            sines = sin_p * cos_m + cos_p * sin_m
            columns.append(
                jnp.concatenate(
                    [real * cosine + imag * sines, imag * cosine - real * sines], axis=0
                )
            )
        wide = jnp.concatenate(columns, axis=1)
        high, low = parts(wide)
        third = jnp.dot(
            table_c[...],
            jnp.concatenate([high, low, high], axis=0),
            preferred_element_type=jnp.float32,
        )
        rows = []
        for index in range(group):
            part = third[:, index * size_d : (index + 1) * size_d]
            real, imag = part[:size_c], part[size_c:]
            rows.append(
                jnp.concatenate(
                    [real * cos_c + imag * sin_c, imag * cos_c - real * sin_c], axis=1
                )
            )
        tall = jnp.concatenate(rows, axis=0)
        high, low = parts(tall)
        fourth = jnp.dot(
            jnp.concatenate([high, low, high], axis=1),
            table_d[...],
            preferred_element_type=jnp.float32,
        )
        for index in range(group):
            part = fourth[index * size_c : (index + 1) * size_c]
            m = step * group + index
            out[0, 0, m] = part[:, :size_d]
            out[1, 0, m] = part[:, size_d:]
        return carry

    lax.fori_loop(0, count_m // group, body, 0)


def finish(sections, turn_p, turn_m, table_c, turn_c, table_d):
    count_p, _, count_m, share_c, size_d = sections[0].shape
    pieces = len(sections)
    size_c = share_c * pieces
    group = math.gcd(count_m, 4)
    piece = pl.BlockSpec((1, 2, count_m, share_c, size_d), lambda p: (p, 0, 0, 0, 0))
    whole = lambda table: pl.BlockSpec(table.shape, lambda p: (0,) * table.ndim)
    return pl.pallas_call(
        functools.partial(last_factors, pieces, group),
        grid=(count_p,),
        out_shape=jax.ShapeDtypeStruct((2, count_p, count_m, size_c, size_d), jnp.float32),
        in_specs=[piece] * pieces
        + [
            pl.BlockSpec((2, 1, size_c, size_d), lambda p: (0, p, 0, 0)),
            whole(turn_m),
            whole(table_c),
            whole(turn_c),
            whole(table_d),
        ],
        out_specs=pl.BlockSpec((2, 1, count_m, size_c, size_d), lambda p: (0, p, 0, 0, 0)),
        compiler_params=pltpu.CompilerParams(vmem_limit_bytes=40 * 1024 * 1024),
        cost_estimate=pl.CostEstimate(
            flops=2 * 3 * count_p * count_m * size_c * size_d * 2 * 2 * (size_c + size_d),
            bytes_accessed=16 * count_p * count_m * size_c * size_d,
            transcendentals=0,
        ),
        name="last_factors",
    )(*sections, turn_p, turn_m, table_c, turn_c, table_d)


def shards(record):
    local_a, local_b, size_c, size_d = record.shape
    wide_size = lax.axis_size("wide")
    narrow_size = lax.axis_size("narrow")
    narrow_levels = narrow_size.bit_length() - 1
    levels = wide_size.bit_length() - 2
    size_a = local_a * wide_size
    size_b = local_b * narrow_size
    total_count = size_a * size_b * size_c * size_d
    inner = size_c * size_d
    wide_at = lax.axis_index("wide")
    narrow_at = lax.axis_index("narrow")
    bits = [wide_at // (1 << place) % 2 for place in range(levels)]
    share_c = size_c // CHUNKS

    def positions(slots):
        return (
            local_a * (wide_at ^ jnp.arange(slots, dtype=jnp.int32))[:, None]
            + jnp.arange(local_a, dtype=jnp.int32)
        )

    inputs_a = positions(wide_size).reshape(-1)
    outputs_a = positions(wide_size // 2)[:, :, None]
    cosine, sines = turn(
        outputs_a * (inputs_a * narrow_size + narrow_at), size_a * narrow_size
    )
    scale = 1.0 / math.sqrt(total_count)
    table_a = (jnp.stack([cosine, -sines], axis=1) * scale).reshape(-1, size_a)

    own_p = local_a * wide_at + jnp.arange(local_a, dtype=jnp.int32)
    index_m = jnp.arange(local_b, dtype=jnp.int32)
    outputs_b = narrow_size * index_m + reversed_digits(narrow_at, narrow_levels)
    mask = 0
    left_b = local_b
    for bit in bits:
        left_b //= 2
        mask = mask + bit * left_b
    inputs_b = jnp.arange(local_b, dtype=jnp.int32) ^ mask
    frequency = own_p[:, None] + size_a * outputs_b[None, :]
    cosine, sines = turn(frequency[:, :, None] * inputs_b, size_a * size_b)
    table_b = jnp.stack(
        [jnp.stack([cosine, sines], axis=2), jnp.stack([-sines, cosine], axis=2)], axis=1
    )

    offset = jnp.arange(inner, dtype=jnp.int32).reshape(size_c, size_d)
    turn_p = jnp.stack(turn(own_p[:, None, None] * offset, total_count))
    turn_m = jnp.stack(turn(outputs_b[:, None, None] * offset, size_b * inner))
    index_c = jnp.arange(size_c, dtype=jnp.int32)
    index_d = jnp.arange(size_d, dtype=jnp.int32)
    cosine, sines = turn(index_c[:, None] * index_c, size_c)
    high, low = two_parts(jnp.block([[cosine, sines], [-sines, cosine]]))
    table_c = jnp.concatenate([high, high, low], axis=1)
    turn_c = jnp.stack(turn(index_c[:, None] * index_d, inner))
    cosine, sines = turn(index_d[:, None] * index_d, size_d)
    high, low = two_parts(jnp.block([[cosine, -sines], [sines, cosine]]))
    table_d = jnp.concatenate([high, high, low], axis=0)

    sections = []
    for chunk in range(CHUNKS):
        values = lax.slice_in_dim(record, chunk * share_c, (chunk + 1) * share_c, axis=2)
        values = values.reshape(local_a, local_b * share_c, size_d)
        for place in range(levels):
            keep, send = halves(values, bits[place])
            values = jnp.concatenate([keep, swap(send, "wide", place)], axis=0)
        values = jnp.concatenate([values, swap(values, "wide", levels)], axis=0)
        rows = values.shape[1]
        spread = jnp.einsum(
            "pa,an->pn", table_a, values.reshape(size_a, rows * size_d), precision=SPLIT
        ).reshape(wide_size // 2, 2, local_a, rows, size_d)
        for place in reversed(range(levels)):
            half = spread.shape[0] // 2
            mine, other = spread[:half], swap(spread[half:], "wide", place)
            spread = jnp.concatenate([mine, other], axis=3)
            if mine.shape[3] < share_c:
                spread = jnp.where(
                    bits[place] > 0, jnp.concatenate([other, mine], axis=3), spread
                )
        current = spread[0]
        for place in reversed(range(narrow_levels)):
            partner = swap(current, "narrow", place)
            upper = narrow_at // (1 << place) % 2
            current = partner + (1 - 2 * upper).astype(jnp.float32) * current
            if place > 0:
                cosine, sines = turn(upper * (narrow_at % (1 << place)), 2 << place)
                current = jnp.stack(
                    [
                        current[0] * cosine + current[1] * sines,
                        current[1] * cosine - current[0] * sines,
                    ]
                )
        current = current.reshape(2, local_a, local_b, share_c * size_d)
        section = jnp.einsum("aomib,iabn->aomn", table_b, current, precision=SPLIT)
        sections.append(section.reshape(local_a, 2, local_b, share_c, size_d))
    result = finish(sections, turn_p, turn_m, table_c, turn_c, table_d)
    return result.reshape(2, local_a, 1, local_b, size_c, size_d)


def solution(mesh):
    return jax.shard_map(
        shards,
        mesh=mesh,
        in_specs=(P("wide", "narrow", None, None),),
        out_specs=P(None, "wide", "narrow", None, None, None),
        check_vma=False,
    )
```

time: 2370 us -> 2240 us (0.945)
  blocking collectives: 728 us -> 0 us
  waiting for transfers between devices: 1130 us -> 1710 us
  matrix products: 169 us -> 69.4 us
  other arithmetic: 252 us -> 174 us
  local copies, waits for them, and re-layouts: 86.4 us -> 156 us
  Pallas kernels: 0 us -> 69.3 us
  starting transfers between devices: 8.81 us -> 55.1 us
    ppermute x2 -> x56, waiting for transfers between devices: 763 us -> 1710 us  [swap(): lax.ppermute(block, axis, [(at, at ^ 1 << place) for at in range(count)])]
    all_to_all x1 -> x0, blocking collectives: 728 us -> none  [shards(): lax.all_to_all(section_a, 'wide', split_axis=1, concat_axis=2, tiled=True)]
    all_to_all x1 -> x0, waiting for transfers between devices: 362 us -> none  [shards(): lax.all_to_all(record.reshape(local_a, row_count, size_d), 'wide', split_...]
    add x9 -> x25, other arithmetic: 201 us -> 71.6 us  [the longest x12 64.4 us: shards(): current = partner + (1 - 2 * upper).astype(jnp.float32) * current]
    dot_general x4 -> x16, matrix products: 169 us -> 69.4 us  [the longest x8 35.9 us: shards(): section = jnp.einsum('aomib,iabn->aomn', table_b, current, precision=SPLIT)]
    pallas_call x0 -> x1, Pallas kernels: none -> 69.3 us  [finish(): pl.pallas_call(functools.partial(last_factors, pieces, group), grid=(coun...]
    ppermute x2 -> x56, starting transfers between devices: 1.29 us -> 55.1 us  [swap(): lax.ppermute(block, axis, [(at, at ^ 1 << place) for at in range(count)])]
    reshape x1 -> x9, local copies, waits for them, and re-layouts: 11.7 us -> 51.5 us  [the longest x8 39.9 us: shards(): current = current.reshape(2, local_a, local_b, share_c * size_d)]
  transfers between devices with their start and end apart: 3 -> 56, of which waited for: 3 -> 38; matrix products, arithmetic and copies ran while one was open for 0% -> 16% of each run, Pallas kernels for 0% -> 0%
where the time goes in v1:
time: 2240 us; the launch traced here: 2230 us
  waiting for transfers between devices  1710 us (76%)
  other arithmetic  174 us (8%)
  local copies, waits for them, and re-layouts  156 us (7%)
  matrix products  69.4 us (3%)
  Pallas kernels  69.3 us (3%)
  starting transfers between devices  55.1 us (2%)
    ppermute x56, waiting for transfers between devices, swap(): lax.ppermute(block, axis, [(at, at ^ 1 << place) for at in range(count)])  1710 us
    pallas_call x1, Pallas kernels, finish(): pl.pallas_call(functools.partial(last_factors, pieces, group), grid=(coun...  69.3 us
    add x12, other arithmetic, shards(): current = partner + (1 - 2 * upper).astype(jnp.float32) * current  64.4 us
    unnamed x180, local copies, waits for them, and re-layouts  57.6 us
    ppermute x56, starting transfers between devices, swap(): lax.ppermute(block, axis, [(at, at ^ 1 << place) for at in range(count)])  55.1 us
  transfers between devices with their start and end apart: 56, of which 38 were waited for; matrix products, arithmetic and copies ran while one was open for 16% of the time, Pallas kernels for 0%

profile of v1, /device:TPU:0, one launch (start us, length us, event | category | flops | bytes accessed | tf_op | source)
XLA Modules:
  0.0 2232.8 jit_solution(1439146910107229377)
XLA Ops:
  0.0 11.7 slice_bitcast_fusion.16
  31.4 10.7 collective-permute-done.42
  48.0 16.6 collective-permute-done.49
  68.3 18.8 collective-permute-done.28
  89.2 20.4 collective-permute-done.35
  113.4 18.7 collective-permute-done.14
  135.9 18.6 collective-permute-done.21
  162.0 14.9 collective-permute-done
  179.0 19.5 collective-permute-done.7
  206.6 18.9 collective-permute-done.36
  225.7 23.7 %collective-permute-done.15 = f32[32,64,128]{2,1,0:T(8,128)S(1)} collective-permute-done((f32[32,64,128]{2,1,0:T(8,128)S(1)}, f32[32,64,128]{2,1,0:T(8,128)S(1)}, u32[]{:S(2)}, u32[]{:S(2)}) %collective-permute-start.15) | collective-permute-done | bytes 1048608 | tf_op jit(solution)/shard_map/ppermute | solution.py:18
  249.6 88.1 %collective-permute-done.22 = f32[32,64,128]{2,1,0:T(8,128)S(1)} collective-permute-done((f32[32,64,128]{2,1,0:T(8,128)S(1)}, f32[32,64,128]{2,1,0:T(8,128)S(1)}, u32[]{:S(2)}, u32[]{:S(2)}) %collective-permute-start.22) | collective-permute-done | bytes 1048608 | tf_op jit(solution)/shard_map/ppermute | solution.py:18
  338.7 23.0 %collective-permute-done.1 = f32[32,64,128]{2,1,0:T(8,128)S(1)} collective-permute-done((f32[32,64,128]{2,1,0:T(8,128)S(1)}, f32[32,64,128]{2,1,0:T(8,128)S(1)}, u32[]{:S(2)}, u32[]{:S(2)}) %collective-permute-start.1) | collective-permute-done | bytes 1048608 | tf_op jit(solution)/shard_map/ppermute | solution.py:18
  366.3 15.3 collective-permute-done.8
  394.5 190.7 %collective-permute-done.51 = f32[64,64,128]{2,1,0:T(8,128)} collective-permute-done((f32[64,64,128]{2,1,0:T(8,128)S(1)}, f32[64,64,128]{2,1,0:T(8,128)}, u32[]{:S(2)}, u32[]{:S(2)}) %collective-permute-start.51) | collective-permute-done | bytes 2097184 | tf_op jit(solution)/shard_map/ppermute | solution.py:18
  587.4 65.3 %collective-permute-done.30 = f32[64,64,128]{2,1,0:T(8,128)} collective-permute-done((f32[64,64,128]{2,1,0:T(8,128)S(1)}, f32[64,64,128]{2,1,0:T(8,128)}, u32[]{:S(2)}, u32[]{:S(2)}) %collective-permute-start.30) | collective-permute-done | bytes 2097184 | tf_op jit(solution)/shard_map/ppermute | solution.py:18
  654.8 87.8 %collective-permute-done.37 = f32[64,64,128]{2,1,0:T(8,128)} collective-permute-done((f32[64,64,128]{2,1,0:T(8,128)S(1)}, f32[64,64,128]{2,1,0:T(8,128)}, u32[]{:S(2)}, u32[]{:S(2)}) %collective-permute-start.37) | collective-permute-done | bytes 2097184 | tf_op jit(solution)/shard_map/ppermute | solution.py:18
  764.2 23.4 %collective-permute-done.16 = f32[64,64,128]{2,1,0:T(8,128)} collective-permute-done((f32[64,64,128]{2,1,0:T(8,128)}, f32[64,64,128]{2,1,0:T(8,128)}, u32[]{:S(2)}, u32[]{:S(2)}) %collective-permute-start.16) | collective-permute-done | bytes 2097184 | tf_op jit(solution)/shard_map/ppermute | solution.py:18
  796.8 35.7 %collective-permute-done.23 = f32[64,64,128]{2,1,0:T(8,128)} collective-permute-done((f32[64,64,128]{2,1,0:T(8,128)}, f32[64,64,128]{2,1,0:T(8,128)}, u32[]{:S(2)}, u32[]{:S(2)}) %collective-permute-start.23) | collective-permute-done | bytes 2097184 | tf_op jit(solution)/shard_map/ppermute | solution.py:18
  835.5 42.0 %collective-permute-done.2 = f32[64,64,128]{2,1,0:T(8,128)} collective-permute-done((f32[64,64,128]{2,1,0:T(8,128)}, f32[64,64,128]{2,1,0:T(8,128)}, u32[]{:S(2)}, u32[]{:S(2)}) %collective-permute-start.2) | collective-permute-done | bytes 2097184 | tf_op jit(solution)/shard_map/ppermute | solution.py:18
  889.0 31.7 %collective-permute-done.9 = f32[64,64,128]{2,1,0:T(8,128)} collective-permute-done((f32[64,64,128]{2,1,0:T(8,128)}, f32[64,64,128]{2,1,0:T(8,128)}, u32[]{:S(2)}, u32[]{:S(2)}) %collective-permute-start.9) | collective-permute-done | bytes 2097184 | tf_op jit(solution)/shard_map/ppermute | solution.py:18
  935.5 30.1 %collective-permute-done.45 = f32[2,2,16,64,128]{4,3,2,1,0:T(8,128)} collective-permute-done((f32[2,2,16,64,128]{4,3,2,1,0:T(8,128)}, f32[2,2,16,64,128]{4,3,2,1,0:T(8,128)}, u32[]{:S(2)}, u32[]{:S(2)}) %collective-permute-start.45) | collective-permute-done | bytes 2097184 | tf_op jit(solution)/shard_map/ppermute | solution.py:18
  967.7 42.9 %collective-permute-done.52 = f32[2,2,16,64,128]{4,3,2,1,0:T(8,128)} collective-permute-done((f32[2,2,16,64,128]{4,3,2,1,0:T(8,128)}, f32[2,2,16,64,128]{4,3,2,1,0:T(8,128)}, u32[]{:S(2)}, u32[]{:S(2)}) %collective-permute-start.52) | collective-permute-done | bytes 2097184 | tf_op jit(solution)/shard_map/ppermute | solution.py:18
  1014.2 41.3 %collective-permute-done.31 = f32[2,2,16,64,128]{4,3,2,1,0:T(8,128)} collective-permute-done((f32[2,2,16,64,128]{4,3,2,1,0:T(8,128)}, f32[2,2,16,64,128]{4,3,2,1,0:T(8,128)}, u32[]{:S(2)}, u32[]{:S(2)}) %collective-permute-start.31) | collective-permute-done | bytes 2097184 | tf_op jit(solution)/shard_map/ppermute | solution.py:18
  1060.6 39.9 %collective-permute-done.38 = f32[2,2,16,64,128]{4,3,2,1,0:T(8,128)} collective-permute-done((f32[2,2,16,64,128]{4,3,2,1,0:T(8,128)}, f32[2,2,16,64,128]{4,3,2,1,0:T(8,128)}, u32[]{:S(2)}, u32[]{:S(2)}) %collective-permute-start.38) | collective-permute-done | bytes 2097184 | tf_op jit(solution)/shard_map/ppermute | solution.py:18
  1100.4 44.9 %collective-permute-done.17 = f32[2,2,16,64,128]{4,3,2,1,0:T(8,128)} collective-permute-done((f32[2,2,16,64,128]{4,3,2,1,0:T(8,128)S(1)}, f32[2,2,16,64,128]{4,3,2,1,0:T(8,128)}, u32[]{:S(2)}, u32[]{:S(2)}) %collective-permute-start.17) | collective-permute-done | bytes 2097184 | tf_op jit(solution)/shard_map/ppermute | solution.py:18
  1153.0 37.3 %collective-permute-done.24 = f32[2,2,16,64,128]{4,3,2,1,0:T(8,128)} collective-permute-done((f32[2,2,16,64,128]{4,3,2,1,0:T(8,128)S(1)}, f32[2,2,16,64,128]{4,3,2,1,0:T(8,128)}, u32[]{:S(2)}, u32[]{:S(2)}) %collective-permute-start.24) | collective-permute-done | bytes 2097184 | tf_op jit(solution)/shard_map/ppermute | solution.py:18
  1196.0 39.2 %collective-permute-done.3 = f32[2,2,16,64,128]{4,3,2,1,0:T(8,128)S(1)} collective-permute-done((f32[2,2,16,64,128]{4,3,2,1,0:T(8,128)S(1)}, f32[2,2,16,64,128]{4,3,2,1,0:T(8,128)S(1)}, u32[]{:S(2)}, u32[]{:S(2)}) %collective-permute-start.3) | collective-permute-done | bytes 2097184 | tf_op jit(solution)/shard_map/ppermute | solution.py:18
  1244.2 35.9 %collective-permute-done.10 = f32[2,2,16,64,128]{4,3,2,1,0:T(8,128)} collective-permute-done((f32[2,2,16,64,128]{4,3,2,1,0:T(8,128)S(1)}, f32[2,2,16,64,128]{4,3,2,1,0:T(8,128)}, u32[]{:S(2)}, u32[]{:S(2)}) %collective-permute-start.10) | collective-permute-done | bytes 2097184 | tf_op jit(solution)/shard_map/ppermute | solution.py:18
  1288.5 4.8 maximum_bitcast_fusion.7
  1302.0 26.9 %collective-permute-done.18 = f32[1,2,16,128,128]{4,3,2,1,0:T(8,128)} collective-permute-done((f32[1,2,16,128,128]{4,3,2,1,0:T(8,128)}, f32[1,2,16,128,128]{4,3,2,1,0:T(8,128)}, u32[]{:S(2)}, u32[]{:S(2)}) %collective-permute-start.18) | collective-permute-done | bytes 2097184 | tf_op jit(solution)/shard_map/ppermute | solution.py:18
  1332.9 40.9 %collective-permute-done.25 = f32[1,2,16,128,128]{4,3,2,1,0:T(8,128)} collective-permute-done((f32[1,2,16,128,128]{4,3,2,1,0:T(8,128)}, f32[1,2,16,128,128]{4,3,2,1,0:T(8,128)}, u32[]{:S(2)}, u32[]{:S(2)}) %collective-permute-start.25) | collective-permute-done | bytes 2097184 | tf_op jit(solution)/shard_map/ppermute | solution.py:18
  1383.7 35.1 %collective-permute-done.4 = f32[1,2,16,128,128]{4,3,2,1,0:T(8,128)} collective-permute-done((f32[1,2,16,128,128]{4,3,2,1,0:T(8,128)}, f32[1,2,16,128,128]{4,3,2,1,0:T(8,128)}, u32[]{:S(2)}, u32[]{:S(2)}) %collective-permute-start.4) | collective-permute-done | bytes 2097184 | tf_op jit(solution)/shard_map/ppermute | solution.py:18
  1431.3 31.5 %collective-permute-done.11 = f32[1,2,16,128,128]{4,3,2,1,0:T(8,128)} collective-permute-done((f32[1,2,16,128,128]{4,3,2,1,0:T(8,128)}, f32[1,2,16,128,128]{4,3,2,1,0:T(8,128)}, u32[]{:S(2)}, u32[]{:S(2)}) %collective-permute-start.11) | collective-permute-done | bytes 2097184 | tf_op jit(solution)/shard_map/ppermute | solution.py:18
  1480.7 4.9 multiply_add_fusion.1
  1485.7 69.4 %collective-permute-done.33 = f32[2,16,256,128]{3,2,1,0:T(8,128)} collective-permute-done((f32[2,16,256,128]{3,2,1,0:T(8,128)}, f32[2,16,256,128]{3,2,1,0:T(8,128)}, u32[]{:S(2)}, u32[]{:S(2)}) %collective-permute-start.33) | collective-permute-done | bytes 4194336 | tf_op jit(solution)/shard_map/ppermute | solution.py:18
  1564.4 80.5 %collective-permute-done.40 = f32[2,16,256,128]{3,2,1,0:T(8,128)} collective-permute-done((f32[2,16,256,128]{3,2,1,0:T(8,128)}, f32[2,16,256,128]{3,2,1,0:T(8,128)}, u32[]{:S(2)}, u32[]{:S(2)}) %collective-permute-start.40) | collective-permute-done | bytes 4194336 | tf_op jit(solution)/shard_map/ppermute | solution.py:18
  1645.0 6.9 multiply_add_fusion.5
  1658.2 76.7 %collective-permute-done.19 = f32[2,16,256,128]{3,2,1,0:T(8,128)} collective-permute-done((f32[2,16,256,128]{3,2,1,0:T(8,128)}, f32[2,16,256,128]{3,2,1,0:T(8,128)}, u32[]{:S(2)}, u32[]{:S(2)}) %collective-permute-start.19) | collective-permute-done | bytes 4194336 | tf_op jit(solution)/shard_map/ppermute | solution.py:18
  1734.9 89.9 %collective-permute-done.26 = f32[2,16,256,128]{3,2,1,0:T(8,128)} collective-permute-done((f32[2,16,256,128]{3,2,1,0:T(8,128)}, f32[2,16,256,128]{3,2,1,0:T(8,128)}, u32[]{:S(2)}, u32[]{:S(2)}) %collective-permute-start.26) | collective-permute-done | bytes 4194336 | tf_op jit(solution)/shard_map/ppermute | solution.py:18
  1824.7 7.1 multiply_add_fusion.9
  1841.4 73.2 %collective-permute-done.5 = f32[2,16,256,128]{3,2,1,0:T(8,128)} collective-permute-done((f32[2,16,256,128]{3,2,1,0:T(8,128)}, f32[2,16,256,128]{3,2,1,0:T(8,128)}, u32[]{:S(2)}, u32[]{:S(2)}) %collective-permute-start.5) | collective-permute-done | bytes 4194336 | tf_op jit(solution)/shard_map/ppermute | solution.py:18
  1914.6 88.6 %collective-permute-done.12 = f32[2,16,256,128]{3,2,1,0:T(8,128)} collective-permute-done((f32[2,16,256,128]{3,2,1,0:T(8,128)}, f32[2,16,256,128]{3,2,1,0:T(8,128)}, u32[]{:S(2)}, u32[]{:S(2)}) %collective-permute-start.12) | collective-permute-done | bytes 4194336 | tf_op jit(solution)/shard_map/ppermute | solution.py:18
  2003.2 6.8 multiply_add_fusion.13
  2024.2 5.0 multiply_add_fusion
  2029.2 4.9 reshape.594
  2041.8 4.8 multiply_add_fusion.2
  2046.6 5.3 reshape.593
  2051.9 4.5 fusion.26
  2060.0 4.7 multiply_add_fusion.4
  2064.7 4.9 reshape.592
  2077.2 4.9 multiply_add_fusion.6
  2082.1 4.9 reshape.591
  2094.6 4.8 multiply_add_fusion.8
  2099.4 5.0 reshape.590
  2104.5 4.5 fusion.32
  2112.0 4.8 multiply_add_fusion.10
  2116.8 4.9 reshape.589
  2129.3 4.9 multiply_add_fusion.12
  2134.2 4.9 reshape.588
  2146.7 4.8 multiply_add_fusion.14
  2151.5 5.1 reshape.587
  2156.6 4.5 fusion.38
  2163.3 69.3 %last_factors.1 = f32[2,16,32,64,128]{4,3,2,1,0:T(8,128)} custom-call(f32[16,2,32,8,128]{4,3,2,1,0:T(8,128)S(1)} %bitcast.267, f32[16,2,32,8,128]{4,3,2,1,0:T(8,128)S(1)} %bitcast.266, f32[16,2,32,8,128]{4,3,2,1,0:T(8,128)} %bitcast.305, f32[16,2,32,8,128]{4,3,2,1,0:T(8,128)} %bitcast.304, f32[16,2,32,8,128]{4,3,2,1,0:T(8,128)} %bitcast.303, ...), custom_call_target="tpu_custom_call" | custom-call | flops 19327352832 | bytes 67108864 | tf_op jit(solution)/shard_map/last_factors/pallas_call | solution.py:115
  (366 shorter events, 319.8 us)
Async XLA Ops:
  14.9 27.1 %collective-permute-start.42 = (f32[16,128,128]{2,1,0:T(8,128)}, f32[16,128,128]{2,1,0:T(8,128)S(1)}, u32[]{:S(2)}, u32[]{:S(2)}) collective-permute-start(f32[16,128,128]{2,1,0:T(8,128)} %get-tuple-element.67), channel_id=1, source_target_pairs={{0,4},{4,0},{8,12},{12,8},{16,20},{20,16},{24,28},{28,24},{1,5},{5... | collective-permute-start | bytes 3145736 | tf_op jit(solution)/shard_map/ppermute | solution.py:18
  19.3 45.3 %collective-permute-start.49 = (f32[16,128,128]{2,1,0:T(8,128)}, f32[16,128,128]{2,1,0:T(8,128)}, u32[]{:S(2)}, u32[]{:S(2)}) collective-permute-start(f32[16,128,128]{2,1,0:T(8,128)} %get-tuple-element.63), channel_id=1, source_target_pairs={{0,4},{4,0},{8,12},{12,8},{16,20},{20,16},{24,28},{28,24},{1,5},{5... | collective-permute-start | bytes 3145736 | tf_op jit(solution)/shard_map/ppermute | solution.py:18
  20.9 66.3 %collective-permute-start.28 = (f32[16,128,128]{2,1,0:T(8,128)}, f32[16,128,128]{2,1,0:T(8,128)}, u32[]{:S(2)}, u32[]{:S(2)}) collective-permute-start(f32[16,128,128]{2,1,0:T(8,128)} %get-tuple-element.75), channel_id=1, source_target_pairs={{0,4},{4,0},{8,12},{12,8},{16,20},{20,16},{24,28},{28,24},{1,5},{5... | collective-permute-start | bytes 3145736 | tf_op jit(solution)/shard_map/ppermute | solution.py:18
  24.3 85.2 %collective-permute-start.35 = (f32[16,128,128]{2,1,0:T(8,128)}, f32[16,128,128]{2,1,0:T(8,128)}, u32[]{:S(2)}, u32[]{:S(2)}) collective-permute-start(f32[16,128,128]{2,1,0:T(8,128)} %get-tuple-element.71), channel_id=1, source_target_pairs={{0,4},{4,0},{8,12},{12,8},{16,20},{20,16},{24,28},{28,24},{1,5},{5... | collective-permute-start | bytes 3145736 | tf_op jit(solution)/shard_map/ppermute | solution.py:18
  25.9 106.2 %collective-permute-start.14 = (f32[16,128,128]{2,1,0:T(8,128)}, f32[16,128,128]{2,1,0:T(8,128)}, u32[]{:S(2)}, u32[]{:S(2)}) collective-permute-start(f32[16,128,128]{2,1,0:T(8,128)} %get-tuple-element.83), channel_id=1, source_target_pairs={{0,4},{4,0},{8,12},{12,8},{16,20},{20,16},{24,28},{28,24},{1,5},{5... | collective-permute-start | bytes 3145736 | tf_op jit(solution)/shard_map/ppermute | solution.py:18
  42.1 112.5 %collective-permute-start.21 = (f32[16,128,128]{2,1,0:T(8,128)}, f32[16,128,128]{2,1,0:T(8,128)}, u32[]{:S(2)}, u32[]{:S(2)}) collective-permute-start(f32[16,128,128]{2,1,0:T(8,128)} %get-tuple-element.79), channel_id=1, source_target_pairs={{0,4},{4,0},{8,12},{12,8},{16,20},{20,16},{24,28},{28,24},{1,5},{5... | collective-permute-start | bytes 3145736 | tf_op jit(solution)/shard_map/ppermute | solution.py:18
  64.6 95.8 %collective-permute-start.43 = (f32[32,64,128]{2,1,0:T(8,128)}, f32[32,64,128]{2,1,0:T(8,128)}, u32[]{:S(2)}, u32[]{:S(2)}) collective-permute-start(f32[32,64,128]{2,1,0:T(8,128)} %get-tuple-element.66), channel_id=1, source_target_pairs={{0,8},{4,12},{8,0},{12,4},{16,24},{20,28},{24,16},{28,20},{1,9},{5... | collective-permute-start | bytes 3145736 | tf_op jit(solution)/shard_map/ppermute | solution.py:18
  87.1 89.8 %collective-permute-start = (f32[16,128,128]{2,1,0:T(8,128)}, f32[16,128,128]{2,1,0:T(8,128)S(1)}, u32[]{:S(2)}, u32[]{:S(2)}) collective-permute-start(f32[16,128,128]{2,1,0:T(8,128)} %get-tuple-element.91), channel_id=1, source_target_pairs={{0,4},{4,0},{8,12},{12,8},{16,20},{20,16},{24,28},{28,24},{1,5},{5... | collective-permute-start | bytes 3145736 | tf_op jit(solution)/shard_map/ppermute | solution.py:18
  109.6 88.9 %collective-permute-start.7 = (f32[16,128,128]{2,1,0:T(8,128)}, f32[16,128,128]{2,1,0:T(8,128)S(1)}, u32[]{:S(2)}, u32[]{:S(2)}) collective-permute-start(f32[16,128,128]{2,1,0:T(8,128)} %get-tuple-element.87), channel_id=1, source_target_pairs={{0,4},{4,0},{8,12},{12,8},{16,20},{20,16},{24,28},{28,24},{1,5},{5... | collective-permute-start | bytes 3145736 | tf_op jit(solution)/shard_map/ppermute | solution.py:18
  132.1 70.8 %collective-permute-start.50 = (f32[32,64,128]{2,1,0:T(8,128)S(1)}, f32[32,64,128]{2,1,0:T(8,128)S(1)}, u32[]{:S(2)}, u32[]{:S(2)}) collective-permute-start(f32[32,64,128]{2,1,0:T(8,128)S(1)} %get-tuple-element.62), channel_id=1, source_target_pairs={{0,8},{4,12},{8,0},{12,4},{16,24},{20,28},{24,16},{28,20},{1,9},{5... | collective-permute-start | bytes 3145736 | tf_op jit(solution)/shard_map/ppermute | solution.py:18
  154.5 50.3 %collective-permute-start.29 = (f32[32,64,128]{2,1,0:T(8,128)S(1)}, f32[32,64,128]{2,1,0:T(8,128)S(1)}, u32[]{:S(2)}, u32[]{:S(2)}) collective-permute-start(f32[32,64,128]{2,1,0:T(8,128)S(1)} %get-tuple-element.74), channel_id=1, source_target_pairs={{0,8},{4,12},{8,0},{12,4},{16,24},{20,28},{24,16},{28,20},{1,9},{5... | collective-permute-start | bytes 3145736 | tf_op jit(solution)/shard_map/ppermute | solution.py:18
  160.5 65.0 %collective-permute-start.36 = (f32[32,64,128]{2,1,0:T(8,128)S(1)}, f32[32,64,128]{2,1,0:T(8,128)S(1)}, u32[]{:S(2)}, u32[]{:S(2)}) collective-permute-start(f32[32,64,128]{2,1,0:T(8,128)S(1)} %get-tuple-element.70), channel_id=1, source_target_pairs={{0,8},{4,12},{8,0},{12,4},{16,24},{20,28},{24,16},{28,20},{1,9},{5... | collective-permute-start | bytes 3145736 | tf_op jit(solution)/shard_map/ppermute | solution.py:18
  176.9 72.5 %collective-permute-start.15 = (f32[32,64,128]{2,1,0:T(8,128)S(1)}, f32[32,64,128]{2,1,0:T(8,128)S(1)}, u32[]{:S(2)}, u32[]{:S(2)}) collective-permute-start(f32[32,64,128]{2,1,0:T(8,128)S(1)} %get-tuple-element.82), channel_id=1, source_target_pairs={{0,8},{4,12},{8,0},{12,4},{16,24},{20,28},{24,16},{28,20},{1,9},{5... | collective-permute-start | bytes 3145736 | tf_op jit(solution)/shard_map/ppermute | solution.py:18
  198.5 184.4 %collective-permute-start.44 = (f32[64,64,128]{2,1,0:T(8,128)S(1)}, f32[64,64,128]{2,1,0:T(8,128)S(1)}, u32[]{:S(2)}, u32[]{:S(2)}) collective-permute-start(f32[64,64,128]{2,1,0:T(8,128)S(1)} %pad_maximum_fusion.22), channel_id=1, source_target_pairs={{0,16},{4,20},{8,24},{12,28},{16,0},{20,4},{24,8},{28,12},{1,17},{... | collective-permute-start | bytes 6291464 | tf_op jit(solution)/shard_map/ppermute | solution.py:18
  202.9 134.9 %collective-permute-start.22 = (f32[32,64,128]{2,1,0:T(8,128)S(1)}, f32[32,64,128]{2,1,0:T(8,128)S(1)}, u32[]{:S(2)}, u32[]{:S(2)}) collective-permute-start(f32[32,64,128]{2,1,0:T(8,128)S(1)} %get-tuple-element.78), channel_id=1, source_target_pairs={{0,8},{4,12},{8,0},{12,4},{16,24},{20,28},{24,16},{28,20},{1,9},{5... | collective-permute-start | bytes 3145736 | tf_op jit(solution)/shard_map/ppermute | solution.py:18
  204.9 156.9 %collective-permute-start.1 = (f32[32,64,128]{2,1,0:T(8,128)S(1)}, f32[32,64,128]{2,1,0:T(8,128)S(1)}, u32[]{:S(2)}, u32[]{:S(2)}) collective-permute-start(f32[32,64,128]{2,1,0:T(8,128)S(1)} %get-tuple-element.90), channel_id=1, source_target_pairs={{0,8},{4,12},{8,0},{12,4},{16,24},{20,28},{24,16},{28,20},{1,9},{5... | collective-permute-start | bytes 3145736 | tf_op jit(solution)/shard_map/ppermute | solution.py:18
  225.5 156.0 %collective-permute-start.8 = (f32[32,64,128]{2,1,0:T(8,128)S(1)}, f32[32,64,128]{2,1,0:T(8,128)S(1)}, u32[]{:S(2)}, u32[]{:S(2)}) collective-permute-start(f32[32,64,128]{2,1,0:T(8,128)S(1)} %get-tuple-element.86), channel_id=1, source_target_pairs={{0,8},{4,12},{8,0},{12,4},{16,24},{20,28},{24,16},{28,20},{1,9},{5... | collective-permute-start | bytes 3145736 | tf_op jit(solution)/shard_map/ppermute | solution.py:18
  249.4 335.8 %collective-permute-start.51 = (f32[64,64,128]{2,1,0:T(8,128)S(1)}, f32[64,64,128]{2,1,0:T(8,128)}, u32[]{:S(2)}, u32[]{:S(2)}) collective-permute-start(f32[64,64,128]{2,1,0:T(8,128)S(1)} %pad_maximum_fusion.23), channel_id=1, source_target_pairs={{0,16},{4,20},{8,24},{12,28},{16,0},{20,4},{24,8},{28,12},{1,17},{... | collective-permute-start | bytes 6291464 | tf_op jit(solution)/shard_map/ppermute | solution.py:18
  337.8 314.9 %collective-permute-start.30 = (f32[64,64,128]{2,1,0:T(8,128)S(1)}, f32[64,64,128]{2,1,0:T(8,128)}, u32[]{:S(2)}, u32[]{:S(2)}) collective-permute-start(f32[64,64,128]{2,1,0:T(8,128)S(1)} %pad_maximum_fusion.20), channel_id=1, source_target_pairs={{0,16},{4,20},{8,24},{12,28},{16,0},{20,4},{24,8},{28,12},{1,17},{... | collective-permute-start | bytes 6291464 | tf_op jit(solution)/shard_map/ppermute | solution.py:18
  361.7 380.8 %collective-permute-start.37 = (f32[64,64,128]{2,1,0:T(8,128)S(1)}, f32[64,64,128]{2,1,0:T(8,128)}, u32[]{:S(2)}, u32[]{:S(2)}) collective-permute-start(f32[64,64,128]{2,1,0:T(8,128)S(1)} %pad_maximum_fusion.21), channel_id=1, source_target_pairs={{0,16},{4,20},{8,24},{12,28},{16,0},{20,4},{24,8},{28,12},{1,17},{... | collective-permute-start | bytes 6291464 | tf_op jit(solution)/shard_map/ppermute | solution.py:18
  381.5 406.0 %collective-permute-start.16 = (f32[64,64,128]{2,1,0:T(8,128)}, f32[64,64,128]{2,1,0:T(8,128)}, u32[]{:S(2)}, u32[]{:S(2)}) collective-permute-start(f32[64,64,128]{2,1,0:T(8,128)} %pad_maximum_fusion.18), channel_id=1, source_target_pairs={{0,16},{4,20},{8,24},{12,28},{16,0},{20,4},{24,8},{28,12},{1,17},{... | collective-permute-start | bytes 6291464 | tf_op jit(solution)/shard_map/ppermute | solution.py:18
  383.0 449.5 %collective-permute-start.23 = (f32[64,64,128]{2,1,0:T(8,128)}, f32[64,64,128]{2,1,0:T(8,128)}, u32[]{:S(2)}, u32[]{:S(2)}) collective-permute-start(f32[64,64,128]{2,1,0:T(8,128)} %pad_maximum_fusion.19), channel_id=1, source_target_pairs={{0,16},{4,20},{8,24},{12,28},{16,0},{20,4},{24,8},{28,12},{1,17},{... | collective-permute-start | bytes 6291464 | tf_op jit(solution)/shard_map/ppermute | solution.py:18
  585.2 292.2 %collective-permute-start.2 = (f32[64,64,128]{2,1,0:T(8,128)}, f32[64,64,128]{2,1,0:T(8,128)}, u32[]{:S(2)}, u32[]{:S(2)}) collective-permute-start(f32[64,64,128]{2,1,0:T(8,128)} %pad_maximum_fusion.16), channel_id=1, source_target_pairs={{0,16},{4,20},{8,24},{12,28},{16,0},{20,4},{24,8},{28,12},{1,17},{... | collective-permute-start | bytes 6291464 | tf_op jit(solution)/shard_map/ppermute | solution.py:18
  652.6 268.0 %collective-permute-start.9 = (f32[64,64,128]{2,1,0:T(8,128)}, f32[64,64,128]{2,1,0:T(8,128)}, u32[]{:S(2)}, u32[]{:S(2)}) collective-permute-start(f32[64,64,128]{2,1,0:T(8,128)} %pad_maximum_fusion.17), channel_id=1, source_target_pairs={{0,16},{4,20},{8,24},{12,28},{16,0},{20,4},{24,8},{28,12},{1,17},{... | collective-permute-start | bytes 6291464 | tf_op jit(solution)/shard_map/ppermute | solution.py:18
  742.6 223.1 %collective-permute-start.45 = (f32[2,2,16,64,128]{4,3,2,1,0:T(8,128)}, f32[2,2,16,64,128]{4,3,2,1,0:T(8,128)}, u32[]{:S(2)}, u32[]{:S(2)}) collective-permute-start(f32[2,2,16,64,128]{4,3,2,1,0:T(8,128)} %bitcast.139), channel_id=1, source_target_pairs={{0,8},{4,12},{8,0},{12,4},{16,24},{20,28},{24,16},{28,20},{1,9},{5... | collective-permute-start | bytes 6291464 | tf_op jit(solution)/shard_map/ppermute | solution.py:18
  787.6 223.0 %collective-permute-start.52 = (f32[2,2,16,64,128]{4,3,2,1,0:T(8,128)}, f32[2,2,16,64,128]{4,3,2,1,0:T(8,128)}, u32[]{:S(2)}, u32[]{:S(2)}) collective-permute-start(f32[2,2,16,64,128]{4,3,2,1,0:T(8,128)} %bitcast.153), channel_id=1, source_target_pairs={{0,8},{4,12},{8,0},{12,4},{16,24},{20,28},{24,16},{28,20},{1,9},{5... | collective-permute-start | bytes 6291464 | tf_op jit(solution)/shard_map/ppermute | solution.py:18
  832.5 223.0 %collective-permute-start.31 = (f32[2,2,16,64,128]{4,3,2,1,0:T(8,128)}, f32[2,2,16,64,128]{4,3,2,1,0:T(8,128)}, u32[]{:S(2)}, u32[]{:S(2)}) collective-permute-start(f32[2,2,16,64,128]{4,3,2,1,0:T(8,128)} %bitcast.111), channel_id=1, source_target_pairs={{0,8},{4,12},{8,0},{12,4},{16,24},{20,28},{24,16},{28,20},{1,9},{5... | collective-permute-start | bytes 6291464 | tf_op jit(solution)/shard_map/ppermute | solution.py:18
  877.4 223.0 %collective-permute-start.38 = (f32[2,2,16,64,128]{4,3,2,1,0:T(8,128)}, f32[2,2,16,64,128]{4,3,2,1,0:T(8,128)}, u32[]{:S(2)}, u32[]{:S(2)}) collective-permute-start(f32[2,2,16,64,128]{4,3,2,1,0:T(8,128)} %bitcast.125), channel_id=1, source_target_pairs={{0,8},{4,12},{8,0},{12,4},{16,24},{20,28},{24,16},{28,20},{1,9},{5... | collective-permute-start | bytes 6291464 | tf_op jit(solution)/shard_map/ppermute | solution.py:18
  920.7 224.7 %collective-permute-start.17 = (f32[2,2,16,64,128]{4,3,2,1,0:T(8,128)S(1)}, f32[2,2,16,64,128]{4,3,2,1,0:T(8,128)}, u32[]{:S(2)}, u32[]{:S(2)}) collective-permute-start(f32[2,2,16,64,128]{4,3,2,1,0:T(8,128)S(1)} %bitcast.306), channel_id=1, source_target_pairs={{0,8},{4,12},{8,0},{12,4},{16,24},{20,28},{24,16},{28,20},{1,9},{5... | collective-permute-start | bytes 6291464 | tf_op jit(solution)/shard_map/ppermute | solution.py:18
  965.6 224.7 %collective-permute-start.24 = (f32[2,2,16,64,128]{4,3,2,1,0:T(8,128)S(1)}, f32[2,2,16,64,128]{4,3,2,1,0:T(8,128)}, u32[]{:S(2)}, u32[]{:S(2)}) collective-permute-start(f32[2,2,16,64,128]{4,3,2,1,0:T(8,128)S(1)} %bitcast.309), channel_id=1, source_target_pairs={{0,8},{4,12},{8,0},{12,4},{16,24},{20,28},{24,16},{28,20},{1,9},{5... | collective-permute-start | bytes 6291464 | tf_op jit(solution)/shard_map/ppermute | solution.py:18
  1010.5 224.6 %collective-permute-start.3 = (f32[2,2,16,64,128]{4,3,2,1,0:T(8,128)S(1)}, f32[2,2,16,64,128]{4,3,2,1,0:T(8,128)S(1)}, u32[]{:S(2)}, u32[]{:S(2)}) collective-permute-start(f32[2,2,16,64,128]{4,3,2,1,0:T(8,128)S(1)} %bitcast.308), channel_id=1, source_target_pairs={{0,8},{4,12},{8,0},{12,4},{16,24},{20,28},{24,16},{28,20},{1,9},{5... | collective-permute-start | bytes 6291464 | tf_op jit(solution)/shard_map/ppermute | solution.py:18
  1014.2 227.5 %copy-start.33 = (f32[1,2,16,128,128]{4,3,2,1,0:T(8,128)}, f32[1,2,16,128,128]{4,3,2,1,0:T(8,128)S(1)}, u32[]{:S(2)}) copy-start(f32[1,2,16,128,128]{4,3,2,1,0:T(8,128)S(1)} %get-tuple-element.21) | copy-start | bytes 6291460
  1055.5 182.8 %collective-permute-start.46 = (f32[1,2,16,128,128]{4,3,2,1,0:T(8,128)}, f32[1,2,16,128,128]{4,3,2,1,0:T(8,128)S(1)}, u32[]{:S(2)}, u32[]{:S(2)}) collective-permute-start(f32[1,2,16,128,128]{4,3,2,1,0:T(8,128)} %get-tuple-element.22), channel_id=1, source_target_pairs={{0,4},{4,0},{8,12},{12,8},{16,20},{20,16},{24,28},{28,24},{1,5},{5... | collective-permute-start | bytes 6291464 | tf_op jit(solution)/shard_map/ppermute | solution.py:18
  1100.4 179.7 %collective-permute-start.10 = (f32[2,2,16,64,128]{4,3,2,1,0:T(8,128)S(1)}, f32[2,2,16,64,128]{4,3,2,1,0:T(8,128)}, u32[]{:S(2)}, u32[]{:S(2)}) collective-permute-start(f32[2,2,16,64,128]{4,3,2,1,0:T(8,128)S(1)} %bitcast.307), channel_id=1, source_target_pairs={{0,8},{4,12},{8,0},{12,4},{16,24},{20,28},{24,16},{28,20},{1,9},{5... | collective-permute-start | bytes 6291464 | tf_op jit(solution)/shard_map/ppermute | solution.py:18
  1145.4 136.2 %collective-permute-start.53 = (f32[1,2,16,128,128]{4,3,2,1,0:T(8,128)S(1)}, f32[1,2,16,128,128]{4,3,2,1,0:T(8,128)}, u32[]{:S(2)}, u32[]{:S(2)}) collective-permute-start(f32[1,2,16,128,128]{4,3,2,1,0:T(8,128)S(1)} %get-tuple-element.16), channel_id=1, source_target_pairs={{0,4},{4,0},{8,12},{12,8},{16,20},{20,16},{24,28},{28,24},{1,5},{5... | collective-permute-start | bytes 6291464 | tf_op jit(solution)/shard_map/ppermute | solution.py:18
  1190.3 97.6 %collective-permute-start.32 = (f32[1,2,16,128,128]{4,3,2,1,0:T(8,128)}, f32[1,2,16,128,128]{4,3,2,1,0:T(8,128)}, u32[]{:S(2)}, u32[]{:S(2)}) collective-permute-start(f32[1,2,16,128,128]{4,3,2,1,0:T(8,128)} %get-tuple-element.34), channel_id=1, source_target_pairs={{0,4},{4,0},{8,12},{12,8},{16,20},{20,16},{24,28},{28,24},{1,5},{5... | collective-permute-start | bytes 6291464 | tf_op jit(solution)/shard_map/ppermute | solution.py:18
  1235.2 58.1 %collective-permute-start.39 = (f32[1,2,16,128,128]{4,3,2,1,0:T(8,128)}, f32[1,2,16,128,128]{4,3,2,1,0:T(8,128)}, u32[]{:S(2)}, u32[]{:S(2)}) collective-permute-start(f32[1,2,16,128,128]{4,3,2,1,0:T(8,128)} %get-tuple-element.28), channel_id=1, source_target_pairs={{0,4},{4,0},{8,12},{12,8},{16,20},{20,16},{24,28},{28,24},{1,5},{5... | collective-permute-start | bytes 6291464 | tf_op jit(solution)/shard_map/ppermute | solution.py:18
  1238.3 184.6 %copy-start.31 = (f32[1,2,16,128,128]{4,3,2,1,0:T(8,128)}, f32[1,2,16,128,128]{4,3,2,1,0:T(8,128)S(1)}, u32[]{:S(2)}) copy-start(f32[1,2,16,128,128]{4,3,2,1,0:T(8,128)S(1)} %get-tuple-element.45) | copy-start | bytes 6291460
  1238.3 90.6 %collective-permute-start.18 = (f32[1,2,16,128,128]{4,3,2,1,0:T(8,128)}, f32[1,2,16,128,128]{4,3,2,1,0:T(8,128)}, u32[]{:S(2)}, u32[]{:S(2)}) collective-permute-start(f32[1,2,16,128,128]{4,3,2,1,0:T(8,128)} %get-tuple-element.46), channel_id=1, source_target_pairs={{0,4},{4,0},{8,12},{12,8},{16,20},{20,16},{24,28},{28,24},{1,5},{5... | collective-permute-start | bytes 6291464 | tf_op jit(solution)/shard_map/ppermute | solution.py:18
  1280.1 93.7 %collective-permute-start.25 = (f32[1,2,16,128,128]{4,3,2,1,0:T(8,128)}, f32[1,2,16,128,128]{4,3,2,1,0:T(8,128)}, u32[]{:S(2)}, u32[]{:S(2)}) collective-permute-start(f32[1,2,16,128,128]{4,3,2,1,0:T(8,128)} %get-tuple-element.40), channel_id=1, source_target_pairs={{0,4},{4,0},{8,12},{12,8},{16,20},{20,16},{24,28},{28,24},{1,5},{5... | collective-permute-start | bytes 6291464 | tf_op jit(solution)/shard_map/ppermute | solution.py:18
  1281.5 182.7 %collective-permute-start.47 = (f32[2,16,256,128]{3,2,1,0:T(8,128)}, f32[2,16,256,128]{3,2,1,0:T(8,128)}, u32[]{:S(2)}, u32[]{:S(2)}) collective-permute-start(f32[2,16,256,128]{3,2,1,0:T(8,128)} %maximum_bitcast_fusion.6), channel_id=1, source_target_pairs={{0,2},{1,3},{2,0},{3,1},{4,6},{5,7},{6,4},{7,5},{8,10},{9,11},{10,... | collective-permute-start | bytes 12582920 | tf_op jit(solution)/shard_map/ppermute | solution.py:18
  1283.1 93.2 %copy-start.63 = (s32[64,128]{1,0:T(8,128)}, s32[64,128]{1,0:T(8,128)S(1)}, u32[]{:S(2)}) copy-start(s32[64,128]{1,0:T(8,128)S(1)} %multiply_add_fusion.24) | copy-start | bytes 98308
  1287.9 130.8 %collective-permute-start.4 = (f32[1,2,16,128,128]{4,3,2,1,0:T(8,128)}, f32[1,2,16,128,128]{4,3,2,1,0:T(8,128)}, u32[]{:S(2)}, u32[]{:S(2)}) collective-permute-start(f32[1,2,16,128,128]{4,3,2,1,0:T(8,128)} %get-tuple-element.58), channel_id=1, source_target_pairs={{0,4},{4,0},{8,12},{12,8},{16,20},{20,16},{24,28},{28,24},{1,5},{5... | collective-permute-start | bytes 6291464 | tf_op jit(solution)/shard_map/ppermute | solution.py:18
  1293.2 186.1 %collective-permute-start.54 = (f32[2,16,256,128]{3,2,1,0:T(8,128)}, f32[2,16,256,128]{3,2,1,0:T(8,128)}, u32[]{:S(2)}, u32[]{:S(2)}) collective-permute-start(f32[2,16,256,128]{3,2,1,0:T(8,128)} %maximum_bitcast_fusion.7), channel_id=1, source_target_pairs={{0,2},{1,3},{2,0},{3,1},{4,6},{5,7},{6,4},{7,5},{8,10},{9,11},{10,... | collective-permute-start | bytes 12582920 | tf_op jit(solution)/shard_map/ppermute | solution.py:18
  1302.0 74.2 %copy-start.65 = (f32[128,128]{1,0:T(8,128)S(1)}, f32[128,128]{1,0:T(8,128)}, u32[]{:S(2)}) copy-start(f32[128,128]{1,0:T(8,128)} %fusion.99) | copy-start | bytes 196612
  1302.0 77.6 %copy-start.39 = (f32[1,2,16,128,128]{4,3,2,1,0:T(8,128)S(1)}, f32[1,2,16,128,128]{4,3,2,1,0:T(8,128)}, u32[]{:S(2)}) copy-start(f32[1,2,16,128,128]{4,3,2,1,0:T(8,128)} %get-tuple-element.27) | copy-start | bytes 6291460
  1328.9 226.2 %collective-permute-start.33 = (f32[2,16,256,128]{3,2,1,0:T(8,128)}, f32[2,16,256,128]{3,2,1,0:T(8,128)}, u32[]{:S(2)}, u32[]{:S(2)}) collective-permute-start(f32[2,16,256,128]{3,2,1,0:T(8,128)} %maximum_bitcast_fusion.4), channel_id=1, source_target_pairs={{0,2},{1,3},{2,0},{3,1},{4,6},{5,7},{6,4},{7,5},{8,10},{9,11},{10,... | collective-permute-start | bytes 12582920 | tf_op jit(solution)/shard_map/ppermute | solution.py:18
  1373.8 89.0 %collective-permute-start.11 = (f32[1,2,16,128,128]{4,3,2,1,0:T(8,128)}, f32[1,2,16,128,128]{4,3,2,1,0:T(8,128)}, u32[]{:S(2)}, u32[]{:S(2)}) collective-permute-start(f32[1,2,16,128,128]{4,3,2,1,0:T(8,128)} %get-tuple-element.52), channel_id=1, source_target_pairs={{0,4},{4,0},{8,12},{12,8},{16,20},{20,16},{24,28},{28,24},{1,5},{5... | collective-permute-start | bytes 6291464 | tf_op jit(solution)/shard_map/ppermute | solution.py:18
  1418.8 226.2 %collective-permute-start.40 = (f32[2,16,256,128]{3,2,1,0:T(8,128)}, f32[2,16,256,128]{3,2,1,0:T(8,128)}, u32[]{:S(2)}, u32[]{:S(2)}) collective-permute-start(f32[2,16,256,128]{3,2,1,0:T(8,128)} %maximum_bitcast_fusion.5), channel_id=1, source_target_pairs={{0,2},{1,3},{2,0},{3,1},{4,6},{5,7},{6,4},{7,5},{8,10},{9,11},{10,... | collective-permute-start | bytes 12582920 | tf_op jit(solution)/shard_map/ppermute | solution.py:18
  1462.8 272.1 %collective-permute-start.19 = (f32[2,16,256,128]{3,2,1,0:T(8,128)}, f32[2,16,256,128]{3,2,1,0:T(8,128)}, u32[]{:S(2)}, u32[]{:S(2)}) collective-permute-start(f32[2,16,256,128]{3,2,1,0:T(8,128)} %maximum_bitcast_fusion.2), channel_id=1, source_target_pairs={{0,2},{1,3},{2,0},{3,1},{4,6},{5,7},{6,4},{7,5},{8,10},{9,11},{10,... | collective-permute-start | bytes 12582920 | tf_op jit(solution)/shard_map/ppermute | solution.py:18
  1464.3 360.5 %collective-permute-start.26 = (f32[2,16,256,128]{3,2,1,0:T(8,128)}, f32[2,16,256,128]{3,2,1,0:T(8,128)}, u32[]{:S(2)}, u32[]{:S(2)}) collective-permute-start(f32[2,16,256,128]{3,2,1,0:T(8,128)} %maximum_bitcast_fusion.3), channel_id=1, source_target_pairs={{0,2},{1,3},{2,0},{3,1},{4,6},{5,7},{6,4},{7,5},{8,10},{9,11},{10,... | collective-permute-start | bytes 12582920 | tf_op jit(solution)/shard_map/ppermute | solution.py:18
  1479.3 435.3 %collective-permute-start.5 = (f32[2,16,256,128]{3,2,1,0:T(8,128)}, f32[2,16,256,128]{3,2,1,0:T(8,128)}, u32[]{:S(2)}, u32[]{:S(2)}) collective-permute-start(f32[2,16,256,128]{3,2,1,0:T(8,128)} %maximum_bitcast_fusion), channel_id=1, source_target_pairs={{0,2},{1,3},{2,0},{3,1},{4,6},{5,7},{6,4},{7,5},{8,10},{9,11},{10,... | collective-permute-start | bytes 12582920 | tf_op jit(solution)/shard_map/ppermute | solution.py:18
  1555.1 448.2 %collective-permute-start.12 = (f32[2,16,256,128]{3,2,1,0:T(8,128)}, f32[2,16,256,128]{3,2,1,0:T(8,128)}, u32[]{:S(2)}, u32[]{:S(2)}) collective-permute-start(f32[2,16,256,128]{3,2,1,0:T(8,128)} %maximum_bitcast_fusion.1), channel_id=1, source_target_pairs={{0,2},{1,3},{2,0},{3,1},{4,6},{5,7},{6,4},{7,5},{8,10},{9,11},{10,... | collective-permute-start | bytes 12582920 | tf_op jit(solution)/shard_map/ppermute | solution.py:18
  1560.3 84.6 %copy-start.36 = (f32[1,2,16,128,128]{4,3,2,1,0:T(8,128)S(1)}, f32[1,2,16,128,128]{4,3,2,1,0:T(8,128)}, u32[]{:S(2)}) copy-start(f32[1,2,16,128,128]{4,3,2,1,0:T(8,128)} %get-tuple-element.33) | copy-start | bytes 6291460
  1560.4 84.6 %copy-start.40 = (f32[1,2,16,128,128]{4,3,2,1,0:T(8,128)S(1)}, f32[1,2,16,128,128]{4,3,2,1,0:T(8,128)}, u32[]{:S(2)}) copy-start(f32[1,2,16,128,128]{4,3,2,1,0:T(8,128)} %get-tuple-element.27) | copy-start | bytes 6291460
  1645.0 378.7 %collective-permute-start.55 = (f32[2,16,256,128]{3,2,1,0:T(8,128)}, f32[2,16,256,128]{3,2,1,0:T(8,128)}, u32[]{:S(2)}, u32[]{:S(2)}) collective-permute-start(f32[2,16,256,128]{3,2,1,0:T(8,128)} %pad_maximum_fusion.15), channel_id=1, source_target_pairs={{0,1},{1,0},{2,3},{3,2},{4,5},{5,4},{6,7},{7,6},{8,9},{9,8},{10,11... | collective-permute-start | bytes 12582920 | tf_op jit(solution)/shard_map/ppermute | solution.py:18
  1654.8 170.0 %copy-start.32 = (f32[1,2,16,128,128]{4,3,2,1,0:T(8,128)S(1)}, f32[1,2,16,128,128]{4,3,2,1,0:T(8,128)}, u32[]{:S(2)}) copy-start(f32[1,2,16,128,128]{4,3,2,1,0:T(8,128)} %copy-done.31) | copy-start | bytes 6291460
  1734.9 306.9 %collective-permute-start.48 = (f32[2,16,256,128]{3,2,1,0:T(8,128)}, f32[2,16,256,128]{3,2,1,0:T(8,128)}, u32[]{:S(2)}, u32[]{:S(2)}) collective-permute-start(f32[2,16,256,128]{3,2,1,0:T(8,128)} %pad_maximum_fusion.13), channel_id=1, source_target_pairs={{0,1},{1,0},{2,3},{3,2},{4,5},{5,4},{6,7},{7,6},{8,9},{9,8},{10,11... | collective-permute-start | bytes 12582920 | tf_op jit(solution)/shard_map/ppermute | solution.py:18
  1824.7 234.8 %collective-permute-start.41 = (f32[2,16,256,128]{3,2,1,0:T(8,128)}, f32[2,16,256,128]{3,2,1,0:T(8,128)}, u32[]{:S(2)}, u32[]{:S(2)}) collective-permute-start(f32[2,16,256,128]{3,2,1,0:T(8,128)} %pad_maximum_fusion.11), channel_id=1, source_target_pairs={{0,1},{1,0},{2,3},{3,2},{4,5},{5,4},{6,7},{7,6},{8,9},{9,8},{10,11... | collective-permute-start | bytes 12582920 | tf_op jit(solution)/shard_map/ppermute | solution.py:18
  1914.6 162.6 %collective-permute-start.34 = (f32[2,16,256,128]{3,2,1,0:T(8,128)}, f32[2,16,256,128]{3,2,1,0:T(8,128)}, u32[]{:S(2)}, u32[]{:S(2)}) collective-permute-start(f32[2,16,256,128]{3,2,1,0:T(8,128)} %pad_maximum_fusion.9), channel_id=1, source_target_pairs={{0,1},{1,0},{2,3},{3,2},{4,5},{5,4},{6,7},{7,6},{8,9},{9,8},{10,11... | collective-permute-start | bytes 12582920 | tf_op jit(solution)/shard_map/ppermute | solution.py:18
  2003.2 91.3 %collective-permute-start.27 = (f32[2,16,256,128]{3,2,1,0:T(8,128)}, f32[2,16,256,128]{3,2,1,0:T(8,128)}, u32[]{:S(2)}, u32[]{:S(2)}) collective-permute-start(f32[2,16,256,128]{3,2,1,0:T(8,128)} %pad_maximum_fusion.7), channel_id=1, source_target_pairs={{0,1},{1,0},{2,3},{3,2},{4,5},{5,4},{6,7},{7,6},{8,9},{9,8},{10,11... | collective-permute-start | bytes 12582920 | tf_op jit(solution)/shard_map/ppermute | solution.py:18
  2023.7 88.3 %collective-permute-start.20 = (f32[2,16,256,128]{3,2,1,0:T(8,128)}, f32[2,16,256,128]{3,2,1,0:T(8,128)}, u32[]{:S(2)}, u32[]{:S(2)}) collective-permute-start(f32[2,16,256,128]{3,2,1,0:T(8,128)} %pad_maximum_fusion.5), channel_id=1, source_target_pairs={{0,1},{1,0},{2,3},{3,2},{4,5},{5,4},{6,7},{7,6},{8,9},{9,8},{10,11... | collective-permute-start | bytes 12582920 | tf_op jit(solution)/shard_map/ppermute | solution.py:18
  2041.8 87.5 %collective-permute-start.13 = (f32[2,16,256,128]{3,2,1,0:T(8,128)}, f32[2,16,256,128]{3,2,1,0:T(8,128)}, u32[]{:S(2)}, u32[]{:S(2)}) collective-permute-start(f32[2,16,256,128]{3,2,1,0:T(8,128)} %pad_maximum_fusion.3), channel_id=1, source_target_pairs={{0,1},{1,0},{2,3},{3,2},{4,5},{5,4},{6,7},{7,6},{8,9},{9,8},{10,11... | collective-permute-start | bytes 12582920 | tf_op jit(solution)/shard_map/ppermute | solution.py:18
  2059.5 87.2 %collective-permute-start.6 = (f32[2,16,256,128]{3,2,1,0:T(8,128)}, f32[2,16,256,128]{3,2,1,0:T(8,128)}, u32[]{:S(2)}, u32[]{:S(2)}) collective-permute-start(f32[2,16,256,128]{3,2,1,0:T(8,128)} %pad_maximum_fusion.1), channel_id=1, source_target_pairs={{0,1},{1,0},{2,3},{3,2},{4,5},{5,4},{6,7},{7,6},{8,9},{9,8},{10,11... | collective-permute-start | bytes 12582920 | tf_op jit(solution)/shard_map/ppermute | solution.py:18
  (62 other events, 769.6 us)

commit v2 on v1

--- a/solution.py
+++ b/solution.py
@@ -11,6 +11,7 @@
 SPLIT = lax.Precision.HIGH
 TWO_PI = 2.0 * math.pi
 CHUNKS = 8
+SPLIT_B = 2
 
 
 def swap(block, axis, place):
@@ -149,6 +150,7 @@
     narrow_at = lax.axis_index("narrow")
     bits = [wide_at // (1 << place) % 2 for place in range(levels)]
     share_c = size_c // CHUNKS
+    share_b = local_b // SPLIT_B
 
     def positions(slots):
         return (
@@ -168,7 +170,7 @@
     index_m = jnp.arange(local_b, dtype=jnp.int32)
     outputs_b = narrow_size * index_m + reversed_digits(narrow_at, narrow_levels)
     mask = 0
-    left_b = local_b
+    left_b = share_b
     for bit in bits:
         left_b //= 2
         mask = mask + bit * left_b
@@ -192,42 +194,87 @@
     high, low = two_parts(jnp.block([[cosine, -sines], [sines, cosine]]))
     table_d = jnp.concatenate([high, high, low], axis=0)
 
+    def slab(chunk):
+        low_b, low_c = chunk % SPLIT_B * share_b, chunk // SPLIT_B * share_c
+        values = record[:, low_b : low_b + share_b, low_c : low_c + share_c, :]
+        return values.reshape(local_a, share_b * share_c, size_d)
+
+    def stage(step, keep, other):
+        if step <= levels:
+            values = keep if step == 0 else jnp.concatenate([keep, other], axis=0)
+            if step == levels:
+                return values, values, ("wide", levels)
+            return *halves(values, bits[step]), ("wide", step)
+        step -= levels + 1
+        if step <= levels:
+            if step == 0:
+                values = jnp.concatenate([keep, other], axis=0)
+                spread = jnp.einsum("pa,ard->prd", table_a, values, precision=SPLIT).reshape(
+                    wide_size // 2, 2, local_a, values.shape[1], size_d
+                )
+            else:
+                spread = jnp.concatenate([keep, other], axis=3)
+                if keep.shape[3] < share_c:
+                    spread = jnp.where(
+                        bits[levels - step] > 0,
+                        jnp.concatenate([other, keep], axis=3),
+                        spread,
+                    )
+            if step < levels:
+                half = spread.shape[0] // 2
+                return spread[:half], spread[half:], ("wide", levels - 1 - step)
+            return spread[0], spread[0], ("narrow", narrow_levels - 1)
+        place = narrow_levels + levels - step
+        upper = narrow_at // (1 << place) % 2
+        current = other + (1 - 2 * upper).astype(jnp.float32) * keep
+        if place == 0:
+            return current, None, None
+        cosine, sines = turn(upper * (narrow_at % (1 << place)), 2 << place)
+        current = jnp.stack(
+            [
+                current[0] * cosine + current[1] * sines,
+                current[1] * cosine - current[0] * sines,
+            ]
+        )
+        return current, current, ("narrow", place - 1)
+
+    count = CHUNKS * SPLIT_B
+    steps = 2 * levels + 2 + narrow_levels
+    starts = [0.35 * step - 0.5 for step in range(levels + 1)]
+    starts += [1.4 + 0.35 * levels + 0.7 * step for step in range(levels + 1)]
+    starts += [starts[-1] + 0.14 + 1.4 * step for step in range(1, narrow_levels)]
+    starts += [starts[-1] + 0.14]
+    if narrow_levels > 1:
+        starts[-1] = starts[-2] + 0.14
+    plan = sorted(
+        ((chunk + starts[step], chunk, step) for chunk in range(count) for step in range(steps))
+    )
+    held = {}
+    before = None
+    for _, chunk, step in plan:
+        keep, other = held.pop(chunk) if step else (slab(chunk), None)
+        if before is not None and before != chunk:
+            rest = held[before][0]
+            if other is None:
+                keep, rest = lax.optimization_barrier((keep, rest))
+            else:
+                keep, other, rest = lax.optimization_barrier((keep, other, rest))
+            held[before] = (rest, held[before][1])
+        keep, send, way = stage(step, keep, other)
+        held[chunk] = (keep, None if send is None else swap(send, *way))
+        before = chunk
+
     sections = []
     for chunk in range(CHUNKS):
-        values = lax.slice_in_dim(record, chunk * share_c, (chunk + 1) * share_c, axis=2)
-        values = values.reshape(local_a, local_b * share_c, size_d)
-        for place in range(levels):
-            keep, send = halves(values, bits[place])
-            values = jnp.concatenate([keep, swap(send, "wide", place)], axis=0)
-        values = jnp.concatenate([values, swap(values, "wide", levels)], axis=0)
-        rows = values.shape[1]
-        spread = jnp.einsum(
-            "pa,an->pn", table_a, values.reshape(size_a, rows * size_d), precision=SPLIT
-        ).reshape(wide_size // 2, 2, local_a, rows, size_d)
-        for place in reversed(range(levels)):
-            half = spread.shape[0] // 2
-            mine, other = spread[:half], swap(spread[half:], "wide", place)
-            spread = jnp.concatenate([mine, other], axis=3)
-            if mine.shape[3] < share_c:
-                spread = jnp.where(
-                    bits[place] > 0, jnp.concatenate([other, mine], axis=3), spread
-                )
-        current = spread[0]
-        for place in reversed(range(narrow_levels)):
-            partner = swap(current, "narrow", place)
-            upper = narrow_at // (1 << place) % 2
-            current = partner + (1 - 2 * upper).astype(jnp.float32) * current
-            if place > 0:
-                cosine, sines = turn(upper * (narrow_at % (1 << place)), 2 << place)
-                current = jnp.stack(
-                    [
-                        current[0] * cosine + current[1] * sines,
-                        current[1] * cosine - current[0] * sines,
-                    ]
-                )
-        current = current.reshape(2, local_a, local_b, share_c * size_d)
-        section = jnp.einsum("aomib,iabn->aomn", table_b, current, precision=SPLIT)
-        sections.append(section.reshape(local_a, 2, local_b, share_c, size_d))
+        current = jnp.concatenate(
+            [
+                held[chunk * SPLIT_B + part][0].reshape(2, local_a, share_b, share_c, size_d)
+                for part in range(SPLIT_B)
+            ],
+            axis=2,
+        )
+        section = jnp.einsum("aomib,iabcd->aomcd", table_b, current, precision=SPLIT)
+        sections.append(section)
     result = finish(sections, turn_p, turn_m, table_c, turn_c, table_d)
     return result.reshape(2, local_a, 1, local_b, size_c, size_d)
 

time: 2240 us -> 1760 us (0.79)
  waiting for transfers between devices: 1710 us -> 1280 us
  other arithmetic: 174 us -> 72.3 us
  starting transfers between devices: 55.1 us -> 99.2 us
  local copies, waits for them, and re-layouts: 156 us -> 194 us
  matrix products: 69.4 us -> 35.4 us
    ppermute x56 -> x112, waiting for transfers between devices: 1710 us -> 1280 us  [swap(): lax.ppermute(block, axis, [(at, at ^ 1 << place) for at in range(count)])]
    reshape x9 -> x16, local copies, waits for them, and re-layouts: 51.5 us -> 6.04 us  [shards(): held[chunk * SPLIT_B + part][0]]
    slice x8 -> x65, local copies, waits for them, and re-layouts: 18 us -> 62.3 us  [the longest x48 36.6 us: stage(): return (spread[:half], spread[half:], ('wide', levels - 1 - step))]
    ppermute x56 -> x112, starting transfers between devices: 55.1 us -> 99.2 us  [swap(): lax.ppermute(block, axis, [(at, at ^ 1 << place) for at in range(count)])]
    dot_general x0 -> x8, local copies, waits for them, and re-layouts: none -> 43 us  [shards(): jnp.einsum('aomib,iabcd->aomcd', table_b, current, precision=SPLIT)]
    dot_general x16 -> x24, matrix products: 69.4 us -> 35.4 us  [the longest x16 19.2 us: stage(): jnp.einsum('pa,ard->prd', table_a, values, precision=SPLIT)]
    concatenate x24 -> x5, other arithmetic: 34.8 us -> 4.75 us  [stage(): values = keep if step == 0 else jnp.concatenate([keep, other], axis=0)]
    add x20 -> x47, other arithmetic: 71.4 us -> 44.5 us  [the longest x31 38.9 us: stage(): current = other + (1 - 2 * upper).astype(jnp.float32) * keep]
  transfers between devices with their start and end apart: 56 -> 112, of which waited for: 38 -> 65; matrix products, arithmetic and copies ran while one was open for 16% -> 14% of each run, Pallas kernels for 0% -> 0%
where the time goes in v2:
time: 1760 us; the launch traced here: 1750 us
  waiting for transfers between devices  1280 us (73%)
  local copies, waits for them, and re-layouts  194 us (11%)
  starting transfers between devices  99.2 us (6%)
  other arithmetic  72.3 us (4%)
  Pallas kernels  69.3 us (4%)
  matrix products  35.4 us (2%)
    ppermute x112, waiting for transfers between devices, swap(): lax.ppermute(block, axis, [(at, at ^ 1 << place) for at in range(count)])  1280 us
    ppermute x112, starting transfers between devices, swap(): lax.ppermute(block, axis, [(at, at ^ 1 << place) for at in range(count)])  99.2 us
    pallas_call x1, Pallas kernels, finish(): pl.pallas_call(functools.partial(last_factors, pieces, group), grid=(coun...  69.3 us
    dot_general x8, local copies, waits for them, and re-layouts, shards(): jnp.einsum('aomib,iabcd->aomcd', table_b, current, precision=SPLIT)  43 us
    unnamed x109, local copies, waits for them, and re-layouts  40.5 us
    add x31, other arithmetic, stage(): current = other + (1 - 2 * upper).astype(jnp.float32) * keep  38.9 us
    slice x48, local copies, waits for them, and re-layouts, stage(): return (spread[:half], spread[half:], ('wide', levels - 1 - step))  36.6 us
  transfers between devices with their start and end apart: 112, of which 65 were waited for; matrix products, arithmetic and copies ran while one was open for 14% of the time, Pallas kernels for 0%

profile of v2, /device:TPU:0, one launch (start us, length us, event | category | flops | bytes accessed | tf_op | source)
XLA Modules:
  0.0 1752.7 jit_solution(10045232526425203620)
XLA Ops:
  0.0 11.0 fusion.176
  17.8 12.2 collective-permute-done
  33.8 10.7 collective-permute-done.1
  47.1 10.8 collective-permute-done.3
  65.0 14.7 collective-permute-done.4
  82.1 9.3 collective-permute-done.5
  91.5 16.2 collective-permute-done.2
  113.6 50.9 %collective-permute-done.6 = f32[32,32,128]{2,0,1:T(8,128)S(1)} collective-permute-done((f32[32,32,128]{2,0,1:T(8,128)S(1)}, f32[32,32,128]{2,0,1:T(8,128)S(1)}, u32[]{:S(2)}, u32[]{:S(2)}) %collective-permute-start.6) | collective-permute-done | bytes 524320 | tf_op jit(solution)/shard_map/ppermute | solution.py:19
  167.1 9.4 collective-permute-done.8
  184.0 30.1 %collective-permute-done.11 = f32[32,32,128]{2,0,1:T(8,128)S(1)} collective-permute-done((f32[32,32,128]{2,0,1:T(8,128)S(1)}, f32[32,32,128]{2,0,1:T(8,128)S(1)}, u32[]{:S(2)}, u32[]{:S(2)}) %collective-permute-start.11) | collective-permute-done | bytes 524320 | tf_op jit(solution)/shard_map/ppermute | solution.py:19
  216.2 14.4 collective-permute-done.14
  257.8 8.8 collective-permute-done.17
  271.2 12.1 collective-permute-done.12
  290.2 44.5 %collective-permute-done.21 = f32[64,32,128]{2,0,1:T(8,128)S(1)} collective-permute-done((f32[64,32,128]{2,0,1:T(8,128)S(1)}, f32[64,32,128]{2,0,1:T(8,128)S(1)}, u32[]{:S(2)}, u32[]{:S(2)}) %collective-permute-start.21) | collective-permute-done | bytes 1048608 | tf_op jit(solution)/shard_map/ppermute | solution.py:19
  348.2 15.9 collective-permute-done.24
  366.5 10.5 collective-permute-done.26
  377.3 9.2 collective-permute-done.23
  393.0 45.9 %collective-permute-done.28 = f32[64,32,128]{2,0,1:T(8,128)S(1)} collective-permute-done((f32[64,32,128]{2,0,1:T(8,128)}, f32[64,32,128]{2,0,1:T(8,128)S(1)}, u32[]{:S(2)}, u32[]{:S(2)}) %collective-permute-start.28) | collective-permute-done | bytes 1048608 | tf_op jit(solution)/shard_map/ppermute | solution.py:19
  446.6 20.5 %collective-permute-done.31 = f32[2,2,16,32,128]{4,3,2,1,0:T(8,128)S(1)} collective-permute-done((f32[2,2,16,32,128]{4,3,2,1,0:T(8,128)S(1)}, f32[2,2,16,32,128]{4,3,2,1,0:T(8,128)S(1)}, u32[]{:S(2)}, u32[]{:S(2)}) %collective-permute-start.31) | collective-permute-done | bytes 1048608 | tf_op jit(solution)/shard_map/ppermute | solution.py:19
  471.7 7.9 collective-permute-done.33
  482.6 7.0 collective-permute-done.30
  494.0 45.7 %collective-permute-done.35 = f32[64,32,128]{2,0,1:T(8,128)S(1)} collective-permute-done((f32[64,32,128]{2,0,1:T(8,128)S(1)}, f32[64,32,128]{2,0,1:T(8,128)S(1)}, u32[]{:S(2)}, u32[]{:S(2)}) %collective-permute-start.35) | collective-permute-done | bytes 1048608 | tf_op jit(solution)/shard_map/ppermute | solution.py:19
  545.9 20.5 %collective-permute-done.38 = f32[2,2,16,32,128]{4,3,2,1,0:T(8,128)S(1)} collective-permute-done((f32[2,2,16,32,128]{4,3,2,1,0:T(8,128)S(1)}, f32[2,2,16,32,128]{4,3,2,1,0:T(8,128)S(1)}, u32[]{:S(2)}, u32[]{:S(2)}) %collective-permute-start.38) | collective-permute-done | bytes 1048608 | tf_op jit(solution)/shard_map/ppermute | solution.py:19
  571.1 7.9 collective-permute-done.40
  582.1 6.9 collective-permute-done.37
  593.3 45.7 %collective-permute-done.42 = f32[64,32,128]{2,0,1:T(8,128)S(1)} collective-permute-done((f32[64,32,128]{2,0,1:T(8,128)S(1)}, f32[64,32,128]{2,0,1:T(8,128)S(1)}, u32[]{:S(2)}, u32[]{:S(2)}) %collective-permute-start.42) | collective-permute-done | bytes 1048608 | tf_op jit(solution)/shard_map/ppermute | solution.py:19
  645.6 20.2 %collective-permute-done.45 = f32[2,2,16,32,128]{4,3,2,1,0:T(8,128)S(1)} collective-permute-done((f32[2,2,16,32,128]{4,3,2,1,0:T(8,128)S(1)}, f32[2,2,16,32,128]{4,3,2,1,0:T(8,128)S(1)}, u32[]{:S(2)}, u32[]{:S(2)}) %collective-permute-start.45) | collective-permute-done | bytes 1048608 | tf_op jit(solution)/shard_map/ppermute | solution.py:19
  670.4 7.9 collective-permute-done.47
  681.4 7.0 collective-permute-done.44
  692.7 45.7 %collective-permute-done.49 = f32[64,32,128]{2,0,1:T(8,128)S(1)} collective-permute-done((f32[64,32,128]{2,0,1:T(8,128)S(1)}, f32[64,32,128]{2,0,1:T(8,128)S(1)}, u32[]{:S(2)}, u32[]{:S(2)}) %collective-permute-start.49) | collective-permute-done | bytes 1048608 | tf_op jit(solution)/shard_map/ppermute | solution.py:19
  744.7 20.5 %collective-permute-done.52 = f32[2,2,16,32,128]{4,3,2,1,0:T(8,128)S(1)} collective-permute-done((f32[2,2,16,32,128]{4,3,2,1,0:T(8,128)S(1)}, f32[2,2,16,32,128]{4,3,2,1,0:T(8,128)S(1)}, u32[]{:S(2)}, u32[]{:S(2)}) %collective-permute-start.52) | collective-permute-done | bytes 1048608 | tf_op jit(solution)/shard_map/ppermute | solution.py:19
  769.9 7.9 collective-permute-done.54
  780.8 6.9 collective-permute-done.51
  792.1 45.7 %collective-permute-done.56 = f32[64,32,128]{2,0,1:T(8,128)S(1)} collective-permute-done((f32[64,32,128]{2,0,1:T(8,128)S(1)}, f32[64,32,128]{2,0,1:T(8,128)S(1)}, u32[]{:S(2)}, u32[]{:S(2)}) %collective-permute-start.56) | collective-permute-done | bytes 1048608 | tf_op jit(solution)/shard_map/ppermute | solution.py:19
  844.1 20.4 %collective-permute-done.59 = f32[2,2,16,32,128]{4,3,2,1,0:T(8,128)S(1)} collective-permute-done((f32[2,2,16,32,128]{4,3,2,1,0:T(8,128)S(1)}, f32[2,2,16,32,128]{4,3,2,1,0:T(8,128)S(1)}, u32[]{:S(2)}, u32[]{:S(2)}) %collective-permute-start.59) | collective-permute-done | bytes 1048608 | tf_op jit(solution)/shard_map/ppermute | solution.py:19
  869.6 7.5 collective-permute-done.61
  880.1 6.9 collective-permute-done.58
  891.5 45.7 %collective-permute-done.63 = f32[64,32,128]{2,0,1:T(8,128)S(1)} collective-permute-done((f32[64,32,128]{2,0,1:T(8,128)S(1)}, f32[64,32,128]{2,0,1:T(8,128)S(1)}, u32[]{:S(2)}, u32[]{:S(2)}) %collective-permute-start.63) | collective-permute-done | bytes 1048608 | tf_op jit(solution)/shard_map/ppermute | solution.py:19
  943.5 20.5 %collective-permute-done.66 = f32[2,2,16,32,128]{4,3,2,1,0:T(8,128)S(1)} collective-permute-done((f32[2,2,16,32,128]{4,3,2,1,0:T(8,128)S(1)}, f32[2,2,16,32,128]{4,3,2,1,0:T(8,128)S(1)}, u32[]{:S(2)}, u32[]{:S(2)}) %collective-permute-start.66) | collective-permute-done | bytes 1048608 | tf_op jit(solution)/shard_map/ppermute | solution.py:19
  968.6 7.9 collective-permute-done.68
  979.6 6.9 collective-permute-done.65
  990.8 45.7 %collective-permute-done.70 = f32[64,32,128]{2,0,1:T(8,128)S(1)} collective-permute-done((f32[64,32,128]{2,0,1:T(8,128)S(1)}, f32[64,32,128]{2,0,1:T(8,128)S(1)}, u32[]{:S(2)}, u32[]{:S(2)}) %collective-permute-start.70) | collective-permute-done | bytes 1048608 | tf_op jit(solution)/shard_map/ppermute | solution.py:19
  1042.8 20.4 %collective-permute-done.73 = f32[2,2,16,32,128]{4,3,2,1,0:T(8,128)S(1)} collective-permute-done((f32[2,2,16,32,128]{4,3,2,1,0:T(8,128)S(1)}, f32[2,2,16,32,128]{4,3,2,1,0:T(8,128)S(1)}, u32[]{:S(2)}, u32[]{:S(2)}) %collective-permute-start.73) | collective-permute-done | bytes 1048608 | tf_op jit(solution)/shard_map/ppermute | solution.py:19
  1068.0 7.9 collective-permute-done.75
  1078.9 6.9 collective-permute-done.72
  1090.4 45.7 %collective-permute-done.77 = f32[64,32,128]{2,0,1:T(8,128)S(1)} collective-permute-done((f32[64,32,128]{2,0,1:T(8,128)S(1)}, f32[64,32,128]{2,0,1:T(8,128)S(1)}, u32[]{:S(2)}, u32[]{:S(2)}) %collective-permute-start.77) | collective-permute-done | bytes 1048608 | tf_op jit(solution)/shard_map/ppermute | solution.py:19
  1142.4 20.5 %collective-permute-done.80 = f32[2,2,16,32,128]{4,3,2,1,0:T(8,128)S(1)} collective-permute-done((f32[2,2,16,32,128]{4,3,2,1,0:T(8,128)S(1)}, f32[2,2,16,32,128]{4,3,2,1,0:T(8,128)S(1)}, u32[]{:S(2)}, u32[]{:S(2)}) %collective-permute-start.80) | collective-permute-done | bytes 1048608 | tf_op jit(solution)/shard_map/ppermute | solution.py:19
  1167.5 7.9 collective-permute-done.82
  1178.4 7.0 collective-permute-done.79
  1189.8 45.7 %collective-permute-done.84 = f32[64,32,128]{2,0,1:T(8,128)S(1)} collective-permute-done((f32[64,32,128]{2,0,1:T(8,128)S(1)}, f32[64,32,128]{2,0,1:T(8,128)S(1)}, u32[]{:S(2)}, u32[]{:S(2)}) %collective-permute-start.84) | collective-permute-done | bytes 1048608 | tf_op jit(solution)/shard_map/ppermute | solution.py:19
  1241.7 20.5 %collective-permute-done.87 = f32[2,2,16,32,128]{4,3,2,1,0:T(8,128)S(1)} collective-permute-done((f32[2,2,16,32,128]{4,3,2,1,0:T(8,128)S(1)}, f32[2,2,16,32,128]{4,3,2,1,0:T(8,128)S(1)}, u32[]{:S(2)}, u32[]{:S(2)}) %collective-permute-start.87) | collective-permute-done | bytes 1048608 | tf_op jit(solution)/shard_map/ppermute | solution.py:19
  1266.9 7.9 collective-permute-done.89
  1277.8 6.9 collective-permute-done.86
  1290.1 44.5 %collective-permute-done.91 = f32[64,32,128]{2,0,1:T(8,128)S(1)} collective-permute-done((f32[64,32,128]{2,0,1:T(8,128)S(1)}, f32[64,32,128]{2,0,1:T(8,128)S(1)}, u32[]{:S(2)}, u32[]{:S(2)}) %collective-permute-start.91) | collective-permute-done | bytes 1048608 | tf_op jit(solution)/shard_map/ppermute | solution.py:19
  1341.5 53.7 %collective-permute-done.90 = f32[32,32,128]{2,0,1:T(8,128)S(1)} collective-permute-done((f32[32,32,128]{2,0,1:T(8,128)S(1)}, f32[32,32,128]{2,0,1:T(8,128)S(1)}, u32[]{:S(2)}, u32[]{:S(2)}) %collective-permute-start.90) | collective-permute-done | bytes 524320 | tf_op jit(solution)/shard_map/ppermute | solution.py:19
  1405.9 18.4 %collective-permute-done.96 = f32[1,2,16,64,128]{4,3,2,1,0:T(8,128)S(1)} collective-permute-done((f32[1,2,16,64,128]{4,3,2,1,0:T(8,128)S(1)}, f32[1,2,16,64,128]{4,3,2,1,0:T(8,128)S(1)}, u32[]{:S(2)}, u32[]{:S(2)}) %collective-permute-start.96) | collective-permute-done | bytes 1048608 | tf_op jit(solution)/shard_map/ppermute | solution.py:19
  1424.6 23.9 %collective-permute-done.100 = f32[2,2,16,32,128]{4,3,2,1,0:T(8,128)S(1)} collective-permute-done((f32[2,2,16,32,128]{4,3,2,1,0:T(8,128)S(1)}, f32[2,2,16,32,128]{4,3,2,1,0:T(8,128)S(1)}, u32[]{:S(2)}, u32[]{:S(2)}) %collective-permute-start.100) | collective-permute-done | bytes 1048608 | tf_op jit(solution)/shard_map/ppermute | solution.py:19
  1456.4 19.8 %collective-permute-done.101 = f32[1,2,16,64,128]{4,3,2,1,0:T(8,128)S(1)} collective-permute-done((f32[1,2,16,64,128]{4,3,2,1,0:T(8,128)S(1)}, f32[1,2,16,64,128]{4,3,2,1,0:T(8,128)S(1)}, u32[]{:S(2)}, u32[]{:S(2)}) %collective-permute-start.101) | collective-permute-done | bytes 1048608 | tf_op jit(solution)/shard_map/ppermute | solution.py:19
  1480.6 17.8 %collective-permute-done.104 = f32[2,16,128,128]{3,2,1,0:T(8,128)S(1)} collective-permute-done((f32[2,16,128,128]{3,2,1,0:T(8,128)S(1)}, f32[2,16,128,128]{3,2,1,0:T(8,128)S(1)}, u32[]{:S(2)}, u32[]{:S(2)}) %collective-permute-start.104) | collective-permute-done | bytes 2097184 | tf_op jit(solution)/shard_map/ppermute | solution.py:19
  1505.2 20.4 %collective-permute-done.106 = f32[1,2,16,64,128]{4,3,2,1,0:T(8,128)S(1)} collective-permute-done((f32[1,2,16,64,128]{4,3,2,1,0:T(8,128)S(1)}, f32[1,2,16,64,128]{4,3,2,1,0:T(8,128)S(1)}, u32[]{:S(2)}, u32[]{:S(2)}) %collective-permute-start.106) | collective-permute-done | bytes 1048608 | tf_op jit(solution)/shard_map/ppermute | solution.py:19
  1527.1 20.8 %collective-permute-done.108 = f32[2,16,128,128]{3,2,1,0:T(8,128)S(1)} collective-permute-done((f32[2,16,128,128]{3,2,1,0:T(8,128)S(1)}, f32[2,16,128,128]{3,2,1,0:T(8,128)S(1)}, u32[]{:S(2)}, u32[]{:S(2)}) %collective-permute-start.108) | collective-permute-done | bytes 2097184 | tf_op jit(solution)/shard_map/ppermute | solution.py:19
  1556.4 42.0 %collective-permute-done.109 = f32[2,16,128,128]{3,2,1,0:T(8,128)} collective-permute-done((f32[2,16,128,128]{3,2,1,0:T(8,128)}, f32[2,16,128,128]{3,2,1,0:T(8,128)}, u32[]{:S(2)}, u32[]{:S(2)}) %collective-permute-start.109) | collective-permute-done | bytes 2097184 | tf_op jit(solution)/shard_map/ppermute | solution.py:19
  1638.3 6.2 copy.126.refs_3_
  1683.2 69.3 %last_factors.1 = f32[2,16,32,64,128]{4,3,2,1,0:T(8,128)} custom-call(f32[16,2,32,8,128]{4,3,2,1,0:T(8,128)S(1)} %copy.123.refs_0_, f32[16,2,32,8,128]{4,3,2,1,0:T(8,128)S(1)} %copy.124.refs_1_, f32[16,2,32,8,128]{4,3,2,1,0:T(8,128)} %copy.125.refs_2_, f32[16,2,32,8,128]{4,3,2,1,0:T(8,128)} %copy.126.refs_3_, f32[16,2,32,8,128]{4,3,2,1,0:T(8,128)} %copy.127.refs_4_, ...), custom_call_target="tpu_custom_call" | custom-call | flops 19327352832 | bytes 67108864 | tf_op jit(solution)/shard_map/last_factors/pallas_call | solution.py:116
  (568 shorter events, 394.0 us)
Async XLA Ops:
  109.7 56.5 %collective-permute-start.7 = (f32[2,2,16,32,128]{4,3,2,1,0:T(8,128)S(1)}, f32[2,2,16,32,128]{4,3,2,1,0:T(8,128)S(1)}, u32[]{:S(2)}, u32[]{:S(2)}) collective-permute-start(f32[2,2,16,32,128]{4,3,2,1,0:T(8,128)S(1)} %copy.63), channel_id=1, source_target_pairs={{0,8},{4,12},{8,0},{12,4},{16,24},{20,28},{24,16},{28,20},{1,9},{5... | collective-permute-start | bytes 3145736 | tf_op jit(solution)/shard_map/ppermute | solution.py:19
  109.8 54.7 %collective-permute-start.6 = (f32[32,32,128]{2,0,1:T(8,128)S(1)}, f32[32,32,128]{2,0,1:T(8,128)S(1)}, u32[]{:S(2)}, u32[]{:S(2)}) collective-permute-start(f32[32,32,128]{2,0,1:T(8,128)S(1)} %get-tuple-element.853), channel_id=1, source_target_pairs={{0,8},{4,12},{8,0},{12,4},{16,24},{20,28},{24,16},{28,20},{1,9},{5... | collective-permute-start | bytes 1572872 | tf_op jit(solution)/shard_map/ppermute | solution.py:19
  112.4 64.3 %collective-permute-start.10 = (f32[64,32,128]{2,0,1:T(8,128)S(1)}, f32[64,32,128]{2,0,1:T(8,128)S(1)}, u32[]{:S(2)}, u32[]{:S(2)}) collective-permute-start(f32[64,32,128]{2,0,1:T(8,128)S(1)} %pad_maximum_fusion.18), channel_id=1, source_target_pairs={{0,16},{4,20},{8,24},{12,28},{16,0},{20,4},{24,8},{28,12},{1,17},{... | collective-permute-start | bytes 3145736 | tf_op jit(solution)/shard_map/ppermute | solution.py:19
  180.2 50.4 %collective-permute-start.14 = (f32[2,2,16,32,128]{4,3,2,1,0:T(8,128)S(1)}, f32[2,2,16,32,128]{4,3,2,1,0:T(8,128)S(1)}, u32[]{:S(2)}, u32[]{:S(2)}) collective-permute-start(f32[2,2,16,32,128]{4,3,2,1,0:T(8,128)S(1)} %copy.66), channel_id=1, source_target_pairs={{0,8},{4,12},{8,0},{12,4},{16,24},{20,28},{24,16},{28,20},{1,9},{5... | collective-permute-start | bytes 3145736 | tf_op jit(solution)/shard_map/ppermute | solution.py:19
  182.8 52.7 %collective-permute-start.13 = (f32[64,32,128]{2,0,1:T(8,128)S(1)}, f32[64,32,128]{2,0,1:T(8,128)S(1)}, u32[]{:S(2)}, u32[]{:S(2)}) collective-permute-start(f32[64,32,128]{2,0,1:T(8,128)S(1)} %constant_dynamic-update-slice_fusion), channel_id=1, source_target_pairs={{0,16},{4,20},{8,24},{12,28},{16,0},{20,4},{24,8},{28,12},{1,17},{... | collective-permute-start | bytes 3145736 | tf_op jit(solution)/shard_map/ppermute | solution.py:19
  285.8 56.2 %collective-permute-start.22 = (f32[2,16,128,128]{3,2,1,0:T(8,128)S(1)}, f32[2,16,128,128]{3,2,1,0:T(8,128)}, u32[]{:S(2)}, u32[]{:S(2)}) collective-permute-start(f32[2,16,128,128]{3,2,1,0:T(8,128)S(1)} %pad_maximum_fusion), channel_id=1, source_target_pairs={{0,1},{1,0},{2,3},{3,2},{4,5},{5,4},{6,7},{7,6},{8,9},{9,8},{10,11... | collective-permute-start | bytes 6291464 | tf_op jit(solution)/shard_map/ppermute | solution.py:19
  286.8 47.9 %collective-permute-start.21 = (f32[64,32,128]{2,0,1:T(8,128)S(1)}, f32[64,32,128]{2,0,1:T(8,128)S(1)}, u32[]{:S(2)}, u32[]{:S(2)}) collective-permute-start(f32[64,32,128]{2,0,1:T(8,128)S(1)} %copy-done.29), channel_id=1, source_target_pairs={{0,16},{4,20},{8,24},{12,28},{16,0},{20,4},{24,8},{28,12},{1,17},{... | collective-permute-start | bytes 3145736 | tf_op jit(solution)/shard_map/ppermute | solution.py:19
  288.2 57.1 %collective-permute-start.20 = (f32[32,32,128]{2,0,1:T(8,128)}, f32[32,32,128]{2,0,1:T(8,128)}, u32[]{:S(2)}, u32[]{:S(2)}) collective-permute-start(f32[32,32,128]{2,0,1:T(8,128)} %get-tuple-element.841), channel_id=1, source_target_pairs={{0,8},{4,12},{8,0},{12,4},{16,24},{20,28},{24,16},{28,20},{1,9},{5... | collective-permute-start | bytes 1572872 | tf_op jit(solution)/shard_map/ppermute | solution.py:19
  289.9 56.6 %collective-permute-start.25 = (f32[1,2,16,64,128]{4,3,2,1,0:T(8,128)}, f32[1,2,16,64,128]{4,3,2,1,0:T(8,128)}, u32[]{:S(2)}, u32[]{:S(2)}) collective-permute-start(f32[1,2,16,64,128]{4,3,2,1,0:T(8,128)} %get-tuple-element.785), channel_id=1, source_target_pairs={{0,4},{4,0},{8,12},{12,8},{16,20},{20,16},{24,28},{28,24},{1,5},{5... | collective-permute-start | bytes 3145736 | tf_op jit(solution)/shard_map/ppermute | solution.py:19
  338.6 47.9 %collective-permute-start.23 = (f32[2,16,128,128]{3,2,1,0:T(8,128)}, f32[2,16,128,128]{3,2,1,0:T(8,128)}, u32[]{:S(2)}, u32[]{:S(2)}) collective-permute-start(f32[2,16,128,128]{3,2,1,0:T(8,128)} %maximum_bitcast_fusion.33), channel_id=1, source_target_pairs={{0,2},{1,3},{2,0},{3,1},{4,6},{5,7},{6,4},{7,5},{8,10},{9,11},{10,... | collective-permute-start | bytes 6291464 | tf_op jit(solution)/shard_map/ppermute | solution.py:19
  389.7 54.8 %collective-permute-start.29 = (f32[2,16,128,128]{3,2,1,0:T(8,128)S(1)}, f32[2,16,128,128]{3,2,1,0:T(8,128)S(1)}, u32[]{:S(2)}, u32[]{:S(2)}) collective-permute-start(f32[2,16,128,128]{3,2,1,0:T(8,128)S(1)} %pad_maximum_fusion.1), channel_id=1, source_target_pairs={{0,1},{1,0},{2,3},{3,2},{4,5},{5,4},{6,7},{7,6},{8,9},{9,8},{10,11... | collective-permute-start | bytes 6291464 | tf_op jit(solution)/shard_map/ppermute | solution.py:19
  389.8 49.2 %collective-permute-start.28 = (f32[64,32,128]{2,0,1:T(8,128)}, f32[64,32,128]{2,0,1:T(8,128)S(1)}, u32[]{:S(2)}, u32[]{:S(2)}) collective-permute-start(f32[64,32,128]{2,0,1:T(8,128)} %constant_dynamic-update-slice_fusion.10), channel_id=1, source_target_pairs={{0,16},{4,20},{8,24},{12,28},{16,0},{20,4},{24,8},{28,12},{1,17},{... | collective-permute-start | bytes 3145736 | tf_op jit(solution)/shard_map/ppermute | solution.py:19
  392.5 53.8 %collective-permute-start.32 = (f32[1,2,16,64,128]{4,3,2,1,0:T(8,128)S(1)}, f32[1,2,16,64,128]{4,3,2,1,0:T(8,128)S(1)}, u32[]{:S(2)}, u32[]{:S(2)}) collective-permute-start(f32[1,2,16,64,128]{4,3,2,1,0:T(8,128)S(1)} %get-tuple-element.781), channel_id=1, source_target_pairs={{0,4},{4,0},{8,12},{12,8},{16,20},{20,16},{24,28},{28,24},{1,5},{5... | collective-permute-start | bytes 3145736 | tf_op jit(solution)/shard_map/ppermute | solution.py:19
  392.8 53.4 %collective-permute-start.27 = (f32[32,32,128]{2,0,1:T(8,128)S(1)}, f32[32,32,128]{2,0,1:T(8,128)S(1)}, u32[]{:S(2)}, u32[]{:S(2)}) collective-permute-start(f32[32,32,128]{2,0,1:T(8,128)S(1)} %get-tuple-element.837), channel_id=1, source_target_pairs={{0,8},{4,12},{8,0},{12,4},{16,24},{20,28},{24,16},{28,20},{1,9},{5... | collective-permute-start | bytes 1572872 | tf_op jit(solution)/shard_map/ppermute | solution.py:19
  442.3 47.3 %collective-permute-start.30 = (f32[2,16,128,128]{3,2,1,0:T(8,128)S(1)}, f32[2,16,128,128]{3,2,1,0:T(8,128)S(1)}, u32[]{:S(2)}, u32[]{:S(2)}) collective-permute-start(f32[2,16,128,128]{3,2,1,0:T(8,128)S(1)} %maximum_bitcast_fusion.34), channel_id=1, source_target_pairs={{0,2},{1,3},{2,0},{3,1},{4,6},{5,7},{6,4},{7,5},{8,10},{9,11},{10,... | collective-permute-start | bytes 6291464 | tf_op jit(solution)/shard_map/ppermute | solution.py:19
  490.6 53.3 %collective-permute-start.36 = (f32[2,16,128,128]{3,2,1,0:T(8,128)S(1)}, f32[2,16,128,128]{3,2,1,0:T(8,128)S(1)}, u32[]{:S(2)}, u32[]{:S(2)}) collective-permute-start(f32[2,16,128,128]{3,2,1,0:T(8,128)S(1)} %pad_maximum_fusion.2), channel_id=1, source_target_pairs={{0,1},{1,0},{2,3},{3,2},{4,5},{5,4},{6,7},{7,6},{8,9},{9,8},{10,11... | collective-permute-start | bytes 6291464 | tf_op jit(solution)/shard_map/ppermute | solution.py:19
  490.7 48.9 %collective-permute-start.35 = (f32[64,32,128]{2,0,1:T(8,128)S(1)}, f32[64,32,128]{2,0,1:T(8,128)S(1)}, u32[]{:S(2)}, u32[]{:S(2)}) collective-permute-start(f32[64,32,128]{2,0,1:T(8,128)S(1)} %constant_dynamic-update-slice_fusion.15), channel_id=1, source_target_pairs={{0,16},{4,20},{8,24},{12,28},{16,0},{20,4},{24,8},{28,12},{1,17},{... | collective-permute-start | bytes 3145736 | tf_op jit(solution)/shard_map/ppermute | solution.py:19
  493.3 52.3 %collective-permute-start.39 = (f32[1,2,16,64,128]{4,3,2,1,0:T(8,128)S(1)}, f32[1,2,16,64,128]{4,3,2,1,0:T(8,128)S(1)}, u32[]{:S(2)}, u32[]{:S(2)}) collective-permute-start(f32[1,2,16,64,128]{4,3,2,1,0:T(8,128)S(1)} %get-tuple-element.773), channel_id=1, source_target_pairs={{0,4},{4,0},{8,12},{12,8},{16,20},{20,16},{24,28},{28,24},{1,5},{5... | collective-permute-start | bytes 3145736 | tf_op jit(solution)/shard_map/ppermute | solution.py:19
  493.6 51.9 %collective-permute-start.34 = (f32[32,32,128]{2,0,1:T(8,128)S(1)}, f32[32,32,128]{2,0,1:T(8,128)S(1)}, u32[]{:S(2)}, u32[]{:S(2)}) collective-permute-start(f32[32,32,128]{2,0,1:T(8,128)S(1)} %get-tuple-element.833), channel_id=1, source_target_pairs={{0,8},{4,12},{8,0},{12,4},{16,24},{20,28},{24,16},{28,20},{1,9},{5... | collective-permute-start | bytes 1572872 | tf_op jit(solution)/shard_map/ppermute | solution.py:19
  541.7 47.3 %collective-permute-start.37 = (f32[2,16,128,128]{3,2,1,0:T(8,128)S(1)}, f32[2,16,128,128]{3,2,1,0:T(8,128)S(1)}, u32[]{:S(2)}, u32[]{:S(2)}) collective-permute-start(f32[2,16,128,128]{3,2,1,0:T(8,128)S(1)} %maximum_bitcast_fusion.35), channel_id=1, source_target_pairs={{0,2},{1,3},{2,0},{3,1},{4,6},{5,7},{6,4},{7,5},{8,10},{9,11},{10,... | collective-permute-start | bytes 6291464 | tf_op jit(solution)/shard_map/ppermute | solution.py:19
  590.0 53.3 %collective-permute-start.43 = (f32[2,16,128,128]{3,2,1,0:T(8,128)S(1)}, f32[2,16,128,128]{3,2,1,0:T(8,128)S(1)}, u32[]{:S(2)}, u32[]{:S(2)}) collective-permute-start(f32[2,16,128,128]{3,2,1,0:T(8,128)S(1)} %pad_maximum_fusion.3), channel_id=1, source_target_pairs={{0,1},{1,0},{2,3},{3,2},{4,5},{5,4},{6,7},{7,6},{8,9},{9,8},{10,11... | collective-permute-start | bytes 6291464 | tf_op jit(solution)/shard_map/ppermute | solution.py:19
  590.1 48.9 %collective-permute-start.42 = (f32[64,32,128]{2,0,1:T(8,128)S(1)}, f32[64,32,128]{2,0,1:T(8,128)S(1)}, u32[]{:S(2)}, u32[]{:S(2)}) collective-permute-start(f32[64,32,128]{2,0,1:T(8,128)S(1)} %constant_dynamic-update-slice_fusion.20), channel_id=1, source_target_pairs={{0,16},{4,20},{8,24},{12,28},{16,0},{20,4},{24,8},{28,12},{1,17},{... | collective-permute-start | bytes 3145736 | tf_op jit(solution)/shard_map/ppermute | solution.py:19
  592.7 52.5 %collective-permute-start.46 = (f32[1,2,16,64,128]{4,3,2,1,0:T(8,128)S(1)}, f32[1,2,16,64,128]{4,3,2,1,0:T(8,128)S(1)}, u32[]{:S(2)}, u32[]{:S(2)}) collective-permute-start(f32[1,2,16,64,128]{4,3,2,1,0:T(8,128)S(1)} %get-tuple-element.769), channel_id=1, source_target_pairs={{0,4},{4,0},{8,12},{12,8},{16,20},{20,16},{24,28},{28,24},{1,5},{5... | collective-permute-start | bytes 3145736 | tf_op jit(solution)/shard_map/ppermute | solution.py:19
  593.0 52.2 %collective-permute-start.41 = (f32[32,32,128]{2,0,1:T(8,128)S(1)}, f32[32,32,128]{2,0,1:T(8,128)S(1)}, u32[]{:S(2)}, u32[]{:S(2)}) collective-permute-start(f32[32,32,128]{2,0,1:T(8,128)S(1)} %get-tuple-element.829), channel_id=1, source_target_pairs={{0,8},{4,12},{8,0},{12,4},{16,24},{20,28},{24,16},{28,20},{1,9},{5... | collective-permute-start | bytes 1572872 | tf_op jit(solution)/shard_map/ppermute | solution.py:19
  689.4 53.3 %collective-permute-start.50 = (f32[2,16,128,128]{3,2,1,0:T(8,128)S(1)}, f32[2,16,128,128]{3,2,1,0:T(8,128)S(1)}, u32[]{:S(2)}, u32[]{:S(2)}) collective-permute-start(f32[2,16,128,128]{3,2,1,0:T(8,128)S(1)} %pad_maximum_fusion.4), channel_id=1, source_target_pairs={{0,1},{1,0},{2,3},{3,2},{4,5},{5,4},{6,7},{7,6},{8,9},{9,8},{10,11... | collective-permute-start | bytes 6291464 | tf_op jit(solution)/shard_map/ppermute | solution.py:19
  689.5 48.9 %collective-permute-start.49 = (f32[64,32,128]{2,0,1:T(8,128)S(1)}, f32[64,32,128]{2,0,1:T(8,128)S(1)}, u32[]{:S(2)}, u32[]{:S(2)}) collective-permute-start(f32[64,32,128]{2,0,1:T(8,128)S(1)} %constant_dynamic-update-slice_fusion.25), channel_id=1, source_target_pairs={{0,16},{4,20},{8,24},{12,28},{16,0},{20,4},{24,8},{28,12},{1,17},{... | collective-permute-start | bytes 3145736 | tf_op jit(solution)/shard_map/ppermute | solution.py:19
  692.1 52.3 %collective-permute-start.53 = (f32[1,2,16,64,128]{4,3,2,1,0:T(8,128)S(1)}, f32[1,2,16,64,128]{4,3,2,1,0:T(8,128)S(1)}, u32[]{:S(2)}, u32[]{:S(2)}) collective-permute-start(f32[1,2,16,64,128]{4,3,2,1,0:T(8,128)S(1)} %get-tuple-element.761), channel_id=1, source_target_pairs={{0,4},{4,0},{8,12},{12,8},{16,20},{20,16},{24,28},{28,24},{1,5},{5... | collective-permute-start | bytes 3145736 | tf_op jit(solution)/shard_map/ppermute | solution.py:19
  692.4 51.9 %collective-permute-start.48 = (f32[32,32,128]{2,0,1:T(8,128)S(1)}, f32[32,32,128]{2,0,1:T(8,128)S(1)}, u32[]{:S(2)}, u32[]{:S(2)}) collective-permute-start(f32[32,32,128]{2,0,1:T(8,128)S(1)} %get-tuple-element.825), channel_id=1, source_target_pairs={{0,8},{4,12},{8,0},{12,4},{16,24},{20,28},{24,16},{28,20},{1,9},{5... | collective-permute-start | bytes 1572872 | tf_op jit(solution)/shard_map/ppermute | solution.py:19
  740.4 47.3 %collective-permute-start.51 = (f32[2,16,128,128]{3,2,1,0:T(8,128)S(1)}, f32[2,16,128,128]{3,2,1,0:T(8,128)S(1)}, u32[]{:S(2)}, u32[]{:S(2)}) collective-permute-start(f32[2,16,128,128]{3,2,1,0:T(8,128)S(1)} %maximum_bitcast_fusion.37), channel_id=1, source_target_pairs={{0,2},{1,3},{2,0},{3,1},{4,6},{5,7},{6,4},{7,5},{8,10},{9,11},{10,... | collective-permute-start | bytes 6291464 | tf_op jit(solution)/shard_map/ppermute | solution.py:19
  788.8 53.3 %collective-permute-start.57 = (f32[2,16,128,128]{3,2,1,0:T(8,128)S(1)}, f32[2,16,128,128]{3,2,1,0:T(8,128)S(1)}, u32[]{:S(2)}, u32[]{:S(2)}) collective-permute-start(f32[2,16,128,128]{3,2,1,0:T(8,128)S(1)} %pad_maximum_fusion.5), channel_id=1, source_target_pairs={{0,1},{1,0},{2,3},{3,2},{4,5},{5,4},{6,7},{7,6},{8,9},{9,8},{10,11... | collective-permute-start | bytes 6291464 | tf_op jit(solution)/shard_map/ppermute | solution.py:19
  788.8 48.9 %collective-permute-start.56 = (f32[64,32,128]{2,0,1:T(8,128)S(1)}, f32[64,32,128]{2,0,1:T(8,128)S(1)}, u32[]{:S(2)}, u32[]{:S(2)}) collective-permute-start(f32[64,32,128]{2,0,1:T(8,128)S(1)} %constant_dynamic-update-slice_fusion.30), channel_id=1, source_target_pairs={{0,16},{4,20},{8,24},{12,28},{16,0},{20,4},{24,8},{28,12},{1,17},{... | collective-permute-start | bytes 3145736 | tf_op jit(solution)/shard_map/ppermute | solution.py:19
  791.5 52.3 %collective-permute-start.60 = (f32[1,2,16,64,128]{4,3,2,1,0:T(8,128)S(1)}, f32[1,2,16,64,128]{4,3,2,1,0:T(8,128)S(1)}, u32[]{:S(2)}, u32[]{:S(2)}) collective-permute-start(f32[1,2,16,64,128]{4,3,2,1,0:T(8,128)S(1)} %get-tuple-element.757), channel_id=1, source_target_pairs={{0,4},{4,0},{8,12},{12,8},{16,20},{20,16},{24,28},{28,24},{1,5},{5... | collective-permute-start | bytes 3145736 | tf_op jit(solution)/shard_map/ppermute | solution.py:19
  791.7 51.9 %collective-permute-start.55 = (f32[32,32,128]{2,0,1:T(8,128)S(1)}, f32[32,32,128]{2,0,1:T(8,128)S(1)}, u32[]{:S(2)}, u32[]{:S(2)}) collective-permute-start(f32[32,32,128]{2,0,1:T(8,128)S(1)} %get-tuple-element.821), channel_id=1, source_target_pairs={{0,8},{4,12},{8,0},{12,4},{16,24},{20,28},{24,16},{28,20},{1,9},{5... | collective-permute-start | bytes 1572872 | tf_op jit(solution)/shard_map/ppermute | solution.py:19
  839.8 47.3 %collective-permute-start.58 = (f32[2,16,128,128]{3,2,1,0:T(8,128)S(1)}, f32[2,16,128,128]{3,2,1,0:T(8,128)S(1)}, u32[]{:S(2)}, u32[]{:S(2)}) collective-permute-start(f32[2,16,128,128]{3,2,1,0:T(8,128)S(1)} %maximum_bitcast_fusion.38), channel_id=1, source_target_pairs={{0,2},{1,3},{2,0},{3,1},{4,6},{5,7},{6,4},{7,5},{8,10},{9,11},{10,... | collective-permute-start | bytes 6291464 | tf_op jit(solution)/shard_map/ppermute | solution.py:19
  888.1 53.3 %collective-permute-start.64 = (f32[2,16,128,128]{3,2,1,0:T(8,128)S(1)}, f32[2,16,128,128]{3,2,1,0:T(8,128)S(1)}, u32[]{:S(2)}, u32[]{:S(2)}) collective-permute-start(f32[2,16,128,128]{3,2,1,0:T(8,128)S(1)} %pad_maximum_fusion.6), channel_id=1, source_target_pairs={{0,1},{1,0},{2,3},{3,2},{4,5},{5,4},{6,7},{7,6},{8,9},{9,8},{10,11... | collective-permute-start | bytes 6291464 | tf_op jit(solution)/shard_map/ppermute | solution.py:19
  888.2 48.9 %collective-permute-start.63 = (f32[64,32,128]{2,0,1:T(8,128)S(1)}, f32[64,32,128]{2,0,1:T(8,128)S(1)}, u32[]{:S(2)}, u32[]{:S(2)}) collective-permute-start(f32[64,32,128]{2,0,1:T(8,128)S(1)} %constant_dynamic-update-slice_fusion.35), channel_id=1, source_target_pairs={{0,16},{4,20},{8,24},{12,28},{16,0},{20,4},{24,8},{28,12},{1,17},{... | collective-permute-start | bytes 3145736 | tf_op jit(solution)/shard_map/ppermute | solution.py:19
  890.8 52.3 %collective-permute-start.67 = (f32[1,2,16,64,128]{4,3,2,1,0:T(8,128)S(1)}, f32[1,2,16,64,128]{4,3,2,1,0:T(8,128)S(1)}, u32[]{:S(2)}, u32[]{:S(2)}) collective-permute-start(f32[1,2,16,64,128]{4,3,2,1,0:T(8,128)S(1)} %get-tuple-element.749), channel_id=1, source_target_pairs={{0,4},{4,0},{8,12},{12,8},{16,20},{20,16},{24,28},{28,24},{1,5},{5... | collective-permute-start | bytes 3145736 | tf_op jit(solution)/shard_map/ppermute | solution.py:19
  891.1 51.9 %collective-permute-start.62 = (f32[32,32,128]{2,0,1:T(8,128)S(1)}, f32[32,32,128]{2,0,1:T(8,128)S(1)}, u32[]{:S(2)}, u32[]{:S(2)}) collective-permute-start(f32[32,32,128]{2,0,1:T(8,128)S(1)} %get-tuple-element.817), channel_id=1, source_target_pairs={{0,8},{4,12},{8,0},{12,4},{16,24},{20,28},{24,16},{28,20},{1,9},{5... | collective-permute-start | bytes 1572872 | tf_op jit(solution)/shard_map/ppermute | solution.py:19
  987.5 53.3 %collective-permute-start.71 = (f32[2,16,128,128]{3,2,1,0:T(8,128)S(1)}, f32[2,16,128,128]{3,2,1,0:T(8,128)S(1)}, u32[]{:S(2)}, u32[]{:S(2)}) collective-permute-start(f32[2,16,128,128]{3,2,1,0:T(8,128)S(1)} %pad_maximum_fusion.7), channel_id=1, source_target_pairs={{0,1},{1,0},{2,3},{3,2},{4,5},{5,4},{6,7},{7,6},{8,9},{9,8},{10,11... | collective-permute-start | bytes 6291464 | tf_op jit(solution)/shard_map/ppermute | solution.py:19
  987.6 48.9 %collective-permute-start.70 = (f32[64,32,128]{2,0,1:T(8,128)S(1)}, f32[64,32,128]{2,0,1:T(8,128)S(1)}, u32[]{:S(2)}, u32[]{:S(2)}) collective-permute-start(f32[64,32,128]{2,0,1:T(8,128)S(1)} %constant_dynamic-update-slice_fusion.40), channel_id=1, source_target_pairs={{0,16},{4,20},{8,24},{12,28},{16,0},{20,4},{24,8},{28,12},{1,17},{... | collective-permute-start | bytes 3145736 | tf_op jit(solution)/shard_map/ppermute | solution.py:19
  990.2 52.3 %collective-permute-start.74 = (f32[1,2,16,64,128]{4,3,2,1,0:T(8,128)S(1)}, f32[1,2,16,64,128]{4,3,2,1,0:T(8,128)S(1)}, u32[]{:S(2)}, u32[]{:S(2)}) collective-permute-start(f32[1,2,16,64,128]{4,3,2,1,0:T(8,128)S(1)} %get-tuple-element.745), channel_id=1, source_target_pairs={{0,4},{4,0},{8,12},{12,8},{16,20},{20,16},{24,28},{28,24},{1,5},{5... | collective-permute-start | bytes 3145736 | tf_op jit(solution)/shard_map/ppermute | solution.py:19
  990.5 51.9 %collective-permute-start.69 = (f32[32,32,128]{2,0,1:T(8,128)S(1)}, f32[32,32,128]{2,0,1:T(8,128)S(1)}, u32[]{:S(2)}, u32[]{:S(2)}) collective-permute-start(f32[32,32,128]{2,0,1:T(8,128)S(1)} %get-tuple-element.813), channel_id=1, source_target_pairs={{0,8},{4,12},{8,0},{12,4},{16,24},{20,28},{24,16},{28,20},{1,9},{5... | collective-permute-start | bytes 1572872 | tf_op jit(solution)/shard_map/ppermute | solution.py:19
  1038.6 47.3 %collective-permute-start.72 = (f32[2,16,128,128]{3,2,1,0:T(8,128)S(1)}, f32[2,16,128,128]{3,2,1,0:T(8,128)S(1)}, u32[]{:S(2)}, u32[]{:S(2)}) collective-permute-start(f32[2,16,128,128]{3,2,1,0:T(8,128)S(1)} %maximum_bitcast_fusion.40), channel_id=1, source_target_pairs={{0,2},{1,3},{2,0},{3,1},{4,6},{5,7},{6,4},{7,5},{8,10},{9,11},{10,... | collective-permute-start | bytes 6291464 | tf_op jit(solution)/shard_map/ppermute | solution.py:19
  1087.0 53.3 %collective-permute-start.78 = (f32[2,16,128,128]{3,2,1,0:T(8,128)S(1)}, f32[2,16,128,128]{3,2,1,0:T(8,128)S(1)}, u32[]{:S(2)}, u32[]{:S(2)}) collective-permute-start(f32[2,16,128,128]{3,2,1,0:T(8,128)S(1)} %pad_maximum_fusion.8), channel_id=1, source_target_pairs={{0,1},{1,0},{2,3},{3,2},{4,5},{5,4},{6,7},{7,6},{8,9},{9,8},{10,11... | collective-permute-start | bytes 6291464 | tf_op jit(solution)/shard_map/ppermute | solution.py:19
  1087.1 48.9 %collective-permute-start.77 = (f32[64,32,128]{2,0,1:T(8,128)S(1)}, f32[64,32,128]{2,0,1:T(8,128)S(1)}, u32[]{:S(2)}, u32[]{:S(2)}) collective-permute-start(f32[64,32,128]{2,0,1:T(8,128)S(1)} %constant_dynamic-update-slice_fusion.45), channel_id=1, source_target_pairs={{0,16},{4,20},{8,24},{12,28},{16,0},{20,4},{24,8},{28,12},{1,17},{... | collective-permute-start | bytes 3145736 | tf_op jit(solution)/shard_map/ppermute | solution.py:19
  1089.7 52.3 %collective-permute-start.81 = (f32[1,2,16,64,128]{4,3,2,1,0:T(8,128)S(1)}, f32[1,2,16,64,128]{4,3,2,1,0:T(8,128)S(1)}, u32[]{:S(2)}, u32[]{:S(2)}) collective-permute-start(f32[1,2,16,64,128]{4,3,2,1,0:T(8,128)S(1)} %get-tuple-element.737), channel_id=1, source_target_pairs={{0,4},{4,0},{8,12},{12,8},{16,20},{20,16},{24,28},{28,24},{1,5},{5... | collective-permute-start | bytes 3145736 | tf_op jit(solution)/shard_map/ppermute | solution.py:19
  1090.0 51.9 %collective-permute-start.76 = (f32[32,32,128]{2,0,1:T(8,128)S(1)}, f32[32,32,128]{2,0,1:T(8,128)S(1)}, u32[]{:S(2)}, u32[]{:S(2)}) collective-permute-start(f32[32,32,128]{2,0,1:T(8,128)S(1)} %get-tuple-element.809), channel_id=1, source_target_pairs={{0,8},{4,12},{8,0},{12,4},{16,24},{20,28},{24,16},{28,20},{1,9},{5... | collective-permute-start | bytes 1572872 | tf_op jit(solution)/shard_map/ppermute | solution.py:19
  1186.4 53.3 %collective-permute-start.85 = (f32[2,16,128,128]{3,2,1,0:T(8,128)S(1)}, f32[2,16,128,128]{3,2,1,0:T(8,128)S(1)}, u32[]{:S(2)}, u32[]{:S(2)}) collective-permute-start(f32[2,16,128,128]{3,2,1,0:T(8,128)S(1)} %pad_maximum_fusion.9), channel_id=1, source_target_pairs={{0,1},{1,0},{2,3},{3,2},{4,5},{5,4},{6,7},{7,6},{8,9},{9,8},{10,11... | collective-permute-start | bytes 6291464 | tf_op jit(solution)/shard_map/ppermute | solution.py:19
  1186.5 48.9 %collective-permute-start.84 = (f32[64,32,128]{2,0,1:T(8,128)S(1)}, f32[64,32,128]{2,0,1:T(8,128)S(1)}, u32[]{:S(2)}, u32[]{:S(2)}) collective-permute-start(f32[64,32,128]{2,0,1:T(8,128)S(1)} %constant_dynamic-update-slice_fusion.50), channel_id=1, source_target_pairs={{0,16},{4,20},{8,24},{12,28},{16,0},{20,4},{24,8},{28,12},{1,17},{... | collective-permute-start | bytes 3145736 | tf_op jit(solution)/shard_map/ppermute | solution.py:19
  1189.1 52.3 %collective-permute-start.88 = (f32[1,2,16,64,128]{4,3,2,1,0:T(8,128)S(1)}, f32[1,2,16,64,128]{4,3,2,1,0:T(8,128)S(1)}, u32[]{:S(2)}, u32[]{:S(2)}) collective-permute-start(f32[1,2,16,64,128]{4,3,2,1,0:T(8,128)S(1)} %get-tuple-element.733), channel_id=1, source_target_pairs={{0,4},{4,0},{8,12},{12,8},{16,20},{20,16},{24,28},{28,24},{1,5},{5... | collective-permute-start | bytes 3145736 | tf_op jit(solution)/shard_map/ppermute | solution.py:19
  1189.4 51.9 %collective-permute-start.83 = (f32[32,32,128]{2,0,1:T(8,128)S(1)}, f32[32,32,128]{2,0,1:T(8,128)S(1)}, u32[]{:S(2)}, u32[]{:S(2)}) collective-permute-start(f32[32,32,128]{2,0,1:T(8,128)S(1)} %get-tuple-element.805), channel_id=1, source_target_pairs={{0,8},{4,12},{8,0},{12,4},{16,24},{20,28},{24,16},{28,20},{1,9},{5... | collective-permute-start | bytes 1572872 | tf_op jit(solution)/shard_map/ppermute | solution.py:19
  1285.6 53.2 %collective-permute-start.92 = (f32[2,16,128,128]{3,2,1,0:T(8,128)S(1)}, f32[2,16,128,128]{3,2,1,0:T(8,128)S(1)}, u32[]{:S(2)}, u32[]{:S(2)}) collective-permute-start(f32[2,16,128,128]{3,2,1,0:T(8,128)S(1)} %pad_maximum_fusion.10), channel_id=1, source_target_pairs={{0,1},{1,0},{2,3},{3,2},{4,5},{5,4},{6,7},{7,6},{8,9},{9,8},{10,11... | collective-permute-start | bytes 6291464 | tf_op jit(solution)/shard_map/ppermute | solution.py:19
  1285.7 48.9 %collective-permute-start.91 = (f32[64,32,128]{2,0,1:T(8,128)S(1)}, f32[64,32,128]{2,0,1:T(8,128)S(1)}, u32[]{:S(2)}, u32[]{:S(2)}) collective-permute-start(f32[64,32,128]{2,0,1:T(8,128)S(1)} %constant_dynamic-update-slice_fusion.55), channel_id=1, source_target_pairs={{0,16},{4,20},{8,24},{12,28},{16,0},{20,4},{24,8},{28,12},{1,17},{... | collective-permute-start | bytes 3145736 | tf_op jit(solution)/shard_map/ppermute | solution.py:19
  1288.4 108.2 %collective-permute-start.93 = (f32[2,16,128,128]{3,2,1,0:T(8,128)S(1)}, f32[2,16,128,128]{3,2,1,0:T(8,128)S(1)}, u32[]{:S(2)}, u32[]{:S(2)}) collective-permute-start(f32[2,16,128,128]{3,2,1,0:T(8,128)S(1)} %maximum_bitcast_fusion.43), channel_id=1, source_target_pairs={{0,2},{1,3},{2,0},{3,1},{4,6},{5,7},{6,4},{7,5},{8,10},{9,11},{10,... | collective-permute-start | bytes 6291464 | tf_op jit(solution)/shard_map/ppermute | solution.py:19
  1289.9 105.5 %collective-permute-start.95 = (f32[1,2,16,64,128]{4,3,2,1,0:T(8,128)S(1)}, f32[1,2,16,64,128]{4,3,2,1,0:T(8,128)S(1)}, u32[]{:S(2)}, u32[]{:S(2)}) collective-permute-start(f32[1,2,16,64,128]{4,3,2,1,0:T(8,128)S(1)} %get-tuple-element.725), channel_id=1, source_target_pairs={{0,4},{4,0},{8,12},{12,8},{16,20},{20,16},{24,28},{28,24},{1,5},{5... | collective-permute-start | bytes 3145736 | tf_op jit(solution)/shard_map/ppermute | solution.py:19
  1336.8 58.8 %collective-permute-start.94 = (f32[2,2,16,32,128]{4,3,2,1,0:T(8,128)S(1)}, f32[2,2,16,32,128]{4,3,2,1,0:T(8,128)S(1)}, u32[]{:S(2)}, u32[]{:S(2)}) collective-permute-start(f32[2,2,16,32,128]{4,3,2,1,0:T(8,128)S(1)} %copy.111), channel_id=1, source_target_pairs={{0,8},{4,12},{8,0},{12,4},{16,24},{20,28},{24,16},{28,20},{1,9},{5... | collective-permute-start | bytes 3145736 | tf_op jit(solution)/shard_map/ppermute | solution.py:19
  1336.8 58.4 %collective-permute-start.90 = (f32[32,32,128]{2,0,1:T(8,128)S(1)}, f32[32,32,128]{2,0,1:T(8,128)S(1)}, u32[]{:S(2)}, u32[]{:S(2)}) collective-permute-start(f32[32,32,128]{2,0,1:T(8,128)S(1)} %get-tuple-element.801), channel_id=1, source_target_pairs={{0,8},{4,12},{8,0},{12,4},{16,24},{20,28},{24,16},{28,20},{1,9},{5... | collective-permute-start | bytes 1572872 | tf_op jit(solution)/shard_map/ppermute | solution.py:19
  1338.9 60.5 %collective-permute-start.97 = (f32[64,32,128]{2,0,1:T(8,128)S(1)}, f32[64,32,128]{2,0,1:T(8,128)S(1)}, u32[]{:S(2)}, u32[]{:S(2)}) collective-permute-start(f32[64,32,128]{2,0,1:T(8,128)S(1)} %constant_dynamic-update-slice_fusion.60), channel_id=1, source_target_pairs={{0,16},{4,20},{8,24},{12,28},{16,0},{20,4},{24,8},{28,12},{1,17},{... | collective-permute-start | bytes 3145736 | tf_op jit(solution)/shard_map/ppermute | solution.py:19
  1397.5 51.9 %collective-permute-start.99 = (f32[2,16,128,128]{3,2,1,0:T(8,128)S(1)}, f32[2,16,128,128]{3,2,1,0:T(8,128)S(1)}, u32[]{:S(2)}, u32[]{:S(2)}) collective-permute-start(f32[2,16,128,128]{3,2,1,0:T(8,128)S(1)} %maximum_bitcast_fusion.44), channel_id=1, source_target_pairs={{0,2},{1,3},{2,0},{3,1},{4,6},{5,7},{6,4},{7,5},{8,10},{9,11},{10,... | collective-permute-start | bytes 6291464 | tf_op jit(solution)/shard_map/ppermute | solution.py:19
  1401.4 51.4 %collective-permute-start.102 = (f32[64,32,128]{2,0,1:T(8,128)S(1)}, f32[64,32,128]{2,0,1:T(8,128)S(1)}, u32[]{:S(2)}, u32[]{:S(2)}) collective-permute-start(f32[64,32,128]{2,0,1:T(8,128)S(1)} %constant_dynamic-update-slice_fusion.65), channel_id=1, source_target_pairs={{0,16},{4,20},{8,24},{12,28},{16,0},{20,4},{24,8},{28,12},{1,17},{... | collective-permute-start | bytes 3145736 | tf_op jit(solution)/shard_map/ppermute | solution.py:19
  1450.4 48.0 %collective-permute-start.104 = (f32[2,16,128,128]{3,2,1,0:T(8,128)S(1)}, f32[2,16,128,128]{3,2,1,0:T(8,128)S(1)}, u32[]{:S(2)}, u32[]{:S(2)}) collective-permute-start(f32[2,16,128,128]{3,2,1,0:T(8,128)S(1)} %maximum_bitcast_fusion.45), channel_id=1, source_target_pairs={{0,2},{1,3},{2,0},{3,1},{4,6},{5,7},{6,4},{7,5},{8,10},{9,11},{10,... | collective-permute-start | bytes 6291464 | tf_op jit(solution)/shard_map/ppermute | solution.py:19
  1499.4 48.4 %collective-permute-start.108 = (f32[2,16,128,128]{3,2,1,0:T(8,128)S(1)}, f32[2,16,128,128]{3,2,1,0:T(8,128)S(1)}, u32[]{:S(2)}, u32[]{:S(2)}) collective-permute-start(f32[2,16,128,128]{3,2,1,0:T(8,128)S(1)} %maximum_bitcast_fusion.46), channel_id=1, source_target_pairs={{0,2},{1,3},{2,0},{3,1},{4,6},{5,7},{6,4},{7,5},{8,10},{9,11},{10,... | collective-permute-start | bytes 6291464 | tf_op jit(solution)/shard_map/ppermute | solution.py:19
  1550.0 48.4 %collective-permute-start.109 = (f32[2,16,128,128]{3,2,1,0:T(8,128)}, f32[2,16,128,128]{3,2,1,0:T(8,128)}, u32[]{:S(2)}, u32[]{:S(2)}) collective-permute-start(f32[2,16,128,128]{3,2,1,0:T(8,128)} %maximum_bitcast_fusion.47), channel_id=1, source_target_pairs={{0,2},{1,3},{2,0},{3,1},{4,6},{5,7},{6,4},{7,5},{8,10},{9,11},{10,... | collective-permute-start | bytes 6291464 | tf_op jit(solution)/shard_map/ppermute | solution.py:19
  1601.4 72.9 %collective-permute-start.111 = (f32[2,16,128,128]{3,2,1,0:T(8,128)S(1)}, f32[2,16,128,128]{3,2,1,0:T(8,128)S(1)}, u32[]{:S(2)}, u32[]{:S(2)}) collective-permute-start(f32[2,16,128,128]{3,2,1,0:T(8,128)S(1)} %pad_maximum_fusion.15), channel_id=1, source_target_pairs={{0,1},{1,0},{2,3},{3,2},{4,5},{5,4},{6,7},{7,6},{8,9},{9,8},{10,11... | collective-permute-start | bytes 6291464 | tf_op jit(solution)/shard_map/ppermute | solution.py:19
  (81 other events, 1628.9 us)

commit v3 on v2

--- a/solution.py
+++ b/solution.py
@@ -240,12 +240,10 @@
 
     count = CHUNKS * SPLIT_B
     steps = 2 * levels + 2 + narrow_levels
-    starts = [0.35 * step - 0.5 for step in range(levels + 1)]
-    starts += [1.4 + 0.35 * levels + 0.7 * step for step in range(levels + 1)]
-    starts += [starts[-1] + 0.14 + 1.4 * step for step in range(1, narrow_levels)]
-    starts += [starts[-1] + 0.14]
-    if narrow_levels > 1:
-        starts[-1] = starts[-2] + 0.14
+    starts = [-1.3 - 0.96 * (levels - step) for step in range(levels + 1)]
+    starts += [0.3 + 0.92 * step for step in range(levels + 1)]
+    starts += [starts[-1] + 1.32 + 1.23 * step for step in range(narrow_levels)]
+    starts = [round(start, 2) for start in starts]
     plan = sorted(
         ((chunk + starts[step], chunk, step) for chunk in range(count) for step in range(steps))
     )
@@ -263,18 +261,18 @@
         keep, send, way = stage(step, keep, other)
         held[chunk] = (keep, None if send is None else swap(send, *way))
         before = chunk
-
-    sections = []
-    for chunk in range(CHUNKS):
-        current = jnp.concatenate(
-            [
-                held[chunk * SPLIT_B + part][0].reshape(2, local_a, share_b, share_c, size_d)
-                for part in range(SPLIT_B)
-            ],
-            axis=2,
-        )
-        section = jnp.einsum("aomib,iabcd->aomcd", table_b, current, precision=SPLIT)
-        sections.append(section)
+        if step == steps - 1 and chunk % SPLIT_B == SPLIT_B - 1:
+            first = chunk - SPLIT_B + 1
+            current = jnp.concatenate(
+                [
+                    held[part][0].reshape(2, local_a, share_b, share_c, size_d)
+                    for part in range(first, chunk + 1)
+                ],
+                axis=2,
+            )
+            section = jnp.einsum("aomib,iabcd->aomcd", table_b, current, precision=SPLIT)
+            held[chunk] = (section, None)
+    sections = [held[chunk * SPLIT_B + SPLIT_B - 1][0] for chunk in range(CHUNKS)]
     result = finish(sections, turn_p, turn_m, table_c, turn_c, table_d)
     return result.reshape(2, local_a, 1, local_b, size_c, size_d)
 

time: 1760 us -> 1230 us (0.70)
  waiting for transfers between devices: 1280 us -> 843 us
  local copies, waits for them, and re-layouts: 194 us -> 139 us
  other arithmetic: 72.3 us -> 40 us
    ppermute x112, waiting for transfers between devices: 1280 us -> 843 us  [swap(): lax.ppermute(block, axis, [(at, at ^ 1 << place) for at in range(count)])]
    dot_general x8 -> x1, local copies, waits for them, and re-layouts: 43 us -> 5.81 us  [shards(): jnp.einsum('aomib,iabcd->aomcd', table_b, current, precision=SPLIT)]
    optimization_barrier x0 -> x7, local copies, waits for them, and re-layouts: none -> 37 us  [shards(): keep, other, rest = lax.optimization_barrier((keep, other, rest))]
    add x31 -> x24, other arithmetic: 38.9 us -> 9.04 us  [stage(): current = other + (1 - 2 * upper).astype(jnp.float32) * keep]
    unnamed x109 -> x103, local copies, waits for them, and re-layouts: 40.5 us -> 18.7 us
  transfers between devices with their start and end apart: 112 -> 112, of which waited for: 65 -> 54; matrix products, arithmetic and copies ran while one was open for 14% -> 15% of each run, Pallas kernels for 0% -> 0%
where the time goes in v3:
time: 1230 us; the launch traced here: 1220 us
  waiting for transfers between devices  843 us (69%)
  local copies, waits for them, and re-layouts  139 us (11%)
  starting transfers between devices  83.1 us (7%)
  Pallas kernels  69.3 us (6%)
  matrix products  42.2 us (3%)
  other arithmetic  40 us (3%)
    ppermute x112, waiting for transfers between devices, swap(): lax.ppermute(block, axis, [(at, at ^ 1 << place) for at in range(count)])  843 us
    ppermute x112, starting transfers between devices, swap(): lax.ppermute(block, axis, [(at, at ^ 1 << place) for at in range(count)])  83.1 us
    pallas_call x1, Pallas kernels, finish(): pl.pallas_call(functools.partial(last_factors, pieces, group), grid=(coun...  69.3 us
    optimization_barrier x7, local copies, waits for them, and re-layouts, shards(): keep, other, rest = lax.optimization_barrier((keep, other, rest))  37 us
    slice x17, local copies, waits for them, and re-layouts, slab(): values = record[:, low_b:low_b + share_b, low_c:low_c + share_c, :]  27.6 us
  transfers between devices with their start and end apart: 112, of which 54 were waited for; matrix products, arithmetic and copies ran while one was open for 15% of the time, Pallas kernels for 0%

profile of v3, /device:TPU:0, one launch (start us, length us, event | category | flops | bytes accessed | tf_op | source)
XLA Modules:
  0.0 1219.8 jit_solution(10811250770311935247)
XLA Ops:
  0.0 11.0 fusion.172
  17.8 12.2 %collective-permute-done = f32[16,64,128]{2,0,1:T(8,128)} collective-permute-done((f32[16,64,128]{2,0,1:T(8,128)}, f32[16,64,128]{2,0,1:T(8,128)}, u32[]{:S(2)}, u32[]{:S(2)}) %collective-permute-start) | collective-permute-done | bytes 524320 | tf_op jit(solution)/shard_map/ppermute | solution.py:19
  37.5 8.2 collective-permute-done.1
  64.0 9.3 collective-permute-done.3
  78.2 23.8 %collective-permute-done.6 = f32[64,32,128]{2,0,1:T(8,128)} collective-permute-done((f32[64,32,128]{2,0,1:T(8,128)}, f32[64,32,128]{2,0,1:T(8,128)}, u32[]{:S(2)}, u32[]{:S(2)}) %collective-permute-start.6) | collective-permute-done | bytes 1048608 | tf_op jit(solution)/shard_map/ppermute | solution.py:19
  113.9 38.3 %collective-permute-done.7 = f32[2,2,16,32,128]{4,3,2,1,0:T(8,128)S(1)} collective-permute-done((f32[2,2,16,32,128]{4,3,2,1,0:T(8,128)S(1)}, f32[2,2,16,32,128]{4,3,2,1,0:T(8,128)S(1)}, u32[]{:S(2)}, u32[]{:S(2)}) %collective-permute-start.7) | collective-permute-done | bytes 1048608 | tf_op jit(solution)/shard_map/ppermute | solution.py:19
  179.7 21.9 %collective-permute-done.15 = f32[2,2,16,32,128]{4,3,2,1,0:T(8,128)} collective-permute-done((f32[2,2,16,32,128]{4,3,2,1,0:T(8,128)}, f32[2,2,16,32,128]{4,3,2,1,0:T(8,128)}, u32[]{:S(2)}, u32[]{:S(2)}) %collective-permute-start.15) | collective-permute-done | bytes 1048608 | tf_op jit(solution)/shard_map/ppermute | solution.py:19
  203.8 13.6 %collective-permute-done.14 = f32[64,32,128]{2,0,1:T(8,128)S(1)} collective-permute-done((f32[64,32,128]{2,0,1:T(8,128)S(1)}, f32[64,32,128]{2,0,1:T(8,128)S(1)}, u32[]{:S(2)}, u32[]{:S(2)}) %collective-permute-start.14) | collective-permute-done | bytes 1048608 | tf_op jit(solution)/shard_map/ppermute | solution.py:19
  221.8 20.3 %collective-permute-done.13 = f32[32,32,128]{2,0,1:T(8,128)S(1)} collective-permute-done((f32[32,32,128]{2,0,1:T(8,128)S(1)}, f32[32,32,128]{2,0,1:T(8,128)S(1)}, u32[]{:S(2)}, u32[]{:S(2)}) %collective-permute-start.13) | collective-permute-done | bytes 524320 | tf_op jit(solution)/shard_map/ppermute | solution.py:19
  246.6 17.1 %collective-permute-done.17 = f32[2,2,16,32,128]{4,3,2,1,0:T(8,128)S(1)} collective-permute-done((f32[2,2,16,32,128]{4,3,2,1,0:T(8,128)S(1)}, f32[2,2,16,32,128]{4,3,2,1,0:T(8,128)S(1)}, u32[]{:S(2)}, u32[]{:S(2)}) %collective-permute-start.17) | collective-permute-done | bytes 1048608 | tf_op jit(solution)/shard_map/ppermute | solution.py:19
  269.5 15.5 %collective-permute-done.23 = f32[2,16,128,128]{3,2,1,0:T(8,128)S(1)} collective-permute-done((f32[2,16,128,128]{3,2,1,0:T(8,128)S(1)}, f32[2,16,128,128]{3,2,1,0:T(8,128)S(1)}, u32[]{:S(2)}, u32[]{:S(2)}) %collective-permute-start.23) | collective-permute-done | bytes 2097184 | tf_op jit(solution)/shard_map/ppermute | solution.py:19
  285.9 13.3 %collective-permute-done.22 = f32[32,32,128]{2,0,1:T(8,128)S(1)} collective-permute-done((f32[32,32,128]{2,0,1:T(8,128)S(1)}, f32[32,32,128]{2,0,1:T(8,128)S(1)}, u32[]{:S(2)}, u32[]{:S(2)}) %collective-permute-start.22) | collective-permute-done | bytes 524320 | tf_op jit(solution)/shard_map/ppermute | solution.py:19
  304.2 33.5 %collective-permute-done.29 = f32[2,2,16,32,128]{4,3,2,1,0:T(8,128)S(1)} collective-permute-done((f32[2,2,16,32,128]{4,3,2,1,0:T(8,128)S(1)}, f32[2,2,16,32,128]{4,3,2,1,0:T(8,128)S(1)}, u32[]{:S(2)}, u32[]{:S(2)}) %collective-permute-start.29) | collective-permute-done | bytes 1048608 | tf_op jit(solution)/shard_map/ppermute | solution.py:19
  346.0 16.5 %collective-permute-done.25 = f32[32,32,128]{2,0,1:T(8,128)S(1)} collective-permute-done((f32[32,32,128]{2,0,1:T(8,128)S(1)}, f32[32,32,128]{2,0,1:T(8,128)S(1)}, u32[]{:S(2)}, u32[]{:S(2)}) %collective-permute-start.25) | collective-permute-done | bytes 524320 | tf_op jit(solution)/shard_map/ppermute | solution.py:19
  363.6 7.0 collective-permute-done.35
  370.8 17.6 %collective-permute-done.34 = f32[2,2,16,32,128]{4,3,2,1,0:T(8,128)S(1)} collective-permute-done((f32[2,2,16,32,128]{4,3,2,1,0:T(8,128)S(1)}, f32[2,2,16,32,128]{4,3,2,1,0:T(8,128)S(1)}, u32[]{:S(2)}, u32[]{:S(2)}) %collective-permute-start.34) | collective-permute-done | bytes 1048608 | tf_op jit(solution)/shard_map/ppermute | solution.py:19
  391.2 14.4 %collective-permute-done.32 = f32[2,16,128,128]{3,2,1,0:T(8,128)S(1)} collective-permute-done((f32[2,16,128,128]{3,2,1,0:T(8,128)S(1)}, f32[2,16,128,128]{3,2,1,0:T(8,128)S(1)}, u32[]{:S(2)}, u32[]{:S(2)}) %collective-permute-start.32) | collective-permute-done | bytes 2097184 | tf_op jit(solution)/shard_map/ppermute | solution.py:19
  407.8 4.0 fusion.31
  411.9 6.8 collective-permute-done.30
  419.1 7.6 collective-permute-done.36
  427.7 19.4 %collective-permute-done.43 = f32[2,2,16,32,128]{4,3,2,1,0:T(8,128)S(1)} collective-permute-done((f32[2,2,16,32,128]{4,3,2,1,0:T(8,128)S(1)}, f32[2,2,16,32,128]{4,3,2,1,0:T(8,128)S(1)}, u32[]{:S(2)}, u32[]{:S(2)}) %collective-permute-start.43) | collective-permute-done | bytes 1048608 | tf_op jit(solution)/shard_map/ppermute | solution.py:19
  458.6 19.5 %collective-permute-done.39 = f32[32,32,128]{2,0,1:T(8,128)S(1)} collective-permute-done((f32[32,32,128]{2,0,1:T(8,128)S(1)}, f32[32,32,128]{2,0,1:T(8,128)S(1)}, u32[]{:S(2)}, u32[]{:S(2)}) %collective-permute-start.39) | collective-permute-done | bytes 524320 | tf_op jit(solution)/shard_map/ppermute | solution.py:19
  482.6 24.4 %collective-permute-done.48 = f32[2,2,16,32,128]{4,3,2,1,0:T(8,128)S(1)} collective-permute-done((f32[2,2,16,32,128]{4,3,2,1,0:T(8,128)S(1)}, f32[2,2,16,32,128]{4,3,2,1,0:T(8,128)S(1)}, u32[]{:S(2)}, u32[]{:S(2)}) %collective-permute-start.48) | collective-permute-done | bytes 1048608 | tf_op jit(solution)/shard_map/ppermute | solution.py:19
  513.4 10.0 collective-permute-done.46
  525.0 4.0 fusion.30
  528.9 6.8 collective-permute-done.44
  537.1 9.1 collective-permute-done.50
  548.6 9.5 collective-permute-done.57
  560.8 20.3 %collective-permute-done.55 = f32[2,16,128,128]{3,2,1,0:T(8,128)S(1)} collective-permute-done((f32[2,16,128,128]{3,2,1,0:T(8,128)S(1)}, f32[2,16,128,128]{3,2,1,0:T(8,128)S(1)}, u32[]{:S(2)}, u32[]{:S(2)}) %collective-permute-start.55) | collective-permute-done | bytes 2097184 | tf_op jit(solution)/shard_map/ppermute | solution.py:19
  582.4 12.9 %collective-permute-done.53 = f32[32,32,128]{2,0,1:T(8,128)S(1)} collective-permute-done((f32[32,32,128]{2,0,1:T(8,128)S(1)}, f32[32,32,128]{2,0,1:T(8,128)S(1)}, u32[]{:S(2)}, u32[]{:S(2)}) %collective-permute-start.53) | collective-permute-done | bytes 524320 | tf_op jit(solution)/shard_map/ppermute | solution.py:19
  596.7 7.4 collective-permute-done.63
  605.7 11.0 collective-permute-done.62
  621.9 16.9 %collective-permute-done.60 = f32[2,16,128,128]{3,2,1,0:T(8,128)S(1)} collective-permute-done((f32[2,16,128,128]{3,2,1,0:T(8,128)S(1)}, f32[2,16,128,128]{3,2,1,0:T(8,128)S(1)}, u32[]{:S(2)}, u32[]{:S(2)}) %collective-permute-start.60) | collective-permute-done | bytes 2097184 | tf_op jit(solution)/shard_map/ppermute | solution.py:19
  643.9 17.6 %collective-permute-done.58 = f32[32,32,128]{2,0,1:T(8,128)S(1)} collective-permute-done((f32[32,32,128]{2,0,1:T(8,128)S(1)}, f32[32,32,128]{2,0,1:T(8,128)S(1)}, u32[]{:S(2)}, u32[]{:S(2)}) %collective-permute-start.58) | collective-permute-done | bytes 524320 | tf_op jit(solution)/shard_map/ppermute | solution.py:19
  664.5 31.0 %collective-permute-done.71 = f32[2,2,16,32,128]{4,3,2,1,0:T(8,128)S(1)} collective-permute-done((f32[2,2,16,32,128]{4,3,2,1,0:T(8,128)S(1)}, f32[2,2,16,32,128]{4,3,2,1,0:T(8,128)S(1)}, u32[]{:S(2)}, u32[]{:S(2)}) %collective-permute-start.71) | collective-permute-done | bytes 1048608 | tf_op jit(solution)/shard_map/ppermute | solution.py:19
  704.0 9.7 collective-permute-done.67
  719.0 15.1 %collective-permute-done.76 = f32[2,2,16,32,128]{4,3,2,1,0:T(8,128)S(1)} collective-permute-done((f32[2,2,16,32,128]{4,3,2,1,0:T(8,128)S(1)}, f32[2,2,16,32,128]{4,3,2,1,0:T(8,128)S(1)}, u32[]{:S(2)}, u32[]{:S(2)}) %collective-permute-start.76) | collective-permute-done | bytes 1048608 | tf_op jit(solution)/shard_map/ppermute | solution.py:19
  737.7 10.6 collective-permute-done.74
  753.7 16.9 %collective-permute-done.72 = f32[32,32,128]{2,0,1:T(8,128)S(1)} collective-permute-done((f32[32,32,128]{2,0,1:T(8,128)S(1)}, f32[32,32,128]{2,0,1:T(8,128)S(1)}, u32[]{:S(2)}, u32[]{:S(2)}) %collective-permute-start.72) | collective-permute-done | bytes 524320 | tf_op jit(solution)/shard_map/ppermute | solution.py:19
  773.4 13.6 %collective-permute-done.79 = f32[2,2,16,32,128]{4,3,2,1,0:T(8,128)S(1)} collective-permute-done((f32[2,2,16,32,128]{4,3,2,1,0:T(8,128)S(1)}, f32[2,2,16,32,128]{4,3,2,1,0:T(8,128)S(1)}, u32[]{:S(2)}, u32[]{:S(2)}) %collective-permute-start.79) | collective-permute-done | bytes 1048608 | tf_op jit(solution)/shard_map/ppermute | solution.py:19
  792.5 4.6 collective-permute-done.86
  801.5 37.7 %collective-permute-done.84 = f32[32,32,128]{2,0,1:T(8,128)S(1)} collective-permute-done((f32[32,32,128]{2,0,1:T(8,128)S(1)}, f32[32,32,128]{2,0,1:T(8,128)S(1)}, u32[]{:S(2)}, u32[]{:S(2)}) %collective-permute-start.84) | collective-permute-done | bytes 524320 | tf_op jit(solution)/shard_map/ppermute | solution.py:19
  842.9 28.4 %collective-permute-done.91 = f32[2,2,16,32,128]{4,3,2,1,0:T(8,128)S(1)} collective-permute-done((f32[2,2,16,32,128]{4,3,2,1,0:T(8,128)S(1)}, f32[2,2,16,32,128]{4,3,2,1,0:T(8,128)S(1)}, u32[]{:S(2)}, u32[]{:S(2)}) %collective-permute-start.91) | collective-permute-done | bytes 1048608 | tf_op jit(solution)/shard_map/ppermute | solution.py:19
  881.5 5.0 collective-permute-done.87
  887.7 5.1 collective-permute-done.92
  894.1 8.9 collective-permute-done.96
  906.0 20.5 %collective-permute-done.94 = f32[2,16,128,128]{3,2,1,0:T(8,128)S(1)} collective-permute-done((f32[2,16,128,128]{3,2,1,0:T(8,128)S(1)}, f32[2,16,128,128]{3,2,1,0:T(8,128)S(1)}, u32[]{:S(2)}, u32[]{:S(2)}) %collective-permute-start.94) | collective-permute-done | bytes 2097184 | tf_op jit(solution)/shard_map/ppermute | solution.py:19
  927.8 15.5 %collective-permute-done.98 = f32[1,2,16,64,128]{4,3,2,1,0:T(8,128)S(1)} collective-permute-done((f32[1,2,16,64,128]{4,3,2,1,0:T(8,128)S(1)}, f32[1,2,16,64,128]{4,3,2,1,0:T(8,128)S(1)}, u32[]{:S(2)}, u32[]{:S(2)}) %collective-permute-start.98) | collective-permute-done | bytes 1048608 | tf_op jit(solution)/shard_map/ppermute | solution.py:19
  950.3 21.3 %collective-permute-done.102 = f32[2,16,128,128]{3,2,1,0:T(8,128)S(1)} collective-permute-done((f32[2,16,128,128]{3,2,1,0:T(8,128)S(1)}, f32[2,16,128,128]{3,2,1,0:T(8,128)S(1)}, u32[]{:S(2)}, u32[]{:S(2)}) %collective-permute-start.102) | collective-permute-done | bytes 2097184 | tf_op jit(solution)/shard_map/ppermute | solution.py:19
  973.1 3.9 fusion.26
  978.2 38.3 %collective-permute-done.105 = f32[2,16,128,128]{3,2,1,0:T(8,128)S(1)} collective-permute-done((f32[2,16,128,128]{3,2,1,0:T(8,128)S(1)}, f32[2,16,128,128]{3,2,1,0:T(8,128)S(1)}, u32[]{:S(2)}, u32[]{:S(2)}) %collective-permute-start.105) | collective-permute-done | bytes 2097184 | tf_op jit(solution)/shard_map/ppermute | solution.py:19
  1018.7 42.6 %collective-permute-done.104 = f32[2,16,128,128]{3,2,1,0:T(8,128)S(1)} collective-permute-done((f32[2,16,128,128]{3,2,1,0:T(8,128)S(1)}, f32[2,16,128,128]{3,2,1,0:T(8,128)S(1)}, u32[]{:S(2)}, u32[]{:S(2)}) %collective-permute-start.104) | collective-permute-done | bytes 2097184 | tf_op jit(solution)/shard_map/ppermute | solution.py:19
  1062.9 4.0 fusion.25
  1066.9 23.1 %collective-permute-done.108 = f32[2,16,128,128]{3,2,1,0:T(8,128)S(1)} collective-permute-done((f32[2,16,128,128]{3,2,1,0:T(8,128)S(1)}, f32[2,16,128,128]{3,2,1,0:T(8,128)S(1)}, u32[]{:S(2)}, u32[]{:S(2)}) %collective-permute-start.108) | collective-permute-done | bytes 2097184 | tf_op jit(solution)/shard_map/ppermute | solution.py:19
  1094.1 4.1 fusion.105
  1100.5 3.8 copy.123.refs_0_
  1104.3 4.2 copy.124.refs_1_
  1108.5 5.8 copy.125.refs_2_
  1114.2 5.8 copy.126.refs_3_
  1120.0 5.9 copy.127.refs_4_
  1126.0 5.8 copy.128.refs_5_
  1131.8 5.7 copy.129.refs_6_
  1144.4 5.8 copy.130.refs_7_
  1150.2 69.3 %last_factors.1 = f32[2,16,32,64,128]{4,3,2,1,0:T(8,128)} custom-call(f32[16,2,32,8,128]{4,3,2,1,0:T(8,128)S(1)} %copy.123.refs_0_, f32[16,2,32,8,128]{4,3,2,1,0:T(8,128)S(1)} %copy.124.refs_1_, f32[16,2,32,8,128]{4,3,2,1,0:T(8,128)} %copy.125.refs_2_, f32[16,2,32,8,128]{4,3,2,1,0:T(8,128)} %copy.126.refs_3_, f32[16,2,32,8,128]{4,3,2,1,0:T(8,128)} %copy.127.refs_4_, ...), custom_call_target="tpu_custom_call" | custom-call | flops 19327352832 | bytes 67108864 | tf_op jit(solution)/shard_map/last_factors/pallas_call | solution.py:116
  (564 shorter events, 243.2 us)
Async XLA Ops:
  55.4 46.6 %collective-permute-start.6 = (f32[64,32,128]{2,0,1:T(8,128)}, f32[64,32,128]{2,0,1:T(8,128)}, u32[]{:S(2)}, u32[]{:S(2)}) collective-permute-start(f32[64,32,128]{2,0,1:T(8,128)} %constant_dynamic-update-slice_fusion), channel_id=1, source_target_pairs={{0,16},{4,20},{8,24},{12,28},{16,0},{20,4},{24,8},{28,12},{1,17},{... | collective-permute-start | bytes 3145736 | tf_op jit(solution)/shard_map/ppermute | solution.py:19
  105.4 46.8 %collective-permute-start.7 = (f32[2,2,16,32,128]{4,3,2,1,0:T(8,128)S(1)}, f32[2,2,16,32,128]{4,3,2,1,0:T(8,128)S(1)}, u32[]{:S(2)}, u32[]{:S(2)}) collective-permute-start(f32[2,2,16,32,128]{4,3,2,1,0:T(8,128)S(1)} %copy.63), channel_id=1, source_target_pairs={{0,8},{4,12},{8,0},{12,4},{16,24},{20,28},{24,16},{28,20},{1,9},{5... | collective-permute-start | bytes 3145736 | tf_op jit(solution)/shard_map/ppermute | solution.py:19
  106.7 47.6 %collective-permute-start.11 = (f32[64,32,128]{2,0,1:T(8,128)S(1)}, f32[64,32,128]{2,0,1:T(8,128)S(1)}, u32[]{:S(2)}, u32[]{:S(2)}) collective-permute-start(f32[64,32,128]{2,0,1:T(8,128)S(1)} %constant_dynamic-update-slice_fusion.4), channel_id=1, source_target_pairs={{0,16},{4,20},{8,24},{12,28},{16,0},{20,4},{24,8},{28,12},{1,17},{... | collective-permute-start | bytes 3145736 | tf_op jit(solution)/shard_map/ppermute | solution.py:19
  111.9 63.9 %collective-permute-start.9 = (f32[16,64,128]{2,0,1:T(8,128)}, f32[16,64,128]{2,0,1:T(8,128)}, u32[]{:S(2)}, u32[]{:S(2)}) collective-permute-start(f32[16,64,128]{2,0,1:T(8,128)} %get-tuple-element.891), channel_id=1, source_target_pairs={{0,4},{4,0},{8,12},{12,8},{16,20},{20,16},{24,28},{28,24},{1,5},{5... | collective-permute-start | bytes 1572872 | tf_op jit(solution)/shard_map/ppermute | solution.py:19
  113.3 61.3 %collective-permute-start.10 = (f32[32,32,128]{2,0,1:T(8,128)}, f32[32,32,128]{2,0,1:T(8,128)}, u32[]{:S(2)}, u32[]{:S(2)}) collective-permute-start(f32[32,32,128]{2,0,1:T(8,128)} %get-tuple-element.889), channel_id=1, source_target_pairs={{0,8},{4,12},{8,0},{12,4},{16,24},{20,28},{24,16},{28,20},{1,9},{5... | collective-permute-start | bytes 1572872 | tf_op jit(solution)/shard_map/ppermute | solution.py:19
  159.7 41.9 %collective-permute-start.15 = (f32[2,2,16,32,128]{4,3,2,1,0:T(8,128)}, f32[2,2,16,32,128]{4,3,2,1,0:T(8,128)}, u32[]{:S(2)}, u32[]{:S(2)}) collective-permute-start(f32[2,2,16,32,128]{4,3,2,1,0:T(8,128)} %copy.67), channel_id=1, source_target_pairs={{0,8},{4,12},{8,0},{12,4},{16,24},{20,28},{24,16},{28,20},{1,9},{5... | collective-permute-start | bytes 3145736 | tf_op jit(solution)/shard_map/ppermute | solution.py:19
  172.3 45.0 %collective-permute-start.14 = (f32[64,32,128]{2,0,1:T(8,128)S(1)}, f32[64,32,128]{2,0,1:T(8,128)S(1)}, u32[]{:S(2)}, u32[]{:S(2)}) collective-permute-start(f32[64,32,128]{2,0,1:T(8,128)S(1)} %copy-done.18), channel_id=1, source_target_pairs={{0,16},{4,20},{8,24},{12,28},{16,0},{20,4},{24,8},{28,12},{1,17},{... | collective-permute-start | bytes 3145736 | tf_op jit(solution)/shard_map/ppermute | solution.py:19
  177.1 65.1 %collective-permute-start.13 = (f32[32,32,128]{2,0,1:T(8,128)S(1)}, f32[32,32,128]{2,0,1:T(8,128)S(1)}, u32[]{:S(2)}, u32[]{:S(2)}) collective-permute-start(f32[32,32,128]{2,0,1:T(8,128)S(1)} %get-tuple-element.887), channel_id=1, source_target_pairs={{0,8},{4,12},{8,0},{12,4},{16,24},{20,28},{24,16},{28,20},{1,9},{5... | collective-permute-start | bytes 1572872 | tf_op jit(solution)/shard_map/ppermute | solution.py:19
  177.2 67.3 %collective-permute-start.19 = (f32[16,64,128]{2,0,1:T(8,128)S(1)}, f32[16,64,128]{2,0,1:T(8,128)S(1)}, u32[]{:S(2)}, u32[]{:S(2)}) collective-permute-start(f32[16,64,128]{2,0,1:T(8,128)S(1)} %get-tuple-element.885), channel_id=1, source_target_pairs={{0,4},{4,0},{8,12},{12,8},{16,20},{20,16},{24,28},{28,24},{1,5},{5... | collective-permute-start | bytes 1572872 | tf_op jit(solution)/shard_map/ppermute | solution.py:19
  219.3 44.4 %collective-permute-start.17 = (f32[2,2,16,32,128]{4,3,2,1,0:T(8,128)S(1)}, f32[2,2,16,32,128]{4,3,2,1,0:T(8,128)S(1)}, u32[]{:S(2)}, u32[]{:S(2)}) collective-permute-start(f32[2,2,16,32,128]{4,3,2,1,0:T(8,128)S(1)} %copy.69), channel_id=1, source_target_pairs={{0,8},{4,12},{8,0},{12,4},{16,24},{20,28},{24,16},{28,20},{1,9},{5... | collective-permute-start | bytes 3145736 | tf_op jit(solution)/shard_map/ppermute | solution.py:19
  219.9 45.7 %collective-permute-start.12 = (f32[64,32,128]{2,0,1:T(8,128)S(1)}, f32[64,32,128]{2,0,1:T(8,128)S(1)}, u32[]{:S(2)}, u32[]{:S(2)}) collective-permute-start(f32[64,32,128]{2,0,1:T(8,128)S(1)} %constant_dynamic-update-slice_fusion.13), channel_id=1, source_target_pairs={{0,16},{4,20},{8,24},{12,28},{16,0},{20,4},{24,8},{28,12},{1,17},{... | collective-permute-start | bytes 3145736 | tf_op jit(solution)/shard_map/ppermute | solution.py:19
  242.2 42.9 %collective-permute-start.23 = (f32[2,16,128,128]{3,2,1,0:T(8,128)S(1)}, f32[2,16,128,128]{3,2,1,0:T(8,128)S(1)}, u32[]{:S(2)}, u32[]{:S(2)}) collective-permute-start(f32[2,16,128,128]{3,2,1,0:T(8,128)S(1)} %maximum_bitcast_fusion.32), channel_id=1, source_target_pairs={{0,2},{1,3},{2,0},{3,1},{4,6},{5,7},{6,4},{7,5},{8,10},{9,11},{10,... | collective-permute-start | bytes 6291464 | tf_op jit(solution)/shard_map/ppermute | solution.py:19
  244.5 95.5 %collective-permute-start.28 = (f32[64,32,128]{2,0,1:T(8,128)S(1)}, f32[64,32,128]{2,0,1:T(8,128)S(1)}, u32[]{:S(2)}, u32[]{:S(2)}) collective-permute-start(f32[64,32,128]{2,0,1:T(8,128)S(1)} %constant_dynamic-update-slice_fusion.18), channel_id=1, source_target_pairs={{0,16},{4,20},{8,24},{12,28},{16,0},{20,4},{24,8},{28,12},{1,17},{... | collective-permute-start | bytes 3145736 | tf_op jit(solution)/shard_map/ppermute | solution.py:19
  245.0 55.8 %collective-permute-start.21 = (f32[16,64,128]{2,0,1:T(8,128)S(1)}, f32[16,64,128]{2,0,1:T(8,128)S(1)}, u32[]{:S(2)}, u32[]{:S(2)}) collective-permute-start(f32[16,64,128]{2,0,1:T(8,128)S(1)} %get-tuple-element.883), channel_id=1, source_target_pairs={{0,4},{4,0},{8,12},{12,8},{16,20},{20,16},{24,28},{28,24},{1,5},{5... | collective-permute-start | bytes 1572872 | tf_op jit(solution)/shard_map/ppermute | solution.py:19
  265.6 38.4 %collective-permute-start.20 = (f32[1,2,16,64,128]{4,3,2,1,0:T(8,128)S(1)}, f32[1,2,16,64,128]{4,3,2,1,0:T(8,128)S(1)}, u32[]{:S(2)}, u32[]{:S(2)}) collective-permute-start(f32[1,2,16,64,128]{4,3,2,1,0:T(8,128)S(1)} %get-tuple-element.831), channel_id=1, source_target_pairs={{0,4},{4,0},{8,12},{12,8},{16,20},{20,16},{24,28},{28,24},{1,5},{5... | collective-permute-start | bytes 3145736 | tf_op jit(solution)/shard_map/ppermute | solution.py:19
  285.0 52.7 %collective-permute-start.29 = (f32[2,2,16,32,128]{4,3,2,1,0:T(8,128)S(1)}, f32[2,2,16,32,128]{4,3,2,1,0:T(8,128)S(1)}, u32[]{:S(2)}, u32[]{:S(2)}) collective-permute-start(f32[2,2,16,32,128]{4,3,2,1,0:T(8,128)S(1)} %copy.73), channel_id=1, source_target_pairs={{0,8},{4,12},{8,0},{12,4},{16,24},{20,28},{24,16},{28,20},{1,9},{5... | collective-permute-start | bytes 3145736 | tf_op jit(solution)/shard_map/ppermute | solution.py:19
  299.3 42.8 %collective-permute-start.27 = (f32[2,16,128,128]{3,2,1,0:T(8,128)S(1)}, f32[2,16,128,128]{3,2,1,0:T(8,128)S(1)}, u32[]{:S(2)}, u32[]{:S(2)}) collective-permute-start(f32[2,16,128,128]{3,2,1,0:T(8,128)S(1)} %maximum_bitcast_fusion.33), channel_id=1, source_target_pairs={{0,2},{1,3},{2,0},{3,1},{4,6},{5,7},{6,4},{7,5},{8,10},{9,11},{10,... | collective-permute-start | bytes 6291464 | tf_op jit(solution)/shard_map/ppermute | solution.py:19
  300.9 88.4 %collective-permute-start.33 = (f32[64,32,128]{2,0,1:T(8,128)S(1)}, f32[64,32,128]{2,0,1:T(8,128)S(1)}, u32[]{:S(2)}, u32[]{:S(2)}) collective-permute-start(f32[64,32,128]{2,0,1:T(8,128)S(1)} %constant_dynamic-update-slice_fusion.23), channel_id=1, source_target_pairs={{0,16},{4,20},{8,24},{12,28},{16,0},{20,4},{24,8},{28,12},{1,17},{... | collective-permute-start | bytes 3145736 | tf_op jit(solution)/shard_map/ppermute | solution.py:19
  303.9 41.1 %collective-permute-start.26 = (f32[2,16,128,128]{3,2,1,0:T(8,128)S(1)}, f32[2,16,128,128]{3,2,1,0:T(8,128)S(1)}, u32[]{:S(2)}, u32[]{:S(2)}) collective-permute-start(f32[2,16,128,128]{3,2,1,0:T(8,128)S(1)} %pad_maximum_fusion), channel_id=1, source_target_pairs={{0,1},{1,0},{2,3},{3,2},{4,5},{5,4},{6,7},{7,6},{8,9},{9,8},{10,11... | collective-permute-start | bytes 6291464 | tf_op jit(solution)/shard_map/ppermute | solution.py:19
  342.0 46.4 %collective-permute-start.34 = (f32[2,2,16,32,128]{4,3,2,1,0:T(8,128)S(1)}, f32[2,2,16,32,128]{4,3,2,1,0:T(8,128)S(1)}, u32[]{:S(2)}, u32[]{:S(2)}) collective-permute-start(f32[2,2,16,32,128]{4,3,2,1,0:T(8,128)S(1)} %copy.76), channel_id=1, source_target_pairs={{0,8},{4,12},{8,0},{12,4},{16,24},{20,28},{24,16},{28,20},{1,9},{5... | collective-permute-start | bytes 3145736 | tf_op jit(solution)/shard_map/ppermute | solution.py:19
  362.5 43.1 %collective-permute-start.32 = (f32[2,16,128,128]{3,2,1,0:T(8,128)S(1)}, f32[2,16,128,128]{3,2,1,0:T(8,128)S(1)}, u32[]{:S(2)}, u32[]{:S(2)}) collective-permute-start(f32[2,16,128,128]{3,2,1,0:T(8,128)S(1)} %maximum_bitcast_fusion.34), channel_id=1, source_target_pairs={{0,2},{1,3},{2,0},{3,1},{4,6},{5,7},{6,4},{7,5},{8,10},{9,11},{10,... | collective-permute-start | bytes 6291464 | tf_op jit(solution)/shard_map/ppermute | solution.py:19
  363.2 43.7 %collective-permute-start.31 = (f32[2,16,128,128]{3,2,1,0:T(8,128)S(1)}, f32[2,16,128,128]{3,2,1,0:T(8,128)S(1)}, u32[]{:S(2)}, u32[]{:S(2)}) collective-permute-start(f32[2,16,128,128]{3,2,1,0:T(8,128)S(1)} %pad_maximum_fusion.1), channel_id=1, source_target_pairs={{0,1},{1,0},{2,3},{3,2},{4,5},{5,4},{6,7},{7,6},{8,9},{9,8},{10,11... | collective-permute-start | bytes 6291464 | tf_op jit(solution)/shard_map/ppermute | solution.py:19
  370.6 78.6 %collective-permute-start.42 = (f32[64,32,128]{2,0,1:T(8,128)S(1)}, f32[64,32,128]{2,0,1:T(8,128)S(1)}, u32[]{:S(2)}, u32[]{:S(2)}) collective-permute-start(f32[64,32,128]{2,0,1:T(8,128)S(1)} %constant_dynamic-update-slice_fusion.28), channel_id=1, source_target_pairs={{0,16},{4,20},{8,24},{12,28},{16,0},{20,4},{24,8},{28,12},{1,17},{... | collective-permute-start | bytes 3145736 | tf_op jit(solution)/shard_map/ppermute | solution.py:19
  405.6 41.6 %collective-permute-start.43 = (f32[2,2,16,32,128]{4,3,2,1,0:T(8,128)S(1)}, f32[2,2,16,32,128]{4,3,2,1,0:T(8,128)S(1)}, u32[]{:S(2)}, u32[]{:S(2)}) collective-permute-start(f32[2,2,16,32,128]{4,3,2,1,0:T(8,128)S(1)} %copy.82), channel_id=1, source_target_pairs={{0,8},{4,12},{8,0},{12,4},{16,24},{20,28},{24,16},{28,20},{1,9},{5... | collective-permute-start | bytes 3145736 | tf_op jit(solution)/shard_map/ppermute | solution.py:19
  426.7 81.2 %collective-permute-start.47 = (f32[64,32,128]{2,0,1:T(8,128)S(1)}, f32[64,32,128]{2,0,1:T(8,128)S(1)}, u32[]{:S(2)}, u32[]{:S(2)}) collective-permute-start(f32[64,32,128]{2,0,1:T(8,128)S(1)} %constant_dynamic-update-slice_fusion.33), channel_id=1, source_target_pairs={{0,16},{4,20},{8,24},{12,28},{16,0},{20,4},{24,8},{28,12},{1,17},{... | collective-permute-start | bytes 3145736 | tf_op jit(solution)/shard_map/ppermute | solution.py:19
  453.9 53.1 %collective-permute-start.48 = (f32[2,2,16,32,128]{4,3,2,1,0:T(8,128)S(1)}, f32[2,2,16,32,128]{4,3,2,1,0:T(8,128)S(1)}, u32[]{:S(2)}, u32[]{:S(2)}) collective-permute-start(f32[2,2,16,32,128]{4,3,2,1,0:T(8,128)S(1)} %copy.84), channel_id=1, source_target_pairs={{0,8},{4,12},{8,0},{12,4},{16,24},{20,28},{24,16},{28,20},{1,9},{5... | collective-permute-start | bytes 3145736 | tf_op jit(solution)/shard_map/ppermute | solution.py:19
  478.1 45.3 %collective-permute-start.46 = (f32[2,16,128,128]{3,2,1,0:T(8,128)S(1)}, f32[2,16,128,128]{3,2,1,0:T(8,128)S(1)}, u32[]{:S(2)}, u32[]{:S(2)}) collective-permute-start(f32[2,16,128,128]{3,2,1,0:T(8,128)S(1)} %maximum_bitcast_fusion.36), channel_id=1, source_target_pairs={{0,2},{1,3},{2,0},{3,1},{4,6},{5,7},{6,4},{7,5},{8,10},{9,11},{10,... | collective-permute-start | bytes 6291464 | tf_op jit(solution)/shard_map/ppermute | solution.py:19
  479.5 79.4 %collective-permute-start.56 = (f32[64,32,128]{2,0,1:T(8,128)S(1)}, f32[64,32,128]{2,0,1:T(8,128)S(1)}, u32[]{:S(2)}, u32[]{:S(2)}) collective-permute-start(f32[64,32,128]{2,0,1:T(8,128)S(1)} %constant_dynamic-update-slice_fusion.38), channel_id=1, source_target_pairs={{0,16},{4,20},{8,24},{12,28},{16,0},{20,4},{24,8},{28,12},{1,17},{... | collective-permute-start | bytes 3145736 | tf_op jit(solution)/shard_map/ppermute | solution.py:19
  482.4 41.8 %collective-permute-start.45 = (f32[2,16,128,128]{3,2,1,0:T(8,128)S(1)}, f32[2,16,128,128]{3,2,1,0:T(8,128)S(1)}, u32[]{:S(2)}, u32[]{:S(2)}) collective-permute-start(f32[2,16,128,128]{3,2,1,0:T(8,128)S(1)} %pad_maximum_fusion.3), channel_id=1, source_target_pairs={{0,1},{1,0},{2,3},{3,2},{4,5},{5,4},{6,7},{7,6},{8,9},{9,8},{10,11... | collective-permute-start | bytes 6291464 | tf_op jit(solution)/shard_map/ppermute | solution.py:19
  535.8 45.4 %collective-permute-start.55 = (f32[2,16,128,128]{3,2,1,0:T(8,128)S(1)}, f32[2,16,128,128]{3,2,1,0:T(8,128)S(1)}, u32[]{:S(2)}, u32[]{:S(2)}) collective-permute-start(f32[2,16,128,128]{3,2,1,0:T(8,128)S(1)} %maximum_bitcast_fusion.37), channel_id=1, source_target_pairs={{0,2},{1,3},{2,0},{3,1},{4,6},{5,7},{6,4},{7,5},{8,10},{9,11},{10,... | collective-permute-start | bytes 6291464 | tf_op jit(solution)/shard_map/ppermute | solution.py:19
  536.7 45.3 %collective-permute-start.54 = (f32[2,16,128,128]{3,2,1,0:T(8,128)S(1)}, f32[2,16,128,128]{3,2,1,0:T(8,128)S(1)}, u32[]{:S(2)}, u32[]{:S(2)}) collective-permute-start(f32[2,16,128,128]{3,2,1,0:T(8,128)S(1)} %pad_maximum_fusion.4), channel_id=1, source_target_pairs={{0,1},{1,0},{2,3},{3,2},{4,5},{5,4},{6,7},{7,6},{8,9},{9,8},{10,11... | collective-permute-start | bytes 6291464 | tf_op jit(solution)/shard_map/ppermute | solution.py:19
  546.2 71.5 %collective-permute-start.61 = (f32[64,32,128]{2,0,1:T(8,128)S(1)}, f32[64,32,128]{2,0,1:T(8,128)S(1)}, u32[]{:S(2)}, u32[]{:S(2)}) collective-permute-start(f32[64,32,128]{2,0,1:T(8,128)S(1)} %constant_dynamic-update-slice_fusion.43), channel_id=1, source_target_pairs={{0,16},{4,20},{8,24},{12,28},{16,0},{20,4},{24,8},{28,12},{1,17},{... | collective-permute-start | bytes 3145736 | tf_op jit(solution)/shard_map/ppermute | solution.py:19
  595.3 43.5 %collective-permute-start.60 = (f32[2,16,128,128]{3,2,1,0:T(8,128)S(1)}, f32[2,16,128,128]{3,2,1,0:T(8,128)S(1)}, u32[]{:S(2)}, u32[]{:S(2)}) collective-permute-start(f32[2,16,128,128]{3,2,1,0:T(8,128)S(1)} %maximum_bitcast_fusion.38), channel_id=1, source_target_pairs={{0,2},{1,3},{2,0},{3,1},{4,6},{5,7},{6,4},{7,5},{8,10},{9,11},{10,... | collective-permute-start | bytes 6291464 | tf_op jit(solution)/shard_map/ppermute | solution.py:19
  596.3 43.4 %collective-permute-start.59 = (f32[2,16,128,128]{3,2,1,0:T(8,128)S(1)}, f32[2,16,128,128]{3,2,1,0:T(8,128)S(1)}, u32[]{:S(2)}, u32[]{:S(2)}) collective-permute-start(f32[2,16,128,128]{3,2,1,0:T(8,128)S(1)} %pad_maximum_fusion.5), channel_id=1, source_target_pairs={{0,1},{1,0},{2,3},{3,2},{4,5},{5,4},{6,7},{7,6},{8,9},{9,8},{10,11... | collective-permute-start | bytes 6291464 | tf_op jit(solution)/shard_map/ppermute | solution.py:19
  604.0 94.7 %collective-permute-start.70 = (f32[64,32,128]{2,0,1:T(8,128)S(1)}, f32[64,32,128]{2,0,1:T(8,128)S(1)}, u32[]{:S(2)}, u32[]{:S(2)}) collective-permute-start(f32[64,32,128]{2,0,1:T(8,128)S(1)} %constant_dynamic-update-slice_fusion.48), channel_id=1, source_target_pairs={{0,16},{4,20},{8,24},{12,28},{16,0},{20,4},{24,8},{28,12},{1,17},{... | collective-permute-start | bytes 3145736 | tf_op jit(solution)/shard_map/ppermute | solution.py:19
  616.7 44.7 %collective-permute-start.58 = (f32[32,32,128]{2,0,1:T(8,128)S(1)}, f32[32,32,128]{2,0,1:T(8,128)S(1)}, u32[]{:S(2)}, u32[]{:S(2)}) collective-permute-start(f32[32,32,128]{2,0,1:T(8,128)S(1)} %get-tuple-element.859), channel_id=1, source_target_pairs={{0,8},{4,12},{8,0},{12,4},{16,24},{20,28},{24,16},{28,20},{1,9},{5... | collective-permute-start | bytes 1572872 | tf_op jit(solution)/shard_map/ppermute | solution.py:19
  617.7 44.6 %collective-permute-start.65 = (f32[16,64,128]{2,0,1:T(8,128)S(1)}, f32[16,64,128]{2,0,1:T(8,128)S(1)}, u32[]{:S(2)}, u32[]{:S(2)}) collective-permute-start(f32[16,64,128]{2,0,1:T(8,128)S(1)} %get-tuple-element.857), channel_id=1, source_target_pairs={{0,4},{4,0},{8,12},{12,8},{16,20},{20,16},{24,28},{28,24},{1,5},{5... | collective-permute-start | bytes 1572872 | tf_op jit(solution)/shard_map/ppermute | solution.py:19
  638.9 56.7 %collective-permute-start.71 = (f32[2,2,16,32,128]{4,3,2,1,0:T(8,128)S(1)}, f32[2,2,16,32,128]{4,3,2,1,0:T(8,128)S(1)}, u32[]{:S(2)}, u32[]{:S(2)}) collective-permute-start(f32[2,2,16,32,128]{4,3,2,1,0:T(8,128)S(1)} %copy.98), channel_id=1, source_target_pairs={{0,8},{4,12},{8,0},{12,4},{16,24},{20,28},{24,16},{28,20},{1,9},{5... | collective-permute-start | bytes 3145736 | tf_op jit(solution)/shard_map/ppermute | solution.py:19
  661.5 39.2 %collective-permute-start.69 = (f32[2,16,128,128]{3,2,1,0:T(8,128)S(1)}, f32[2,16,128,128]{3,2,1,0:T(8,128)S(1)}, u32[]{:S(2)}, u32[]{:S(2)}) collective-permute-start(f32[2,16,128,128]{3,2,1,0:T(8,128)S(1)} %maximum_bitcast_fusion.39), channel_id=1, source_target_pairs={{0,2},{1,3},{2,0},{3,1},{4,6},{5,7},{6,4},{7,5},{8,10},{9,11},{10,... | collective-permute-start | bytes 6291464 | tf_op jit(solution)/shard_map/ppermute | solution.py:19
  662.3 72.6 %collective-permute-start.75 = (f32[64,32,128]{2,0,1:T(8,128)S(1)}, f32[64,32,128]{2,0,1:T(8,128)S(1)}, u32[]{:S(2)}, u32[]{:S(2)}) collective-permute-start(f32[64,32,128]{2,0,1:T(8,128)S(1)} %constant_dynamic-update-slice_fusion.53), channel_id=1, source_target_pairs={{0,16},{4,20},{8,24},{12,28},{16,0},{20,4},{24,8},{28,12},{1,17},{... | collective-permute-start | bytes 3145736 | tf_op jit(solution)/shard_map/ppermute | solution.py:19
  664.3 39.3 %collective-permute-start.68 = (f32[2,16,128,128]{3,2,1,0:T(8,128)S(1)}, f32[2,16,128,128]{3,2,1,0:T(8,128)S(1)}, u32[]{:S(2)}, u32[]{:S(2)}) collective-permute-start(f32[2,16,128,128]{3,2,1,0:T(8,128)S(1)} %pad_maximum_fusion.6), channel_id=1, source_target_pairs={{0,1},{1,0},{2,3},{3,2},{4,5},{5,4},{6,7},{7,6},{8,9},{9,8},{10,11... | collective-permute-start | bytes 6291464 | tf_op jit(solution)/shard_map/ppermute | solution.py:19
  718.8 71.8 %collective-permute-start.78 = (f32[64,32,128]{2,0,1:T(8,128)S(1)}, f32[64,32,128]{2,0,1:T(8,128)S(1)}, u32[]{:S(2)}, u32[]{:S(2)}) collective-permute-start(f32[64,32,128]{2,0,1:T(8,128)S(1)} %constant_dynamic-update-slice_fusion.58), channel_id=1, source_target_pairs={{0,16},{4,20},{8,24},{12,28},{16,0},{20,4},{24,8},{28,12},{1,17},{... | collective-permute-start | bytes 3145736 | tf_op jit(solution)/shard_map/ppermute | solution.py:19
  748.3 38.7 %collective-permute-start.79 = (f32[2,2,16,32,128]{4,3,2,1,0:T(8,128)S(1)}, f32[2,2,16,32,128]{4,3,2,1,0:T(8,128)S(1)}, u32[]{:S(2)}, u32[]{:S(2)}) collective-permute-start(f32[2,2,16,32,128]{4,3,2,1,0:T(8,128)S(1)} %copy.104), channel_id=1, source_target_pairs={{0,8},{4,12},{8,0},{12,4},{16,24},{20,28},{24,16},{28,20},{1,9},{5... | collective-permute-start | bytes 3145736 | tf_op jit(solution)/shard_map/ppermute | solution.py:19
  773.2 100.2 %collective-permute-start.90 = (f32[64,32,128]{2,0,1:T(8,128)S(1)}, f32[64,32,128]{2,0,1:T(8,128)S(1)}, u32[]{:S(2)}, u32[]{:S(2)}) collective-permute-start(f32[64,32,128]{2,0,1:T(8,128)S(1)} %constant_dynamic-update-slice_fusion.63), channel_id=1, source_target_pairs={{0,16},{4,20},{8,24},{12,28},{16,0},{20,4},{24,8},{28,12},{1,17},{... | collective-permute-start | bytes 3145736 | tf_op jit(solution)/shard_map/ppermute | solution.py:19
  787.0 52.6 %collective-permute-start.83 = (f32[16,64,128]{2,0,1:T(8,128)S(1)}, f32[16,64,128]{2,0,1:T(8,128)S(1)}, u32[]{:S(2)}, u32[]{:S(2)}) collective-permute-start(f32[16,64,128]{2,0,1:T(8,128)S(1)} %get-tuple-element.847), channel_id=1, source_target_pairs={{0,4},{4,0},{8,12},{12,8},{16,20},{20,16},{24,28},{28,24},{1,5},{5... | collective-permute-start | bytes 1572872 | tf_op jit(solution)/shard_map/ppermute | solution.py:19
  790.7 48.5 %collective-permute-start.84 = (f32[32,32,128]{2,0,1:T(8,128)S(1)}, f32[32,32,128]{2,0,1:T(8,128)S(1)}, u32[]{:S(2)}, u32[]{:S(2)}) collective-permute-start(f32[32,32,128]{2,0,1:T(8,128)S(1)} %get-tuple-element.845), channel_id=1, source_target_pairs={{0,8},{4,12},{8,0},{12,4},{16,24},{20,28},{24,16},{28,20},{1,9},{5... | collective-permute-start | bytes 1572872 | tf_op jit(solution)/shard_map/ppermute | solution.py:19
  797.1 45.7 %collective-permute-start.82 = (f32[1,2,16,64,128]{4,3,2,1,0:T(8,128)S(1)}, f32[1,2,16,64,128]{4,3,2,1,0:T(8,128)S(1)}, u32[]{:S(2)}, u32[]{:S(2)}) collective-permute-start(f32[1,2,16,64,128]{4,3,2,1,0:T(8,128)S(1)} %get-tuple-element.777), channel_id=1, source_target_pairs={{0,4},{4,0},{8,12},{12,8},{16,20},{20,16},{24,28},{28,24},{1,5},{5... | collective-permute-start | bytes 3145736 | tf_op jit(solution)/shard_map/ppermute | solution.py:19
  798.6 72.7 %collective-permute-start.91 = (f32[2,2,16,32,128]{4,3,2,1,0:T(8,128)S(1)}, f32[2,2,16,32,128]{4,3,2,1,0:T(8,128)S(1)}, u32[]{:S(2)}, u32[]{:S(2)}) collective-permute-start(f32[2,2,16,32,128]{4,3,2,1,0:T(8,128)S(1)} %copy.107), channel_id=1, source_target_pairs={{0,8},{4,12},{8,0},{12,4},{16,24},{20,28},{24,16},{28,20},{1,9},{5... | collective-permute-start | bytes 3145736 | tf_op jit(solution)/shard_map/ppermute | solution.py:19
  839.2 38.5 %collective-permute-start.89 = (f32[2,16,128,128]{3,2,1,0:T(8,128)S(1)}, f32[2,16,128,128]{3,2,1,0:T(8,128)S(1)}, u32[]{:S(2)}, u32[]{:S(2)}) collective-permute-start(f32[2,16,128,128]{3,2,1,0:T(8,128)S(1)} %maximum_bitcast_fusion.42), channel_id=1, source_target_pairs={{0,2},{1,3},{2,0},{3,1},{4,6},{5,7},{6,4},{7,5},{8,10},{9,11},{10,... | collective-permute-start | bytes 6291464 | tf_op jit(solution)/shard_map/ppermute | solution.py:19
  839.6 64.5 %collective-permute-start.95 = (f32[64,32,128]{2,0,1:T(8,128)S(1)}, f32[64,32,128]{2,0,1:T(8,128)S(1)}, u32[]{:S(2)}, u32[]{:S(2)}) collective-permute-start(f32[64,32,128]{2,0,1:T(8,128)S(1)} %constant_dynamic-update-slice_fusion.68), channel_id=1, source_target_pairs={{0,16},{4,20},{8,24},{12,28},{16,0},{20,4},{24,8},{28,12},{1,17},{... | collective-permute-start | bytes 3145736 | tf_op jit(solution)/shard_map/ppermute | solution.py:19
  878.5 48.1 %collective-permute-start.94 = (f32[2,16,128,128]{3,2,1,0:T(8,128)S(1)}, f32[2,16,128,128]{3,2,1,0:T(8,128)S(1)}, u32[]{:S(2)}, u32[]{:S(2)}) collective-permute-start(f32[2,16,128,128]{3,2,1,0:T(8,128)S(1)} %maximum_bitcast_fusion.43), channel_id=1, source_target_pairs={{0,2},{1,3},{2,0},{3,1},{4,6},{5,7},{6,4},{7,5},{8,10},{9,11},{10,... | collective-permute-start | bytes 6291464 | tf_op jit(solution)/shard_map/ppermute | solution.py:19
  886.5 40.9 %collective-permute-start.99 = (f32[2,16,128,128]{3,2,1,0:T(8,128)S(1)}, f32[2,16,128,128]{3,2,1,0:T(8,128)S(1)}, u32[]{:S(2)}, u32[]{:S(2)}) collective-permute-start(f32[2,16,128,128]{3,2,1,0:T(8,128)S(1)} %pad_maximum_fusion.10), channel_id=1, source_target_pairs={{0,1},{1,0},{2,3},{3,2},{4,5},{5,4},{6,7},{7,6},{8,9},{9,8},{10,11... | collective-permute-start | bytes 6291464 | tf_op jit(solution)/shard_map/ppermute | solution.py:19
  892.8 54.9 %collective-permute-start.93 = (f32[64,32,128]{2,0,1:T(8,128)S(1)}, f32[64,32,128]{2,0,1:T(8,128)S(1)}, u32[]{:S(2)}, u32[]{:S(2)}) collective-permute-start(f32[64,32,128]{2,0,1:T(8,128)S(1)} %constant_dynamic-update-slice_fusion.73), channel_id=1, source_target_pairs={{0,16},{4,20},{8,24},{12,28},{16,0},{20,4},{24,8},{28,12},{1,17},{... | collective-permute-start | bytes 3145736 | tf_op jit(solution)/shard_map/ppermute | solution.py:19
  903.1 68.4 %collective-permute-start.102 = (f32[2,16,128,128]{3,2,1,0:T(8,128)S(1)}, f32[2,16,128,128]{3,2,1,0:T(8,128)S(1)}, u32[]{:S(2)}, u32[]{:S(2)}) collective-permute-start(f32[2,16,128,128]{3,2,1,0:T(8,128)S(1)} %maximum_bitcast_fusion.44), channel_id=1, source_target_pairs={{0,2},{1,3},{2,0},{3,1},{4,6},{5,7},{6,4},{7,5},{8,10},{9,11},{10,... | collective-permute-start | bytes 6291464 | tf_op jit(solution)/shard_map/ppermute | solution.py:19
  905.9 40.8 %collective-permute-start.97 = (f32[2,2,16,32,128]{4,3,2,1,0:T(8,128)S(1)}, f32[2,2,16,32,128]{4,3,2,1,0:T(8,128)S(1)}, u32[]{:S(2)}, u32[]{:S(2)}) collective-permute-start(f32[2,2,16,32,128]{4,3,2,1,0:T(8,128)S(1)} %copy.113), channel_id=1, source_target_pairs={{0,8},{4,12},{8,0},{12,4},{16,24},{20,28},{24,16},{28,20},{1,9},{5... | collective-permute-start | bytes 3145736 | tf_op jit(solution)/shard_map/ppermute | solution.py:19
  927.4 44.9 %collective-permute-start.101 = (f32[2,16,128,128]{3,2,1,0:T(8,128)S(1)}, f32[2,16,128,128]{3,2,1,0:T(8,128)S(1)}, u32[]{:S(2)}, u32[]{:S(2)}) collective-permute-start(f32[2,16,128,128]{3,2,1,0:T(8,128)S(1)} %pad_maximum_fusion.11), channel_id=1, source_target_pairs={{0,1},{1,0},{2,3},{3,2},{4,5},{5,4},{6,7},{7,6},{8,9},{9,8},{10,11... | collective-permute-start | bytes 6291464 | tf_op jit(solution)/shard_map/ppermute | solution.py:19
  943.5 73.0 %collective-permute-start.105 = (f32[2,16,128,128]{3,2,1,0:T(8,128)S(1)}, f32[2,16,128,128]{3,2,1,0:T(8,128)S(1)}, u32[]{:S(2)}, u32[]{:S(2)}) collective-permute-start(f32[2,16,128,128]{3,2,1,0:T(8,128)S(1)} %maximum_bitcast_fusion.45), channel_id=1, source_target_pairs={{0,2},{1,3},{2,0},{3,1},{4,6},{5,7},{6,4},{7,5},{8,10},{9,11},{10,... | collective-permute-start | bytes 6291464 | tf_op jit(solution)/shard_map/ppermute | solution.py:19
  972.3 45.1 %collective-permute-start.107 = (f32[2,16,128,128]{3,2,1,0:T(8,128)S(1)}, f32[2,16,128,128]{3,2,1,0:T(8,128)S(1)}, u32[]{:S(2)}, u32[]{:S(2)}) collective-permute-start(f32[2,16,128,128]{3,2,1,0:T(8,128)S(1)} %pad_maximum_fusion.12), channel_id=1, source_target_pairs={{0,1},{1,0},{2,3},{3,2},{4,5},{5,4},{6,7},{7,6},{8,9},{9,8},{10,11... | collective-permute-start | bytes 6291464 | tf_op jit(solution)/shard_map/ppermute | solution.py:19
  977.2 84.2 %collective-permute-start.104 = (f32[2,16,128,128]{3,2,1,0:T(8,128)S(1)}, f32[2,16,128,128]{3,2,1,0:T(8,128)S(1)}, u32[]{:S(2)}, u32[]{:S(2)}) collective-permute-start(f32[2,16,128,128]{3,2,1,0:T(8,128)S(1)} %maximum_bitcast_fusion.46), channel_id=1, source_target_pairs={{0,2},{1,3},{2,0},{3,1},{4,6},{5,7},{6,4},{7,5},{8,10},{9,11},{10,... | collective-permute-start | bytes 6291464 | tf_op jit(solution)/shard_map/ppermute | solution.py:19
  978.1 39.6 %collective-permute-start.106 = (f32[1,2,16,64,128]{4,3,2,1,0:T(8,128)S(1)}, f32[1,2,16,64,128]{4,3,2,1,0:T(8,128)S(1)}, u32[]{:S(2)}, u32[]{:S(2)}) collective-permute-start(f32[1,2,16,64,128]{4,3,2,1,0:T(8,128)S(1)} %get-tuple-element.753), channel_id=1, source_target_pairs={{0,4},{4,0},{8,12},{12,8},{16,20},{20,16},{24,28},{28,24},{1,5},{5... | collective-permute-start | bytes 3145736 | tf_op jit(solution)/shard_map/ppermute | solution.py:19
  1017.3 44.9 %collective-permute-start.109 = (f32[2,16,128,128]{3,2,1,0:T(8,128)S(1)}, f32[2,16,128,128]{3,2,1,0:T(8,128)S(1)}, u32[]{:S(2)}, u32[]{:S(2)}) collective-permute-start(f32[2,16,128,128]{3,2,1,0:T(8,128)S(1)} %pad_maximum_fusion.13), channel_id=1, source_target_pairs={{0,1},{1,0},{2,3},{3,2},{4,5},{5,4},{6,7},{7,6},{8,9},{9,8},{10,11... | collective-permute-start | bytes 6291464 | tf_op jit(solution)/shard_map/ppermute | solution.py:19
  1017.9 72.1 %collective-permute-start.108 = (f32[2,16,128,128]{3,2,1,0:T(8,128)S(1)}, f32[2,16,128,128]{3,2,1,0:T(8,128)S(1)}, u32[]{:S(2)}, u32[]{:S(2)}) collective-permute-start(f32[2,16,128,128]{3,2,1,0:T(8,128)S(1)} %maximum_bitcast_fusion.47), channel_id=1, source_target_pairs={{0,2},{1,3},{2,0},{3,1},{4,6},{5,7},{6,4},{7,5},{8,10},{9,11},{10,... | collective-permute-start | bytes 6291464 | tf_op jit(solution)/shard_map/ppermute | solution.py:19
  1062.1 75.4 %collective-permute-start.110 = (f32[2,16,128,128]{3,2,1,0:T(8,128)S(1)}, f32[2,16,128,128]{3,2,1,0:T(8,128)}, u32[]{:S(2)}, u32[]{:S(2)}) collective-permute-start(f32[2,16,128,128]{3,2,1,0:T(8,128)S(1)} %pad_maximum_fusion.14), channel_id=1, source_target_pairs={{0,1},{1,0},{2,3},{3,2},{4,5},{5,4},{6,7},{7,6},{8,9},{9,8},{10,11... | collective-permute-start | bytes 6291464 | tf_op jit(solution)/shard_map/ppermute | solution.py:19
  1090.8 48.6 %collective-permute-start.111 = (f32[2,16,128,128]{3,2,1,0:T(8,128)S(1)}, f32[2,16,128,128]{3,2,1,0:T(8,128)}, u32[]{:S(2)}, u32[]{:S(2)}) collective-permute-start(f32[2,16,128,128]{3,2,1,0:T(8,128)S(1)} %pad_maximum_fusion.15), channel_id=1, source_target_pairs={{0,1},{1,0},{2,3},{3,2},{4,5},{5,4},{6,7},{7,6},{8,9},{9,8},{10,11... | collective-permute-start | bytes 6291464 | tf_op jit(solution)/shard_map/ppermute | solution.py:19
  (76 other events, 1447.1 us)
